TPU v7x, 512 devices: a whole 4x4x16 slice. The times are simulated.
512 devices in a mesh: blk: 128 (over x, z, y_hi), uly: 4 (over y_lo, core).
Axes of the slice: x: 4, y: 4 (y_hi: 2, y_lo: 2; y = y_hi * 2 + y_lo), z: 16, core: 2. Of those that a mesh axis runs over, the one named last changes fastest.
Arguments:
- query_states: bfloat16 [65536, 4096], P(('blk', 'uly')), may hold values from -6 to 6
- key_states: bfloat16 [65536, 512], P(('blk', 'uly')), may hold values from -6 to 6
- value_states: bfloat16 [65536, 512], P(('blk', 'uly')), may hold values from -6 to 6
- out_grad: bfloat16 [65536, 4096], P(('blk', 'uly')), may hold values from -6 to 6
- block_list: int32 [128, 2], replicated, may hold values from 0 to 127, as said below
- block_count: int32 [128], replicated, may hold values from 1 to 2, as said below
Outputs:
- attention: bfloat16 [65536, 4096], P(('blk', 'uly'))
- query_grad: bfloat16 [65536, 4096], P(('blk', 'uly'))
- key_grad: bfloat16 [65536, 512], P(('blk', 'uly'))
- value_grad: bfloat16 [65536, 512], P(('blk', 'uly'))
Inputs may be any that keep to these rules, and one draw needn't show every extreme that they name: `block_list`: the first block_count[b] entries of row b are distinct, in any order, and hold b itself and, when block_count[b] is 2, one block from 1 to 8 blocks before b; the later entries are padding of any value and carry no meaning. In every draw some query block's gated block lies exactly 8 blocks before it. `block_count`: block 0 has the count 1; block 1 and the last block have the count 2.
All inputs are finite; a program needn't handle non-finite values.
Results may differ from a plain program's by a relative error of at most 0.029.
Values may be sent and summed in bfloat16 or wider, within the bound.
No kernel may reach another device: no remote copies, remote signals or barrier semaphores. Data moves between devices by JAX's collectives and lax.ppermute only.
A program may use at most 64 MiB of HBM per device.

v0:
```python
import math

import jax
import jax.numpy as jnp
from jax import lax
from jax.sharding import PartitionSpec as P

QH = 32
KVH = 4
HD = 128


NEG_FILL = -1e30


def from_behind(array, axis, by):
    peers = lax.axis_size(axis)
    pairs = [(i, i + by) for i in range(peers) if 0 <= i + by < peers]
    return lax.ppermute(array, axis, pairs)


def block_pick(block_list, block_count, block):
    entries = lax.dynamic_index_in_dim(block_list, block, 0, keepdims=False)
    needed = lax.dynamic_index_in_dim(block_count, block, 0, keepdims=False)
    slots = jnp.arange(entries.shape[0], dtype=jnp.int32)
    others = (slots < needed) & (entries != block)
    has_remote = jnp.any(others)
    gated = jnp.sum(jnp.where(others, entries, 0))
    return (has_remote, gated)


def head_pass(query_in, grad_in, key_both, value_both, allowed, group):
    scale = 1.0 / math.sqrt(query_in.shape[2])
    width = 2
    turns = query_in.shape[1] // width

    def one_pair(turn, carry):
        out_all, query_grad, key_sum, value_sum = carry
        first_head = turn * width
        query_pair = lax.dynamic_slice_in_dim(query_in, first_head, width, 1)
        grad_pair = lax.dynamic_slice_in_dim(grad_in, first_head, width, 1)
        paired = first_head // group
        key_head = lax.dynamic_index_in_dim(key_both, paired, 1, keepdims=False)
        value_head = lax.dynamic_index_in_dim(value_both, paired, 1, keepdims=False)
        scores = (
            jnp.einsum("rgd,cd->grc", query_pair, key_head, preferred_element_type=jnp.float32)
            * scale
        )
        scores = jnp.where(allowed[None], scores, NEG_FILL)
        top = jnp.max(scores, axis=2, keepdims=True)
        log_total = top + jnp.log(jnp.sum(jnp.exp(scores - top), axis=2, keepdims=True))
        probs = jnp.exp(scores - log_total)
        probs_low = probs.astype(jnp.bfloat16)
        out_pair = jnp.einsum(
            "grc,cd->rgd", probs_low, value_head, preferred_element_type=jnp.float32
        ).astype(jnp.bfloat16)
        delta = jnp.sum(grad_pair.astype(jnp.float32) * out_pair.astype(jnp.float32), axis=2)
        delta = jnp.transpose(delta)[:, :, None]
        dprob = jnp.einsum("rgd,cd->grc", grad_pair, value_head, preferred_element_type=jnp.float32)
        dscore = (probs * (dprob - delta)).astype(jnp.bfloat16)
        query_part = (
            jnp.einsum("grc,cd->rgd", dscore, key_head, preferred_element_type=jnp.float32) * scale
        ).astype(jnp.bfloat16)
        key_part = (
            jnp.einsum("grc,rgd->cd", dscore, query_pair, preferred_element_type=jnp.float32)
            * scale
        )
        value_part = jnp.einsum(
            "grc,rgd->cd", probs_low, grad_pair, preferred_element_type=jnp.float32
        )
        out_all = lax.dynamic_update_slice_in_dim(out_all, out_pair, first_head, 1)
        query_grad = lax.dynamic_update_slice_in_dim(query_grad, query_part, first_head, 1)
        old_key = lax.dynamic_index_in_dim(key_sum, paired, 1, keepdims=False)
        key_sum = lax.dynamic_update_index_in_dim(key_sum, old_key + key_part, paired, 1)
        old_value = lax.dynamic_index_in_dim(value_sum, paired, 1, keepdims=False)
        value_sum = lax.dynamic_update_index_in_dim(value_sum, old_value + value_part, paired, 1)
        return (out_all, query_grad, key_sum, value_sum)

    start = (
        jnp.zeros(query_in.shape, jnp.bfloat16),
        jnp.zeros(query_in.shape, jnp.bfloat16),
        jnp.zeros(key_both.shape, jnp.float32),
        jnp.zeros(key_both.shape, jnp.float32),
    )
    return lax.fori_loop(0, turns, one_pair, start)


def body(query_states, key_states, value_states, out_grad, block_list, block_count):
    tokens_here = query_states.shape[0]
    group = QH // KVH
    reach = min(8, lax.axis_size("blk") // 2)
    query_in, key_in, value_in, grad_in = (
        lax.all_to_all(
            query_states.reshape(tokens_here, QH, HD),
            "uly",
            split_axis=1,
            concat_axis=0,
            tiled=True,
        ),
        lax.all_to_all(
            key_states.reshape(tokens_here, KVH, HD), "uly", split_axis=1, concat_axis=0, tiled=True
        ),
        lax.all_to_all(
            value_states.reshape(tokens_here, KVH, HD),
            "uly",
            split_axis=1,
            concat_axis=0,
            tiled=True,
        ),
        lax.all_to_all(
            out_grad.reshape(tokens_here, QH, HD), "uly", split_axis=1, concat_axis=0, tiled=True
        ),
    )
    block = lax.axis_index("blk")
    has_remote, gated = block_pick(block_list, block_count, block)
    distance = block - gated

    def pass_block(step, carry):
        moving_key, moving_value, held_key, held_value = carry
        moving_key, moving_value = from_behind((moving_key, moving_value), "blk", 1)
        chosen = has_remote & (distance == step)
        return (
            moving_key,
            moving_value,
            jnp.where(chosen, moving_key, held_key),
            jnp.where(chosen, moving_value, held_value),
        )

    fetched = lax.fori_loop(
        1,
        reach + 1,
        pass_block,
        (key_in, value_in, jnp.zeros_like(key_in), jnp.zeros_like(value_in)),
    )
    far_key, far_value = (fetched[2], fetched[3])
    block_rows = key_in.shape[0]
    positions = jnp.arange(block_rows, dtype=jnp.int32)
    columns = jnp.arange(2 * block_rows, dtype=jnp.int32)
    allowed = jnp.where(
        columns[None, :] < block_rows, columns[None, :] <= positions[:, None], has_remote
    )
    key_both = jnp.concatenate([key_in, far_key], 0)
    value_both = jnp.concatenate([value_in, far_value], 0)
    attention, query_grad, key_sum, value_sum = head_pass(
        query_in, grad_in, key_both, value_both, allowed, group
    )
    own_key, part_key = (key_sum[:block_rows], key_sum[block_rows:])
    own_value, part_value = (value_sum[:block_rows], value_sum[block_rows:])
    first = has_remote & (distance == reach)
    start = (jnp.where(first, part_key, 0.0), jnp.where(first, part_value, 0.0))

    def carry_back(step, carry):
        moving_key, moving_value = from_behind((carry[0], carry[1]), "blk", -1)
        chosen = has_remote & (distance == reach - step)
        return (
            moving_key + jnp.where(chosen, part_key, 0.0),
            moving_value + jnp.where(chosen, part_value, 0.0),
        )

    came_key, came_value = lax.fori_loop(1, reach + 1, carry_back, start)
    total_key = own_key + came_key
    total_value = own_value + came_value
    key_grad = total_key.astype(jnp.bfloat16)
    value_grad = total_value.astype(jnp.bfloat16)
    attention, query_grad, key_grad, value_grad = (
        lax.all_to_all(attention, "uly", split_axis=0, concat_axis=1, tiled=True),
        lax.all_to_all(query_grad, "uly", split_axis=0, concat_axis=1, tiled=True),
        lax.all_to_all(key_grad, "uly", split_axis=0, concat_axis=1, tiled=True),
        lax.all_to_all(value_grad, "uly", split_axis=0, concat_axis=1, tiled=True),
    )
    return (
        attention.reshape(tokens_here, QH * HD),
        query_grad.reshape(tokens_here, QH * HD),
        key_grad.reshape(tokens_here, KVH * HD),
        value_grad.reshape(tokens_here, KVH * HD),
    )


def solution(mesh):
    placed = (
        P(("blk", "uly"), None),
        P(("blk", "uly"), None),
        P(("blk", "uly"), None),
        P(("blk", "uly"), None),
        P(),
        P(),
    )
    return jax.shard_map(
        body,
        mesh=mesh,
        in_specs=placed,
        out_specs=(
            P(("blk", "uly"), None),
            P(("blk", "uly"), None),
            P(("blk", "uly"), None),
            P(("blk", "uly"), None),
        ),
        check_vma=False,
    )
```

profile of v0, /device:TPU:6, one launch (start us, length us, event | category | flops | bytes accessed | tf_op | source)
XLA Modules:
  0.0 501.0 jit_solution(9443317273968014928)
XLA Ops:
  31.2 4.9 all-to-all-done.3
  39.7 169.6 %while.57 = (s32[]{:T(128)}, bf16[512,1,128]{2,1,0:T(2,128)(2,1)}, bf16[512,1,128]{2,1,0:T(2,128)(2,1)}, bf16[512,1,128]{2,1,0:T(2,128)(2,1)S(1)}, bf16[512,1,12...) while((s32[]{:T(128)}, bf16[512,1,128]{2,1,0:T(2,128)(2,1)}, ...), condition=%wide.region_3.4_spmd.clone, body=%wide.region_2.3_spmd.clone.sunk | while | flops 262149 | bytes 2359502 | solution.py:129
  39.7 5.1 %collective-permute-start.2 = (bf16[512,1,128]{2,1,0:T(2,128)(2,1)}, bf16[512,1,128]{2,1,0:T(2,128)(2,1)S(1)}, u32[]{:S(2)}, u32[]{:S(2)}) collective-permute-start(bf16[512,1,128]{2,1,0:T(2,128)(2,1)} %get-tuple-element.870), channel_id=1, source_target_pairs={{0,4},{4,8},{8,12},{12,16},{16,20},{20,24},{24,28},{28,32},{32,36}... | collective-permute-start | bytes 393224 | tf_op jit(solution)/shard_map/while/body/eval_jaxpr/ppermute | solution.py:19
  49.0 12.4 %collective-permute-done.2 = bf16[512,1,128]{2,1,0:T(2,128)(2,1)S(1)} collective-permute-done((bf16[512,1,128]{2,1,0:T(2,128)(2,1)}, bf16[512,1,128]{2,1,0:T(2,128)(2,1)S(1)}, u32[]{:S(2)}, u32[]{:S(2)}) %collective-permute-start.2) | collective-permute-done | bytes 131104 | tf_op jit(solution)/shard_map/while/body/eval_jaxpr/ppermute | solution.py:19
  62.1 4.7 collective-permute-done.3
  74.3 13.0 %collective-permute-done.2 = bf16[512,1,128]{2,1,0:T(2,128)(2,1)S(1)} collective-permute-done((bf16[512,1,128]{2,1,0:T(2,128)(2,1)}, bf16[512,1,128]{2,1,0:T(2,128)(2,1)S(1)}, u32[]{:S(2)}, u32[]{:S(2)}) %collective-permute-start.2) | collective-permute-done | bytes 131104 | tf_op jit(solution)/shard_map/while/body/eval_jaxpr/ppermute | solution.py:19
  98.3 11.4 %collective-permute-done.2 = bf16[512,1,128]{2,1,0:T(2,128)(2,1)S(1)} collective-permute-done((bf16[512,1,128]{2,1,0:T(2,128)(2,1)}, bf16[512,1,128]{2,1,0:T(2,128)(2,1)S(1)}, u32[]{:S(2)}, u32[]{:S(2)}) %collective-permute-start.2) | collective-permute-done | bytes 131104 | tf_op jit(solution)/shard_map/while/body/eval_jaxpr/ppermute | solution.py:19
  119.7 11.4 %collective-permute-done.2 = bf16[512,1,128]{2,1,0:T(2,128)(2,1)S(1)} collective-permute-done((bf16[512,1,128]{2,1,0:T(2,128)(2,1)}, bf16[512,1,128]{2,1,0:T(2,128)(2,1)S(1)}, u32[]{:S(2)}, u32[]{:S(2)}) %collective-permute-start.2) | collective-permute-done | bytes 131104 | tf_op jit(solution)/shard_map/while/body/eval_jaxpr/ppermute | solution.py:19
  140.3 10.7 %collective-permute-done.2 = bf16[512,1,128]{2,1,0:T(2,128)(2,1)S(1)} collective-permute-done((bf16[512,1,128]{2,1,0:T(2,128)(2,1)}, bf16[512,1,128]{2,1,0:T(2,128)(2,1)S(1)}, u32[]{:S(2)}, u32[]{:S(2)}) %collective-permute-start.2) | collective-permute-done | bytes 131104 | tf_op jit(solution)/shard_map/while/body/eval_jaxpr/ppermute | solution.py:19
  159.9 9.7 %collective-permute-done.2 = bf16[512,1,128]{2,1,0:T(2,128)(2,1)S(1)} collective-permute-done((bf16[512,1,128]{2,1,0:T(2,128)(2,1)}, bf16[512,1,128]{2,1,0:T(2,128)(2,1)S(1)}, u32[]{:S(2)}, u32[]{:S(2)}) %collective-permute-start.2) | collective-permute-done | bytes 131104 | tf_op jit(solution)/shard_map/while/body/eval_jaxpr/ppermute | solution.py:19
  178.6 8.8 %collective-permute-done.2 = bf16[512,1,128]{2,1,0:T(2,128)(2,1)S(1)} collective-permute-done((bf16[512,1,128]{2,1,0:T(2,128)(2,1)}, bf16[512,1,128]{2,1,0:T(2,128)(2,1)S(1)}, u32[]{:S(2)}, u32[]{:S(2)}) %collective-permute-start.2) | collective-permute-done | bytes 131104 | tf_op jit(solution)/shard_map/while/body/eval_jaxpr/ppermute | solution.py:19
  196.3 8.5 %collective-permute-done.2 = bf16[512,1,128]{2,1,0:T(2,128)(2,1)S(1)} collective-permute-done((bf16[512,1,128]{2,1,0:T(2,128)(2,1)}, bf16[512,1,128]{2,1,0:T(2,128)(2,1)S(1)}, u32[]{:S(2)}, u32[]{:S(2)}) %collective-permute-start.2) | collective-permute-done | bytes 131104 | tf_op jit(solution)/shard_map/while/body/eval_jaxpr/ppermute | solution.py:19
  216.6 98.5 %while.56 = (s32[]{:T(128)}, bf16[512,8,128]{2,1,0:T(8,128)(2,1)}, bf16[512,8,128]{2,1,0:T(8,128)(2,1)}, f32[1024,1,128]{2,0,1:T(8,128)S(1)}, f32[1024,1,128]{2,...) while((s32[]{:T(128)}, bf16[512,8,128]{2,1,0:T(8,128)(2,1)}, ...), condition=%wide.region_8.9_spmd.clone, body=%wide.region_4.8_spmd.clone.sunk | while | flops 1634990080 | bytes 73184544 | solution.py:85
  225.9 4.7 fusion.66
  250.5 4.7 fusion.66
  275.1 4.7 fusion.66
  299.8 4.7 fusion.66
  316.3 130.4 %while.55 = (s32[]{:T(128)}, f32[512,1,128]{2,1,0:T(1,128)S(1)}, f32[512,1,128]{2,1,0:T(1,128)S(1)}, s32[]{:T(128)}, pred[]{:T(512)}, /*index=5*/f32[512,1,128]{...) while((s32[]{:T(128)}, f32[512,1,128]{2,1,0:T(1,128)S(1)}, f32[512,1,128]{2,1,0:T(1,128)S(1)}, ...), condition=%wide.region_10.11_spmd, body=%wide.region_9.10_spmd.sunk | while | flops 262149 | bytes 3670215 | solution.py:160
  323.7 4.7 collective-permute-done
  331.6 6.1 %collective-permute-start = (f32[512,1,128]{2,1,0:T(1,128)S(1)}, f32[512,1,128]{2,1,0:T(1,128)S(1)}, u32[]{:S(2)}, u32[]{:S(2)}) collective-permute-start(f32[512,1,128]{2,1,0:T(1,128)S(1)} %get-tuple-element.942), channel_id=1, source_target_pairs={{4,0},{8,4},{12,8},{16,12},{20,16},{24,20},{28,24},{32,28},{36,32}... | collective-permute-start | bytes 786440 | tf_op jit(solution)/shard_map/while/body/eval_jaxpr/ppermute | solution.py:19
  347.8 5.8 %collective-permute-start = (f32[512,1,128]{2,1,0:T(1,128)S(1)}, f32[512,1,128]{2,1,0:T(1,128)S(1)}, u32[]{:S(2)}, u32[]{:S(2)}) collective-permute-start(f32[512,1,128]{2,1,0:T(1,128)S(1)} %get-tuple-element.942), channel_id=1, source_target_pairs={{4,0},{8,4},{12,8},{16,12},{20,16},{24,20},{28,24},{32,28},{36,32}... | collective-permute-start | bytes 786440 | tf_op jit(solution)/shard_map/while/body/eval_jaxpr/ppermute | solution.py:19
  363.8 5.8 %collective-permute-start = (f32[512,1,128]{2,1,0:T(1,128)S(1)}, f32[512,1,128]{2,1,0:T(1,128)S(1)}, u32[]{:S(2)}, u32[]{:S(2)}) collective-permute-start(f32[512,1,128]{2,1,0:T(1,128)S(1)} %get-tuple-element.942), channel_id=1, source_target_pairs={{4,0},{8,4},{12,8},{16,12},{20,16},{24,20},{28,24},{32,28},{36,32}... | collective-permute-start | bytes 786440 | tf_op jit(solution)/shard_map/while/body/eval_jaxpr/ppermute | solution.py:19
  374.1 5.2 %collective-permute-done.1 = f32[512,1,128]{2,1,0:T(1,128)S(1)} collective-permute-done((f32[512,1,128]{2,1,0:T(1,128)S(1)}, f32[512,1,128]{2,1,0:T(1,128)S(1)}, u32[]{:S(2)}, u32[]{:S(2)}) %collective-permute-start.1) | collective-permute-done | bytes 262176 | tf_op jit(solution)/shard_map/while/body/eval_jaxpr/ppermute | solution.py:19
  379.7 5.8 %collective-permute-start = (f32[512,1,128]{2,1,0:T(1,128)S(1)}, f32[512,1,128]{2,1,0:T(1,128)S(1)}, u32[]{:S(2)}, u32[]{:S(2)}) collective-permute-start(f32[512,1,128]{2,1,0:T(1,128)S(1)} %get-tuple-element.942), channel_id=1, source_target_pairs={{4,0},{8,4},{12,8},{16,12},{20,16},{24,20},{28,24},{32,28},{36,32}... | collective-permute-start | bytes 786440 | tf_op jit(solution)/shard_map/while/body/eval_jaxpr/ppermute | solution.py:19
  389.8 7.4 %collective-permute-done.1 = f32[512,1,128]{2,1,0:T(1,128)S(1)} collective-permute-done((f32[512,1,128]{2,1,0:T(1,128)S(1)}, f32[512,1,128]{2,1,0:T(1,128)S(1)}, u32[]{:S(2)}, u32[]{:S(2)}) %collective-permute-start.1) | collective-permute-done | bytes 262176 | tf_op jit(solution)/shard_map/while/body/eval_jaxpr/ppermute | solution.py:19
  407.8 5.4 %collective-permute-done.1 = f32[512,1,128]{2,1,0:T(1,128)S(1)} collective-permute-done((f32[512,1,128]{2,1,0:T(1,128)S(1)}, f32[512,1,128]{2,1,0:T(1,128)S(1)}, u32[]{:S(2)}, u32[]{:S(2)}) %collective-permute-start.1) | collective-permute-done | bytes 262176 | tf_op jit(solution)/shard_map/while/body/eval_jaxpr/ppermute | solution.py:19
  413.5 5.0 collective-permute-start
  429.5 7.1 %collective-permute-start = (f32[512,1,128]{2,1,0:T(1,128)S(1)}, f32[512,1,128]{2,1,0:T(1,128)S(1)}, u32[]{:S(2)}, u32[]{:S(2)}) collective-permute-start(f32[512,1,128]{2,1,0:T(1,128)S(1)} %get-tuple-element.942), channel_id=1, source_target_pairs={{4,0},{8,4},{12,8},{16,12},{20,16},{24,20},{28,24},{32,28},{36,32}... | collective-permute-start | bytes 786440 | tf_op jit(solution)/shard_map/while/body/eval_jaxpr/ppermute | solution.py:19
  440.8 5.6 %collective-permute-done.1 = f32[512,1,128]{2,1,0:T(1,128)S(1)} collective-permute-done((f32[512,1,128]{2,1,0:T(1,128)S(1)}, f32[512,1,128]{2,1,0:T(1,128)S(1)}, u32[]{:S(2)}, u32[]{:S(2)}) %collective-permute-start.1) | collective-permute-done | bytes 262176 | tf_op jit(solution)/shard_map/while/body/eval_jaxpr/ppermute | solution.py:19
  457.6 7.0 %all_to_all.132 = bf16[4,2,8192]{2,1,0:T(2,128)(2,1)S(1)} all-to-all(bf16[4,2,8192]{2,1,0:T(2,128)(2,1)S(1)} %reshape.86), channel_id=1, replica_groups=mesh['blk'=128,'uly'=4] {'uly'}, dimensions={0} | all-to-all | bytes 262144 | tf_op jit(solution)/shard_map/all_to_all | solution.py:168
  464.6 16.9 %all_to_all.133 = bf16[512,8,128]{2,1,0:T(8,128)(2,1)S(1)} all-to-all(bf16[512,8,128]{2,1,0:T(8,128)(2,1)S(1)} %copy-done.4), channel_id=1, replica_groups=mesh['blk'=128,'uly'=4] {'uly'}, dimensions={0} | all-to-all | bytes 2097152 | tf_op jit(solution)/shard_map/all_to_all | solution.py:167
  488.7 10.7 %all-to-all-done.4 = bf16[512,8,128]{2,1,0:T(8,128)(2,1)S(1)} async-done(((bf16[512,8,128]{2,1,0:T(8,128)(2,1)}), bf16[512,8,128]{2,1,0:T(8,128)(2,1)S(1)}, u32[]{:S(2)}, u32[]{:S(2)}) %all-to-all-start.4) | async-done | bytes 1048608 | tf_op jit(solution)/shard_map/all_to_all | solution.py:166
  (230 shorter events, 270.3 us)
Async XLA Ops:
  18.2 18.0 %all-to-all-start.3 = ((bf16[128,32,128]{2,0,1:T(8,128)(2,1)}), bf16[128,32,128]{2,0,1:T(8,128)(2,1)S(1)}, u32[]{:S(2)}, u32[]{:S(2)}) async-start(bf16[128,32,128]{2,0,1:T(8,128)(2,1)} %copy.162), calls=%async_computation.3 | async-start | bytes 2097152 | tf_op jit(solution)/shard_map/all_to_all | solution.py:110
  36.2 175.7 %all-to-all-start = ((bf16[128,32,128]{2,0,1:T(8,128)(2,1)}), bf16[128,32,128]{2,0,1:T(8,128)(2,1)S(1)}, u32[]{:S(2)}, u32[]{:S(2)}) async-start(bf16[128,32,128]{2,0,1:T(8,128)(2,1)} %copy.150), calls=%async_computation | async-start | bytes 2097152 | tf_op jit(solution)/shard_map/all_to_all | solution.py:93
  39.7 21.8 %collective-permute-start.2 = (bf16[512,1,128]{2,1,0:T(2,128)(2,1)}, bf16[512,1,128]{2,1,0:T(2,128)(2,1)S(1)}, u32[]{:S(2)}, u32[]{:S(2)}) collective-permute-start(bf16[512,1,128]{2,1,0:T(2,128)(2,1)} %get-tuple-element.870), channel_id=1, source_target_pairs={{0,4},{4,8},{8,12},{12,16},{16,20},{20,24},{24,28},{28,32},{32,36}... | collective-permute-start | bytes 393224 | tf_op jit(solution)/shard_map/while/body/eval_jaxpr/ppermute | solution.py:19
  44.8 22.0 %collective-permute-start.3 = (bf16[512,1,128]{2,1,0:T(2,128)(2,1)}, bf16[512,1,128]{2,1,0:T(2,128)(2,1)S(1)}, u32[]{:S(2)}, u32[]{:S(2)}) collective-permute-start(bf16[512,1,128]{2,1,0:T(2,128)(2,1)} %get-tuple-element.871), channel_id=1, source_target_pairs={{0,4},{4,8},{8,12},{12,16},{16,20},{20,24},{24,28},{28,32},{32,36}... | collective-permute-start | bytes 393224 | tf_op jit(solution)/shard_map/while/body/eval_jaxpr/ppermute | solution.py:19
  68.5 18.8 %collective-permute-start.2 = (bf16[512,1,128]{2,1,0:T(2,128)(2,1)}, bf16[512,1,128]{2,1,0:T(2,128)(2,1)S(1)}, u32[]{:S(2)}, u32[]{:S(2)}) collective-permute-start(bf16[512,1,128]{2,1,0:T(2,128)(2,1)} %get-tuple-element.870), channel_id=1, source_target_pairs={{0,4},{4,8},{8,12},{12,16},{16,20},{20,24},{24,28},{28,32},{32,36}... | collective-permute-start | bytes 393224 | tf_op jit(solution)/shard_map/while/body/eval_jaxpr/ppermute | solution.py:19
  70.8 21.4 %collective-permute-start.3 = (bf16[512,1,128]{2,1,0:T(2,128)(2,1)}, bf16[512,1,128]{2,1,0:T(2,128)(2,1)S(1)}, u32[]{:S(2)}, u32[]{:S(2)}) collective-permute-start(bf16[512,1,128]{2,1,0:T(2,128)(2,1)} %get-tuple-element.871), channel_id=1, source_target_pairs={{0,4},{4,8},{8,12},{12,16},{16,20},{20,24},{24,28},{28,32},{32,36}... | collective-permute-start | bytes 393224 | tf_op jit(solution)/shard_map/while/body/eval_jaxpr/ppermute | solution.py:19
  93.8 15.9 %collective-permute-start.2 = (bf16[512,1,128]{2,1,0:T(2,128)(2,1)}, bf16[512,1,128]{2,1,0:T(2,128)(2,1)S(1)}, u32[]{:S(2)}, u32[]{:S(2)}) collective-permute-start(bf16[512,1,128]{2,1,0:T(2,128)(2,1)} %get-tuple-element.870), channel_id=1, source_target_pairs={{0,4},{4,8},{8,12},{12,16},{16,20},{20,24},{24,28},{28,32},{32,36}... | collective-permute-start | bytes 393224 | tf_op jit(solution)/shard_map/while/body/eval_jaxpr/ppermute | solution.py:19
  95.7 17.9 %collective-permute-start.3 = (bf16[512,1,128]{2,1,0:T(2,128)(2,1)}, bf16[512,1,128]{2,1,0:T(2,128)(2,1)S(1)}, u32[]{:S(2)}, u32[]{:S(2)}) collective-permute-start(bf16[512,1,128]{2,1,0:T(2,128)(2,1)} %get-tuple-element.871), channel_id=1, source_target_pairs={{0,4},{4,8},{8,12},{12,16},{16,20},{20,24},{24,28},{28,32},{32,36}... | collective-permute-start | bytes 393224 | tf_op jit(solution)/shard_map/while/body/eval_jaxpr/ppermute | solution.py:19
  115.3 15.9 %collective-permute-start.2 = (bf16[512,1,128]{2,1,0:T(2,128)(2,1)}, bf16[512,1,128]{2,1,0:T(2,128)(2,1)S(1)}, u32[]{:S(2)}, u32[]{:S(2)}) collective-permute-start(bf16[512,1,128]{2,1,0:T(2,128)(2,1)} %get-tuple-element.870), channel_id=1, source_target_pairs={{0,4},{4,8},{8,12},{12,16},{16,20},{20,24},{24,28},{28,32},{32,36}... | collective-permute-start | bytes 393224 | tf_op jit(solution)/shard_map/while/body/eval_jaxpr/ppermute | solution.py:19
  117.2 17.0 %collective-permute-start.3 = (bf16[512,1,128]{2,1,0:T(2,128)(2,1)}, bf16[512,1,128]{2,1,0:T(2,128)(2,1)S(1)}, u32[]{:S(2)}, u32[]{:S(2)}) collective-permute-start(bf16[512,1,128]{2,1,0:T(2,128)(2,1)} %get-tuple-element.871), channel_id=1, source_target_pairs={{0,4},{4,8},{8,12},{12,16},{16,20},{20,24},{24,28},{28,32},{32,36}... | collective-permute-start | bytes 393224 | tf_op jit(solution)/shard_map/while/body/eval_jaxpr/ppermute | solution.py:19
  135.8 15.1 %collective-permute-start.2 = (bf16[512,1,128]{2,1,0:T(2,128)(2,1)}, bf16[512,1,128]{2,1,0:T(2,128)(2,1)S(1)}, u32[]{:S(2)}, u32[]{:S(2)}) collective-permute-start(bf16[512,1,128]{2,1,0:T(2,128)(2,1)} %get-tuple-element.870), channel_id=1, source_target_pairs={{0,4},{4,8},{8,12},{12,16},{16,20},{20,24},{24,28},{28,32},{32,36}... | collective-permute-start | bytes 393224 | tf_op jit(solution)/shard_map/while/body/eval_jaxpr/ppermute | solution.py:19
  137.7 16.0 %collective-permute-start.3 = (bf16[512,1,128]{2,1,0:T(2,128)(2,1)}, bf16[512,1,128]{2,1,0:T(2,128)(2,1)S(1)}, u32[]{:S(2)}, u32[]{:S(2)}) collective-permute-start(bf16[512,1,128]{2,1,0:T(2,128)(2,1)} %get-tuple-element.871), channel_id=1, source_target_pairs={{0,4},{4,8},{8,12},{12,16},{16,20},{20,24},{24,28},{28,32},{32,36}... | collective-permute-start | bytes 393224 | tf_op jit(solution)/shard_map/while/body/eval_jaxpr/ppermute | solution.py:19
  155.4 14.2 %collective-permute-start.2 = (bf16[512,1,128]{2,1,0:T(2,128)(2,1)}, bf16[512,1,128]{2,1,0:T(2,128)(2,1)S(1)}, u32[]{:S(2)}, u32[]{:S(2)}) collective-permute-start(bf16[512,1,128]{2,1,0:T(2,128)(2,1)} %get-tuple-element.870), channel_id=1, source_target_pairs={{0,4},{4,8},{8,12},{12,16},{16,20},{20,24},{24,28},{28,32},{32,36}... | collective-permute-start | bytes 393224 | tf_op jit(solution)/shard_map/while/body/eval_jaxpr/ppermute | solution.py:19
  157.3 15.1 %collective-permute-start.3 = (bf16[512,1,128]{2,1,0:T(2,128)(2,1)}, bf16[512,1,128]{2,1,0:T(2,128)(2,1)S(1)}, u32[]{:S(2)}, u32[]{:S(2)}) collective-permute-start(bf16[512,1,128]{2,1,0:T(2,128)(2,1)} %get-tuple-element.871), channel_id=1, source_target_pairs={{0,4},{4,8},{8,12},{12,16},{16,20},{20,24},{24,28},{28,32},{32,36}... | collective-permute-start | bytes 393224 | tf_op jit(solution)/shard_map/while/body/eval_jaxpr/ppermute | solution.py:19
  174.1 13.3 %collective-permute-start.2 = (bf16[512,1,128]{2,1,0:T(2,128)(2,1)}, bf16[512,1,128]{2,1,0:T(2,128)(2,1)S(1)}, u32[]{:S(2)}, u32[]{:S(2)}) collective-permute-start(bf16[512,1,128]{2,1,0:T(2,128)(2,1)} %get-tuple-element.870), channel_id=1, source_target_pairs={{0,4},{4,8},{8,12},{12,16},{16,20},{20,24},{24,28},{28,32},{32,36}... | collective-permute-start | bytes 393224 | tf_op jit(solution)/shard_map/while/body/eval_jaxpr/ppermute | solution.py:19
  176.0 14.2 %collective-permute-start.3 = (bf16[512,1,128]{2,1,0:T(2,128)(2,1)}, bf16[512,1,128]{2,1,0:T(2,128)(2,1)S(1)}, u32[]{:S(2)}, u32[]{:S(2)}) collective-permute-start(bf16[512,1,128]{2,1,0:T(2,128)(2,1)} %get-tuple-element.871), channel_id=1, source_target_pairs={{0,4},{4,8},{8,12},{12,16},{16,20},{20,24},{24,28},{28,32},{32,36}... | collective-permute-start | bytes 393224 | tf_op jit(solution)/shard_map/while/body/eval_jaxpr/ppermute | solution.py:19
  191.9 13.0 %collective-permute-start.2 = (bf16[512,1,128]{2,1,0:T(2,128)(2,1)}, bf16[512,1,128]{2,1,0:T(2,128)(2,1)S(1)}, u32[]{:S(2)}, u32[]{:S(2)}) collective-permute-start(bf16[512,1,128]{2,1,0:T(2,128)(2,1)} %get-tuple-element.870), channel_id=1, source_target_pairs={{0,4},{4,8},{8,12},{12,16},{16,20},{20,24},{24,28},{28,32},{32,36}... | collective-permute-start | bytes 393224 | tf_op jit(solution)/shard_map/while/body/eval_jaxpr/ppermute | solution.py:19
  193.8 13.9 %collective-permute-start.3 = (bf16[512,1,128]{2,1,0:T(2,128)(2,1)}, bf16[512,1,128]{2,1,0:T(2,128)(2,1)S(1)}, u32[]{:S(2)}, u32[]{:S(2)}) collective-permute-start(bf16[512,1,128]{2,1,0:T(2,128)(2,1)} %get-tuple-element.871), channel_id=1, source_target_pairs={{0,4},{4,8},{8,12},{12,16},{16,20},{20,24},{24,28},{28,32},{32,36}... | collective-permute-start | bytes 393224 | tf_op jit(solution)/shard_map/while/body/eval_jaxpr/ppermute | solution.py:19
  316.3 12.1 %collective-permute-start = (f32[512,1,128]{2,1,0:T(1,128)S(1)}, f32[512,1,128]{2,1,0:T(1,128)S(1)}, u32[]{:S(2)}, u32[]{:S(2)}) collective-permute-start(f32[512,1,128]{2,1,0:T(1,128)S(1)} %get-tuple-element.942), channel_id=1, source_target_pairs={{4,0},{8,4},{12,8},{16,12},{20,16},{24,20},{28,24},{32,28},{36,32}... | collective-permute-start | bytes 786440 | tf_op jit(solution)/shard_map/while/body/eval_jaxpr/ppermute | solution.py:19
  321.0 10.3 %collective-permute-start.1 = (f32[512,1,128]{2,1,0:T(1,128)S(1)}, f32[512,1,128]{2,1,0:T(1,128)S(1)}, u32[]{:S(2)}, u32[]{:S(2)}) collective-permute-start(f32[512,1,128]{2,1,0:T(1,128)S(1)} %get-tuple-element.943), channel_id=1, source_target_pairs={{4,0},{8,4},{12,8},{16,12},{20,16},{24,20},{28,24},{32,28},{36,32}... | collective-permute-start | bytes 786440 | tf_op jit(solution)/shard_map/while/body/eval_jaxpr/ppermute | solution.py:19
  331.6 12.5 %collective-permute-start = (f32[512,1,128]{2,1,0:T(1,128)S(1)}, f32[512,1,128]{2,1,0:T(1,128)S(1)}, u32[]{:S(2)}, u32[]{:S(2)}) collective-permute-start(f32[512,1,128]{2,1,0:T(1,128)S(1)} %get-tuple-element.942), channel_id=1, source_target_pairs={{4,0},{8,4},{12,8},{16,12},{20,16},{24,20},{28,24},{32,28},{36,32}... | collective-permute-start | bytes 786440 | tf_op jit(solution)/shard_map/while/body/eval_jaxpr/ppermute | solution.py:19
  337.7 9.8 %collective-permute-start.1 = (f32[512,1,128]{2,1,0:T(1,128)S(1)}, f32[512,1,128]{2,1,0:T(1,128)S(1)}, u32[]{:S(2)}, u32[]{:S(2)}) collective-permute-start(f32[512,1,128]{2,1,0:T(1,128)S(1)} %get-tuple-element.943), channel_id=1, source_target_pairs={{4,0},{8,4},{12,8},{16,12},{20,16},{24,20},{28,24},{32,28},{36,32}... | collective-permute-start | bytes 786440 | tf_op jit(solution)/shard_map/while/body/eval_jaxpr/ppermute | solution.py:19
  347.8 11.2 %collective-permute-start = (f32[512,1,128]{2,1,0:T(1,128)S(1)}, f32[512,1,128]{2,1,0:T(1,128)S(1)}, u32[]{:S(2)}, u32[]{:S(2)}) collective-permute-start(f32[512,1,128]{2,1,0:T(1,128)S(1)} %get-tuple-element.942), channel_id=1, source_target_pairs={{4,0},{8,4},{12,8},{16,12},{20,16},{24,20},{28,24},{32,28},{36,32}... | collective-permute-start | bytes 786440 | tf_op jit(solution)/shard_map/while/body/eval_jaxpr/ppermute | solution.py:19
  353.6 9.8 %collective-permute-start.1 = (f32[512,1,128]{2,1,0:T(1,128)S(1)}, f32[512,1,128]{2,1,0:T(1,128)S(1)}, u32[]{:S(2)}, u32[]{:S(2)}) collective-permute-start(f32[512,1,128]{2,1,0:T(1,128)S(1)} %get-tuple-element.943), channel_id=1, source_target_pairs={{4,0},{8,4},{12,8},{16,12},{20,16},{24,20},{28,24},{32,28},{36,32}... | collective-permute-start | bytes 786440 | tf_op jit(solution)/shard_map/while/body/eval_jaxpr/ppermute | solution.py:19
  363.8 10.0 %collective-permute-start = (f32[512,1,128]{2,1,0:T(1,128)S(1)}, f32[512,1,128]{2,1,0:T(1,128)S(1)}, u32[]{:S(2)}, u32[]{:S(2)}) collective-permute-start(f32[512,1,128]{2,1,0:T(1,128)S(1)} %get-tuple-element.942), channel_id=1, source_target_pairs={{4,0},{8,4},{12,8},{16,12},{20,16},{24,20},{28,24},{32,28},{36,32}... | collective-permute-start | bytes 786440 | tf_op jit(solution)/shard_map/while/body/eval_jaxpr/ppermute | solution.py:19
  385.5 11.6 %collective-permute-start.1 = (f32[512,1,128]{2,1,0:T(1,128)S(1)}, f32[512,1,128]{2,1,0:T(1,128)S(1)}, u32[]{:S(2)}, u32[]{:S(2)}) collective-permute-start(f32[512,1,128]{2,1,0:T(1,128)S(1)} %get-tuple-element.943), channel_id=1, source_target_pairs={{4,0},{8,4},{12,8},{16,12},{20,16},{24,20},{28,24},{32,28},{36,32}... | collective-permute-start | bytes 786440 | tf_op jit(solution)/shard_map/while/body/eval_jaxpr/ppermute | solution.py:19
  397.5 9.9 %collective-permute-start = (f32[512,1,128]{2,1,0:T(1,128)S(1)}, f32[512,1,128]{2,1,0:T(1,128)S(1)}, u32[]{:S(2)}, u32[]{:S(2)}) collective-permute-start(f32[512,1,128]{2,1,0:T(1,128)S(1)} %get-tuple-element.942), channel_id=1, source_target_pairs={{4,0},{8,4},{12,8},{16,12},{20,16},{24,20},{28,24},{32,28},{36,32}... | collective-permute-start | bytes 786440 | tf_op jit(solution)/shard_map/while/body/eval_jaxpr/ppermute | solution.py:19
  401.5 11.7 %collective-permute-start.1 = (f32[512,1,128]{2,1,0:T(1,128)S(1)}, f32[512,1,128]{2,1,0:T(1,128)S(1)}, u32[]{:S(2)}, u32[]{:S(2)}) collective-permute-start(f32[512,1,128]{2,1,0:T(1,128)S(1)} %get-tuple-element.943), channel_id=1, source_target_pairs={{4,0},{8,4},{12,8},{16,12},{20,16},{24,20},{28,24},{32,28},{36,32}... | collective-permute-start | bytes 786440 | tf_op jit(solution)/shard_map/while/body/eval_jaxpr/ppermute | solution.py:19
  413.5 10.8 %collective-permute-start = (f32[512,1,128]{2,1,0:T(1,128)S(1)}, f32[512,1,128]{2,1,0:T(1,128)S(1)}, u32[]{:S(2)}, u32[]{:S(2)}) collective-permute-start(f32[512,1,128]{2,1,0:T(1,128)S(1)} %get-tuple-element.942), channel_id=1, source_target_pairs={{4,0},{8,4},{12,8},{16,12},{20,16},{24,20},{28,24},{32,28},{36,32}... | collective-permute-start | bytes 786440 | tf_op jit(solution)/shard_map/while/body/eval_jaxpr/ppermute | solution.py:19
  418.5 10.7 %collective-permute-start.1 = (f32[512,1,128]{2,1,0:T(1,128)S(1)}, f32[512,1,128]{2,1,0:T(1,128)S(1)}, u32[]{:S(2)}, u32[]{:S(2)}) collective-permute-start(f32[512,1,128]{2,1,0:T(1,128)S(1)} %get-tuple-element.943), channel_id=1, source_target_pairs={{4,0},{8,4},{12,8},{16,12},{20,16},{24,20},{28,24},{32,28},{36,32}... | collective-permute-start | bytes 786440 | tf_op jit(solution)/shard_map/while/body/eval_jaxpr/ppermute | solution.py:19
  429.5 11.0 %collective-permute-start = (f32[512,1,128]{2,1,0:T(1,128)S(1)}, f32[512,1,128]{2,1,0:T(1,128)S(1)}, u32[]{:S(2)}, u32[]{:S(2)}) collective-permute-start(f32[512,1,128]{2,1,0:T(1,128)S(1)} %get-tuple-element.942), channel_id=1, source_target_pairs={{4,0},{8,4},{12,8},{16,12},{20,16},{24,20},{28,24},{32,28},{36,32}... | collective-permute-start | bytes 786440 | tf_op jit(solution)/shard_map/while/body/eval_jaxpr/ppermute | solution.py:19
  481.4 18.0 %all-to-all-start.4 = ((bf16[512,8,128]{2,1,0:T(8,128)(2,1)}), bf16[512,8,128]{2,1,0:T(8,128)(2,1)S(1)}, u32[]{:S(2)}, u32[]{:S(2)}) async-start(bf16[512,8,128]{2,1,0:T(8,128)(2,1)} %get-tuple-element.428), calls=%async_computation.4 | async-start | bytes 2097152 | tf_op jit(solution)/shard_map/all_to_all | solution.py:166
  (21 other events, 302.0 us)
where the time goes:
time: 504 us; the launch traced here: 501 us
  waiting for transfers between devices  192 us (38%)
  starting transfers between devices  117 us (23%)
  local copies, waits for them, and re-layouts  66.1 us (13%)
  matrix products  60.2 us (12%)
  other arithmetic  28.8 us (6%)
  blocking collectives  23.9 us (5%)
  loops' own time  10.6 us (2%)
    ppermute x32, waiting for transfers between devices, from_behind(): return lax.ppermute(array, axis, pairs)  169 us
    ppermute x32, starting transfers between devices, from_behind(): return lax.ppermute(array, axis, pairs)  96.7 us
    while x40, local copies, waits for them, and re-layouts  19 us
    dot_general x4, matrix products, one_pair(): jnp.einsum('grc,rgd->cd', probs_low, grad_pair, preferred_element_type=jn...  18.9 us
    all_to_all x1, blocking collectives, body(): lax.all_to_all(query_grad, 'uly', split_axis=0, concat_axis=1, tiled=True)  16.9 us
    unnamed x22, local copies, waits for them, and re-layouts  13.8 us
    dot_general x4, matrix products, one_pair(): jnp.einsum('grc,cd->rgd', probs_low, value_head, preferred_element_type=j...  12.1 us
    dot_general x4, matrix products, one_pair(): jnp.einsum('rgd,cd->grc', grad_pair, value_head, preferred_element_type=j...  11.1 us
  transfers between devices with their start and end apart: 38, of which 37 were waited for; matrix products, arithmetic and copies ran while one was open for 8% of the time, Pallas kernels for 0%

commit v1 on v0

v1 whole, which is shorter than its diff:
```python
import math

import jax
import jax.numpy as jnp
from jax import lax
from jax.experimental import pallas as pl
from jax.experimental.pallas import tpu as pltpu
from jax.sharding import Mesh, PartitionSpec as P

QH = 32
KVH = 4
HD = 128
REACH = 8
ROWS = 512
HALF = 256
SCALE = 1.0 / math.sqrt(HD)
LOG2E = math.log2(math.e)
FAR = 1e30
NEG_FILL = -1e30

NN = (((1,), (0,)), ((), ()))
NT = (((1,), (1,)), ((), ()))


def dot(a, b, dims):
    return lax.dot_general(a, b, dims, preferred_element_type=jnp.float32)


def attend_kernel(
    info, q_ref, g_ref, far_ref, own_ref, att_ref, dq_ref, back_ref, mine_ref,
    keys, values, keys_t, values_t, dkeys, dvalues,
):
    head = pl.program_id(0)
    linked = info[1] > 0

    @pl.when(head == 0)
    def _():
        keys[:ROWS] = far_ref[:, :HD]
        keys[ROWS:] = own_ref[:, :HD]
        values[:ROWS] = far_ref[:, HD:]
        values[ROWS:] = own_ref[:, HD:]
        keys_t[...] = keys[...].astype(jnp.float32).T.astype(jnp.bfloat16)
        values_t[...] = values[...].astype(jnp.float32).T.astype(jnp.bfloat16)
        dkeys[...] = jnp.zeros_like(dkeys)
        dvalues[...] = jnp.zeros_like(dvalues)

    shape = (HALF, HALF)
    causal = lax.broadcasted_iota(jnp.int32, shape, 0) <= lax.broadcasted_iota(jnp.int32, shape, 1)
    for part in range(2):
        rows = slice(part * HALF, (part + 1) * HALF)
        depth = ROWS + (part + 1) * HALF
        q = q_ref[rows]
        g = g_ref[rows]
        far = dot(keys[:ROWS], q, NT)
        near = dot(keys[ROWS:depth], q, NT)
        edge = jnp.where(causal, near[depth - ROWS - HALF :], NEG_FILL)
        near = edge if part == 0 else jnp.concatenate([near[:HALF], edge], 0)
        far_top = jnp.where(linked, jnp.max(far, 0, keepdims=True), NEG_FILL)
        top = jnp.maximum(far_top, jnp.max(near, 0, keepdims=True)) * (SCALE * LOG2E)
        far_shift = jnp.where(linked, top, FAR)
        far = jnp.exp2(far * (SCALE * LOG2E) - far_shift)
        near = jnp.exp2(near * (SCALE * LOG2E) - top)
        total = jnp.sum(far, 0, keepdims=True) + jnp.sum(near, 0, keepdims=True)
        probs = jnp.concatenate([far, near], 0) * (1.0 / total)
        low = probs.astype(jnp.bfloat16)
        out = dot(values_t[:, :depth], low, NN).T.astype(jnp.bfloat16)
        att_ref[rows] = out
        dvalues[:depth] += dot(low, g, NN)
        terms = out.astype(jnp.float32) * g.astype(jnp.float32)
        delta = lax.dot_general(
            jnp.ones((8, HD), jnp.float32), terms, NT,
            preferred_element_type=jnp.float32, precision=lax.Precision.HIGHEST,
        )[:1]
        dprob = dot(values[:depth], g, NT)
        dscore = (probs * (dprob - delta)).astype(jnp.bfloat16)
        dq_ref[rows] = (dot(keys_t[:, :depth], dscore, NN) * SCALE).T.astype(jnp.bfloat16)
        dkeys[:depth] += dot(dscore, q, NN)

    @pl.when(head == pl.num_programs(0) - 1)
    def _():
        lane = info[0]
        back_ref[1 - lane] = jnp.zeros((ROWS, 2 * HD), jnp.bfloat16)
        back_ref[lane, :, :HD] = (dkeys[:ROWS] * SCALE).astype(jnp.bfloat16)
        back_ref[lane, :, HD:] = dvalues[:ROWS].astype(jnp.bfloat16)
        mine_ref[:, :HD] = (dkeys[ROWS:] * SCALE).astype(jnp.bfloat16)
        mine_ref[:, HD:] = dvalues[ROWS:].astype(jnp.bfloat16)


def attend(info, q, g, far, own):
    heads = q.shape[1] // HD
    column = pl.BlockSpec((ROWS, HD), lambda h, info: (0, h))
    kv = pl.BlockSpec((ROWS, 2 * HD), lambda h, info: (0, 0))
    spec = pltpu.PrefetchScalarGridSpec(
        num_scalar_prefetch=1,
        grid=(heads,),
        in_specs=[
            column,
            column,
            pl.BlockSpec((None, ROWS, 2 * HD), lambda h, info: (info[0], 0, 0)),
            kv,
        ],
        out_specs=[
            column,
            column,
            pl.BlockSpec((2, ROWS, 2 * HD), lambda h, info: (0, 0, 0)),
            kv,
        ],
        scratch_shapes=[
            pltpu.VMEM((2 * ROWS, HD), jnp.bfloat16),
            pltpu.VMEM((2 * ROWS, HD), jnp.bfloat16),
            pltpu.VMEM((HD, 2 * ROWS), jnp.bfloat16),
            pltpu.VMEM((HD, 2 * ROWS), jnp.bfloat16),
            pltpu.VMEM((2 * ROWS, HD), jnp.float32),
            pltpu.VMEM((2 * ROWS, HD), jnp.float32),
        ],
    )
    return pl.pallas_call(
        attend_kernel,
        grid_spec=spec,
        out_shape=[
            jax.ShapeDtypeStruct(q.shape, jnp.bfloat16),
            jax.ShapeDtypeStruct(q.shape, jnp.bfloat16),
            jax.ShapeDtypeStruct((2, ROWS, 2 * HD), jnp.bfloat16),
            jax.ShapeDtypeStruct((ROWS, 2 * HD), jnp.bfloat16),
        ],
        compiler_params=pltpu.CompilerParams(
            dimension_semantics=("arbitrary",), vmem_limit_bytes=32 * 1024 * 1024
        ),
        cost_estimate=pl.CostEstimate(
            flops=10 * 8 * 512 * 1024 * 128, bytes_accessed=6 * 1024 * 1024, transcendentals=8 * 512 * 1024
        ),
    )(info, q, g, far, own)


def gates(block_list, block_count):
    blocks = jnp.arange(block_count.shape[0], dtype=jnp.int32)
    slots = jnp.arange(block_list.shape[1], dtype=jnp.int32)
    others = (slots[None, :] < block_count[:, None]) & (block_list != blocks[:, None])
    return jnp.any(others, 1), jnp.sum(jnp.where(others, block_list, 0), 1).astype(jnp.int32)


def ring(array, by):
    peers = lax.axis_size("col")
    return lax.ppermute(array, "col", [(i, i + by) for i in range(peers) if 0 <= i + by < peers])


def to_heads(array):
    return lax.all_to_all(array, "uly", split_axis=0, concat_axis=0, tiled=True)


def body(query_states, key_states, value_states, out_grad, block_list, block_count):
    here = query_states.shape[0]
    col, side, place = lax.axis_index("col"), lax.axis_index("yh"), lax.axis_index("uly")
    block = 2 * col + side
    linked, gated = gates(block_list, block_count)
    lane = gated[block] % 2
    info = jnp.stack([lane, linked[block].astype(jnp.int32)])
    steps = REACH // 2

    kv = jnp.concatenate(
        [key_states.reshape(here, KVH, HD), value_states.reshape(here, KVH, HD)], 2
    ).transpose(1, 0, 2)
    pieces = [kv]
    for _ in range(steps):
        pieces.append(ring(pieces[-1], 1))

    q = to_heads(query_states.reshape(here, 4, -1).transpose(1, 0, 2)).reshape(4 * here, -1)
    g = to_heads(out_grad.reshape(here, 4, -1).transpose(1, 0, 2)).reshape(4 * here, -1)
    own = to_heads(kv).reshape(4 * here, 2 * HD)

    gaps = [
        jnp.where(
            linked[2 * col + i] & (gated[2 * col + i] % 2 == side), col - gated[2 * col + i] // 2, -1
        )
        for i in range(2)
    ]

    def wanted(gap):
        got = pieces[steps]
        for k in range(steps - 1, -1, -1):
            got = jnp.where(gap == k, pieces[k], got)
        return got

    sent = jnp.concatenate([wanted(gaps[0]), wanted(gaps[1])], 0)
    far = lax.all_to_all(sent, ("yh", "uly"), split_axis=0, concat_axis=0, tiled=True)
    att, dq, back, mine = attend(info, q, g, far.reshape(2, 4 * here, 2 * HD), own)

    came = lax.all_to_all(
        back.reshape(8, here, 2 * HD), ("yh", "uly"), split_axis=0, concat_axis=0, tiled=True
    ).reshape(2, 4, here, 2 * HD)

    def due(k):
        zero = jnp.zeros((), came.dtype)
        return [jnp.where(gaps[i] == k, came[i], zero).astype(jnp.float32) for i in range(2)]

    moving = sum(due(steps)).astype(jnp.bfloat16)
    for k in range(steps - 1, -1, -1):
        moving = ring(moving, -1).astype(jnp.float32) + sum(due(k))
        if k:
            moving = moving.astype(jnp.bfloat16)

    def to_tokens(array):
        moved = to_heads(array.reshape(4, here, -1))
        return moved.transpose(1, 0, 2).reshape(here, -1)

    attention = to_tokens(att)
    query_grad = to_tokens(dq)
    total = moving + to_heads(mine.reshape(4, here, 2 * HD)).astype(jnp.float32)
    total = total.astype(jnp.bfloat16).transpose(1, 0, 2)
    key_grad = total[:, :, :HD].reshape(here, -1)
    value_grad = total[:, :, HD:].reshape(here, -1)
    return attention, query_grad, key_grad, value_grad


def solution(mesh):
    blocks, places = mesh.devices.shape
    inner = Mesh(mesh.devices.reshape(blocks // 2, 2, places), ("col", "yh", "uly"))
    rows = P(("col", "yh", "uly"), None)
    return jax.shard_map(
        body,
        mesh=inner,
        in_specs=(rows, rows, rows, rows, P(), P()),
        out_specs=(rows, rows, rows, rows),
        check_vma=False,
    )
```

time: 504 us -> 186 us (0.37)
  waiting for transfers between devices: 192 us -> 69.3 us
  matrix products: 60.2 us -> 0 us
  local copies, waits for them, and re-layouts: 66.1 us -> 9.42 us
  starting transfers between devices: 117 us -> 64.1 us
  Pallas kernels: 0 us -> 28.5 us
  other arithmetic: 28.8 us -> 3.56 us
  blocking collectives: 23.9 us -> 0 us
  loops' own time: 10.6 us -> 0 us
  between operations: 2.16 us -> 9.77 us
    ppermute x32 -> x8, waiting for transfers between devices: 169 us -> 42.3 us  [ring(): lax.ppermute(array, 'col', [(i, i + by) for i in range(peers) if 0 <= i +...]
    ppermute x32 -> x8, starting transfers between devices: 96.7 us -> 35.1 us  [ring(): lax.ppermute(array, 'col', [(i, i + by) for i in range(peers) if 0 <= i +...]
    dot_general x24 -> x0, matrix products: 60.2 us -> none  [the longest x4 18.9 us: one_pair(): jnp.einsum('grc,rgd->cd', probs_low, grad_pair, preferred_element_type=jn...]
    pallas_call x0 -> x1, Pallas kernels: none -> 28.5 us  [attend(): pl.pallas_call(attend_kernel, grid_spec=spec, out_shape=[jax.ShapeDtypeSt...]
    all_to_all x2 -> x0, blocking collectives: 23.9 us -> none  [the longest x1 16.9 us: body(): lax.all_to_all(query_grad, 'uly', split_axis=0, concat_axis=1, tiled=True)]
    while x42 -> x0, local copies, waits for them, and re-layouts: 19 us -> none
    unnamed x22 -> x11, local copies, waits for them, and re-layouts: 13.8 us -> 1.62 us
    dynamic_slice x14 -> x2, local copies, waits for them, and re-layouts: 13.4 us -> 1.25 us  [the longest x1 0.66 us: body(): linked[2 * col + i] & (gated[2 * col + i] % 2 == side)]
  transfers between devices with their start and end apart: 38 -> 16, of which waited for: 37 -> 10; matrix products, arithmetic and copies ran while one was open for 8% -> 4% of each run, Pallas kernels for 0% -> 0%
where the time goes in v1:
time: 186 us; the launch traced here: 185 us
  waiting for transfers between devices  69.3 us (37%)
  starting transfers between devices  64.1 us (34%)
  Pallas kernels  28.5 us (15%)
  between operations  9.77 us (5%)
  local copies, waits for them, and re-layouts  9.42 us (5%)
  other arithmetic  3.56 us (2%)
    ppermute x8, waiting for transfers between devices, ring(): lax.ppermute(array, 'col', [(i, i + by) for i in range(peers) if 0 <= i +...  42.3 us
    ppermute x8, starting transfers between devices, ring(): lax.ppermute(array, 'col', [(i, i + by) for i in range(peers) if 0 <= i +...  35.1 us
    pallas_call x1, Pallas kernels, attend(): pl.pallas_call(attend_kernel, grid_spec=spec, out_shape=[jax.ShapeDtypeSt...  28.5 us
    all_to_all x6, starting transfers between devices, to_heads(): return lax.all_to_all(array, 'uly', split_axis=0, concat_axis=0, tiled=True)  21 us
    all_to_all x1, waiting for transfers between devices, body(): lax.all_to_all(back.reshape(8, here, 2 * HD), ('yh', 'uly'), split_axis=0...  10.3 us
    all_to_all x6, waiting for transfers between devices, to_heads(): return lax.all_to_all(array, 'uly', split_axis=0, concat_axis=0, tiled=True)  8.82 us
    all_to_all x1, waiting for transfers between devices, body(): lax.all_to_all(sent, ('yh', 'uly'), split_axis=0, concat_axis=0, tiled=True)  7.94 us
    all_to_all x1, starting transfers between devices, body(): lax.all_to_all(sent, ('yh', 'uly'), split_axis=0, concat_axis=0, tiled=True)  4.47 us
  transfers between devices with their start and end apart: 16, of which 10 were waited for; matrix products, arithmetic and copies ran while one was open for 4% of the time, Pallas kernels for 0%

profile of v1, /device:TPU:6, one launch (start us, length us, event | category | flops | bytes accessed | tf_op | source)
XLA Modules:
  0.0 184.7 jit_solution(4518185440751111897)
XLA Ops:
  3.2 3.4 %all-to-all-start.3 = ((bf16[4,128,256]{2,1,0:T(8,128)(2,1)}), bf16[4,128,256]{2,1,0:T(8,128)(2,1)S(1)}, u32[]{:S(2)}, u32[]{:S(2)}) async-start(bf16[4,128,256]{2,1,0:T(8,128)(2,1)} %maximum_bitcast_fusion), calls=%async_computation.3 | async-start | bytes 524288 | tf_op jit(solution)/shard_map/all_to_all | solution.py:148
  6.7 1.1 copy.33
  7.7 4.9 %all-to-all-done.3 = bf16[4,128,256]{2,1,0:T(8,128)(2,1)S(1)} async-done(((bf16[4,128,256]{2,1,0:T(8,128)(2,1)}), bf16[4,128,256]{2,1,0:T(8,128)(2,1)S(1)}, u32[]{:S(2)}, u32[]{:S(2)}) %all-to-all-start.3) | async-done | bytes 262176 | tf_op jit(solution)/shard_map/all_to_all | solution.py:148
  12.7 3.6 %all-to-all-start = ((bf16[4,128,1024]{2,1,0:T(8,128)(2,1)}), bf16[4,128,1024]{2,1,0:T(8,128)(2,1)S(1)}, u32[]{:S(2)}, u32[]{:S(2)}) async-start(bf16[4,128,1024]{2,1,0:T(8,128)(2,1)} %bitcast.59), calls=%async_computation | async-start | bytes 2097152 | tf_op jit(solution)/shard_map/all_to_all | solution.py:148
  16.3 3.8 %collective-permute-start = (bf16[4,128,256]{2,1,0:T(8,128)(2,1)}, bf16[4,128,256]{2,1,0:T(8,128)(2,1)S(1)}, u32[]{:S(2)}, u32[]{:S(2)}) collective-permute-start(bf16[4,128,256]{2,1,0:T(8,128)(2,1)} %maximum_bitcast_fusion), channel_id=1, source_target_pairs={{0,8},{8,16},{16,24},{24,32},{32,40},{40,48},{48,56},{56,64},{64,7... | collective-permute-start | bytes 786440 | tf_op jit(solution)/shard_map/ppermute | solution.py:144
  20.1 15.0 %collective-permute-done = bf16[4,128,256]{2,1,0:T(8,128)(2,1)S(1)} collective-permute-done((bf16[4,128,256]{2,1,0:T(8,128)(2,1)}, bf16[4,128,256]{2,1,0:T(8,128)(2,1)S(1)}, u32[]{:S(2)}, u32[]{:S(2)}) %collective-permute-start) | collective-permute-done | bytes 262176 | tf_op jit(solution)/shard_map/ppermute | solution.py:144
  35.1 1.9 %collective-permute-start.1 = (bf16[4,128,256]{2,1,0:T(8,128)(2,1)S(1)}, bf16[4,128,256]{2,1,0:T(8,128)(2,1)S(1)}, u32[]{:S(2)}, u32[]{:S(2)}) collective-permute-start(bf16[4,128,256]{2,1,0:T(8,128)(2,1)S(1)} %collective-permute-done), channel_id=1, source_target_pairs={{0,8},{8,16},{16,24},{24,32},{32,40},{40,48},{48,56},{56,64},{64,7... | collective-permute-start | bytes 786440 | tf_op jit(solution)/shard_map/ppermute | solution.py:144
  37.0 10.2 %collective-permute-done.1 = bf16[4,128,256]{2,1,0:T(8,128)(2,1)S(1)} collective-permute-done((bf16[4,128,256]{2,1,0:T(8,128)(2,1)S(1)}, bf16[4,128,256]{2,1,0:T(8,128)(2,1)S(1)}, u32[]{:S(2)}, u32[]{:S(2)}) %collective-permute-start.1) | collective-permute-done | bytes 262176 | tf_op jit(solution)/shard_map/ppermute | solution.py:144
  47.2 1.9 %collective-permute-start.2 = (bf16[4,128,256]{2,1,0:T(8,128)(2,1)S(1)}, bf16[4,128,256]{2,1,0:T(8,128)(2,1)S(1)}, u32[]{:S(2)}, u32[]{:S(2)}) collective-permute-start(bf16[4,128,256]{2,1,0:T(8,128)(2,1)S(1)} %collective-permute-done.1), channel_id=1, source_target_pairs={{0,8},{8,16},{16,24},{24,32},{32,40},{40,48},{48,56},{56,64},{64,7... | collective-permute-start | bytes 786440 | tf_op jit(solution)/shard_map/ppermute | solution.py:144
  49.1 1.1 copy.32
  50.2 3.5 %all-to-all-start.1 = ((bf16[4,128,1024]{2,1,0:T(8,128)(2,1)}), bf16[4,128,1024]{2,1,0:T(8,128)(2,1)S(1)}, u32[]{:S(2)}, u32[]{:S(2)}) async-start(bf16[4,128,1024]{2,1,0:T(8,128)(2,1)} %bitcast.57), calls=%async_computation.1 | async-start | bytes 2097152 | tf_op jit(solution)/shard_map/all_to_all | solution.py:148
  53.7 4.7 %collective-permute-done.2 = bf16[4,128,256]{2,1,0:T(8,128)(2,1)S(1)} collective-permute-done((bf16[4,128,256]{2,1,0:T(8,128)(2,1)S(1)}, bf16[4,128,256]{2,1,0:T(8,128)(2,1)S(1)}, u32[]{:S(2)}, u32[]{:S(2)}) %collective-permute-start.2) | collective-permute-done | bytes 262176 | tf_op jit(solution)/shard_map/ppermute | solution.py:144
  58.4 1.9 %collective-permute-start.3 = (bf16[4,128,256]{2,1,0:T(8,128)(2,1)S(1)}, bf16[4,128,256]{2,1,0:T(8,128)(2,1)}, u32[]{:S(2)}, u32[]{:S(2)}) collective-permute-start(bf16[4,128,256]{2,1,0:T(8,128)(2,1)S(1)} %collective-permute-done.2), channel_id=1, source_target_pairs={{0,8},{8,16},{16,24},{24,32},{32,40},{40,48},{48,56},{56,64},{64,7... | collective-permute-start | bytes 786440 | tf_op jit(solution)/shard_map/ppermute | solution.py:144
  68.9 1.2 select_select_fusion.1
  70.9 4.5 %all-to-all-start.2 = ((bf16[8,128,256]{2,1,0:T(8,128)(2,1)}), bf16[8,128,256]{2,1,0:T(8,128)(2,1)S(1)}, u32[]{:S(2)}, u32[]{:S(2)}) async-start(bf16[8,128,256]{2,1,0:T(8,128)(2,1)} %pad_maximum_fusion), calls=%async_computation.2 | async-start | bytes 1048576 | tf_op jit(solution)/shard_map/all_to_all | solution.py:185
  77.8 7.9 %all-to-all-done.2 = bf16[8,128,256]{2,1,0:T(8,128)(2,1)S(1)} async-done(((bf16[8,128,256]{2,1,0:T(8,128)(2,1)}), bf16[8,128,256]{2,1,0:T(8,128)(2,1)S(1)}, u32[]{:S(2)}, u32[]{:S(2)}) %all-to-all-start.2) | async-done | bytes 524320 | tf_op jit(solution)/shard_map/all_to_all | solution.py:185
  85.8 28.5 %shard_map.93 = (bf16[512,1024]{1,0:T(8,128)(2,1)}, bf16[512,1024]{1,0:T(8,128)(2,1)}, bf16[2,512,256]{2,1,0:T(8,128)(2,1)}, bf16[512,256]{1,0:T(8,128)(2,1)}) custom-call(s32[2]{0:T(128)S(1)} %pad_add_fusion.info, bf16[512,1024]{1,0:T(8,128)(2,1)S(1)} %bitcast.62, bf16[512,1024]{1,0:T(8,128)(2,1)S(1)} %bitcast.63, bf16[2,512,256]{2,1,0:T(8,128)(2,1)S(1)} %bitcast.64, ...), custom_call_target="tpu_custom_call" | custom-call | flops 5368709120 | bytes 6291456 | tf_op jit(solution)/shard_map/pallas_call | solution.py:117
  114.3 3.5 %all-to-all-start.6 = ((bf16[8,128,256]{2,1,0:T(8,128)(2,1)}), bf16[8,128,256]{2,1,0:T(8,128)(2,1)S(1)}, u32[]{:S(2)}, u32[]{:S(2)}) async-start(bf16[8,128,256]{2,1,0:T(8,128)(2,1)} %bitcast.17), calls=%async_computation.6 | async-start | bytes 1048576 | tf_op jit(solution)/shard_map/all_to_all | solution.py:188
  117.8 10.3 %all-to-all-done.6 = bf16[8,128,256]{2,1,0:T(8,128)(2,1)S(1)} async-done(((bf16[8,128,256]{2,1,0:T(8,128)(2,1)}), bf16[8,128,256]{2,1,0:T(8,128)(2,1)S(1)}, u32[]{:S(2)}, u32[]{:S(2)}) %all-to-all-start.6) | async-done | bytes 524320 | tf_op jit(solution)/shard_map/all_to_all | solution.py:188
  128.0 3.5 %all-to-all-start.5 = ((bf16[4,128,1024]{2,1,0:T(8,128)(2,1)}), bf16[4,128,1024]{2,1,0:T(8,128)(2,1)S(1)}, u32[]{:S(2)}, u32[]{:S(2)}) async-start(bf16[4,128,1024]{2,1,0:T(8,128)(2,1)} %bitcast.15), calls=%async_computation.5 | async-start | bytes 2097152 | tf_op jit(solution)/shard_map/all_to_all | solution.py:148
  131.7 6.0 %collective-permute-start.4 = (bf16[4,128,256]{2,1,0:T(8,128)(2,1)S(1)}, bf16[4,128,256]{2,1,0:T(8,128)(2,1)S(1)}, u32[]{:S(2)}, u32[]{:S(2)}) collective-permute-start(bf16[4,128,256]{2,1,0:T(8,128)(2,1)S(1)} %add_convert_fusion.4), channel_id=1, source_target_pairs={{8,0},{16,8},{24,16},{32,24},{40,32},{48,40},{56,48},{64,56},{72,6... | collective-permute-start | bytes 786440 | tf_op jit(solution)/shard_map/ppermute | solution.py:144
  137.7 6.2 %collective-permute-done.4 = bf16[4,128,256]{2,1,0:T(8,128)(2,1)S(1)} collective-permute-done((bf16[4,128,256]{2,1,0:T(8,128)(2,1)S(1)}, bf16[4,128,256]{2,1,0:T(8,128)(2,1)S(1)}, u32[]{:S(2)}, u32[]{:S(2)}) %collective-permute-start.4) | collective-permute-done | bytes 262176 | tf_op jit(solution)/shard_map/ppermute | solution.py:144
  144.0 6.5 %collective-permute-start.5 = (bf16[4,128,256]{2,1,0:T(8,128)(2,1)S(1)}, bf16[4,128,256]{2,1,0:T(8,128)(2,1)S(1)}, u32[]{:S(2)}, u32[]{:S(2)}) collective-permute-start(bf16[4,128,256]{2,1,0:T(8,128)(2,1)S(1)} %add_convert_fusion.3), channel_id=1, source_target_pairs={{8,0},{16,8},{24,16},{32,24},{40,32},{48,40},{56,48},{64,56},{72,6... | collective-permute-start | bytes 786440 | tf_op jit(solution)/shard_map/ppermute | solution.py:144
  150.5 3.5 %all-to-all-start.4 = ((bf16[4,128,1024]{2,1,0:T(8,128)(2,1)}), bf16[4,128,1024]{2,1,0:T(8,128)(2,1)S(1)}, u32[]{:S(2)}, u32[]{:S(2)}) async-start(bf16[4,128,1024]{2,1,0:T(8,128)(2,1)} %bitcast.13), calls=%async_computation.4 | async-start | bytes 2097152 | tf_op jit(solution)/shard_map/all_to_all | solution.py:148
  154.1 1.8 collective-permute-done.5
  156.1 6.5 %collective-permute-start.6 = (bf16[4,128,256]{2,1,0:T(8,128)(2,1)S(1)}, bf16[4,128,256]{2,1,0:T(8,128)(2,1)S(1)}, u32[]{:S(2)}, u32[]{:S(2)}) collective-permute-start(bf16[4,128,256]{2,1,0:T(8,128)(2,1)S(1)} %add_convert_fusion.2), channel_id=1, source_target_pairs={{8,0},{16,8},{24,16},{32,24},{40,32},{48,40},{56,48},{64,56},{72,6... | collective-permute-start | bytes 786440 | tf_op jit(solution)/shard_map/ppermute | solution.py:144
  162.6 4.5 %collective-permute-done.6 = bf16[4,128,256]{2,1,0:T(8,128)(2,1)S(1)} collective-permute-done((bf16[4,128,256]{2,1,0:T(8,128)(2,1)S(1)}, bf16[4,128,256]{2,1,0:T(8,128)(2,1)S(1)}, u32[]{:S(2)}, u32[]{:S(2)}) %collective-permute-start.6) | collective-permute-done | bytes 262176 | tf_op jit(solution)/shard_map/ppermute | solution.py:144
  167.2 6.5 %collective-permute-start.7 = (bf16[4,128,256]{2,1,0:T(8,128)(2,1)S(1)}, bf16[4,128,256]{2,1,0:T(8,128)(2,1)S(1)}, u32[]{:S(2)}, u32[]{:S(2)}) collective-permute-start(bf16[4,128,256]{2,1,0:T(8,128)(2,1)S(1)} %add_convert_fusion.1), channel_id=1, source_target_pairs={{8,0},{16,8},{24,16},{32,24},{40,32},{48,40},{56,48},{64,56},{72,6... | collective-permute-start | bytes 786440 | tf_op jit(solution)/shard_map/ppermute | solution.py:144
  173.7 3.4 %all-to-all-start.7 = ((bf16[4,128,256]{2,1,0:T(8,128)(2,1)}), bf16[4,128,256]{2,1,0:T(8,128)(2,1)S(1)}, u32[]{:S(2)}, u32[]{:S(2)}) async-start(bf16[4,128,256]{2,1,0:T(8,128)(2,1)} %bitcast.18), calls=%async_computation.7 | async-start | bytes 524288 | tf_op jit(solution)/shard_map/all_to_all | solution.py:148
  177.1 1.1 copy.23
  178.2 1.1 copy.22
  179.3 3.9 %all-to-all-done.7 = bf16[4,128,256]{2,1,0:T(8,128)(2,1)S(1)} async-done(((bf16[4,128,256]{2,1,0:T(8,128)(2,1)}), bf16[4,128,256]{2,1,0:T(8,128)(2,1)S(1)}, u32[]{:S(2)}, u32[]{:S(2)}) %all-to-all-start.7) | async-done | bytes 262176 | tf_op jit(solution)/shard_map/all_to_all | solution.py:148
  (32 shorter events, 7.5 us)
Async XLA Ops:
  0.6 0.9 copy-start
  0.6 6.0 %copy-start.1 = (bf16[128,4096]{1,0:T(8,128)(2,1)S(1)}, bf16[128,4096]{1,0:T(8,128)(2,1)}, u32[]{:S(2)}) copy-start(bf16[128,4096]{1,0:T(8,128)(2,1)} %param.6) | copy-start | bytes 3145732
  3.2 9.4 %all-to-all-start.3 = ((bf16[4,128,256]{2,1,0:T(8,128)(2,1)}), bf16[4,128,256]{2,1,0:T(8,128)(2,1)S(1)}, u32[]{:S(2)}, u32[]{:S(2)}) async-start(bf16[4,128,256]{2,1,0:T(8,128)(2,1)} %maximum_bitcast_fusion), calls=%async_computation.3 | async-start | bytes 524288 | tf_op jit(solution)/shard_map/all_to_all | solution.py:148
  12.7 36.5 %copy-start.2 = (bf16[128,4096]{1,0:T(8,128)(2,1)S(1)}, bf16[128,4096]{1,0:T(8,128)(2,1)}, u32[]{:S(2)}) copy-start(bf16[128,4096]{1,0:T(8,128)(2,1)} %param.9) | copy-start | bytes 3145732
  12.7 37.5 %all-to-all-start = ((bf16[4,128,1024]{2,1,0:T(8,128)(2,1)}), bf16[4,128,1024]{2,1,0:T(8,128)(2,1)S(1)}, u32[]{:S(2)}, u32[]{:S(2)}) async-start(bf16[4,128,1024]{2,1,0:T(8,128)(2,1)} %bitcast.59), calls=%async_computation | async-start | bytes 2097152 | tf_op jit(solution)/shard_map/all_to_all | solution.py:148
  16.3 18.8 %collective-permute-start = (bf16[4,128,256]{2,1,0:T(8,128)(2,1)}, bf16[4,128,256]{2,1,0:T(8,128)(2,1)S(1)}, u32[]{:S(2)}, u32[]{:S(2)}) collective-permute-start(bf16[4,128,256]{2,1,0:T(8,128)(2,1)} %maximum_bitcast_fusion), channel_id=1, source_target_pairs={{0,8},{8,16},{16,24},{24,32},{32,40},{40,48},{48,56},{56,64},{64,7... | collective-permute-start | bytes 786440 | tf_op jit(solution)/shard_map/ppermute | solution.py:144
  35.1 12.1 %collective-permute-start.1 = (bf16[4,128,256]{2,1,0:T(8,128)(2,1)S(1)}, bf16[4,128,256]{2,1,0:T(8,128)(2,1)S(1)}, u32[]{:S(2)}, u32[]{:S(2)}) collective-permute-start(bf16[4,128,256]{2,1,0:T(8,128)(2,1)S(1)} %collective-permute-done), channel_id=1, source_target_pairs={{0,8},{8,16},{16,24},{24,32},{32,40},{40,48},{48,56},{56,64},{64,7... | collective-permute-start | bytes 786440 | tf_op jit(solution)/shard_map/ppermute | solution.py:144
  47.2 11.2 %collective-permute-start.2 = (bf16[4,128,256]{2,1,0:T(8,128)(2,1)S(1)}, bf16[4,128,256]{2,1,0:T(8,128)(2,1)S(1)}, u32[]{:S(2)}, u32[]{:S(2)}) collective-permute-start(bf16[4,128,256]{2,1,0:T(8,128)(2,1)S(1)} %collective-permute-done.1), channel_id=1, source_target_pairs={{0,8},{8,16},{16,24},{24,32},{32,40},{40,48},{48,56},{56,64},{64,7... | collective-permute-start | bytes 786440 | tf_op jit(solution)/shard_map/ppermute | solution.py:144
  50.2 20.8 %all-to-all-start.1 = ((bf16[4,128,1024]{2,1,0:T(8,128)(2,1)}), bf16[4,128,1024]{2,1,0:T(8,128)(2,1)S(1)}, u32[]{:S(2)}, u32[]{:S(2)}) async-start(bf16[4,128,1024]{2,1,0:T(8,128)(2,1)} %bitcast.57), calls=%async_computation.1 | async-start | bytes 2097152 | tf_op jit(solution)/shard_map/all_to_all | solution.py:148
  58.4 10.5 %collective-permute-start.3 = (bf16[4,128,256]{2,1,0:T(8,128)(2,1)S(1)}, bf16[4,128,256]{2,1,0:T(8,128)(2,1)}, u32[]{:S(2)}, u32[]{:S(2)}) collective-permute-start(bf16[4,128,256]{2,1,0:T(8,128)(2,1)S(1)} %collective-permute-done.2), channel_id=1, source_target_pairs={{0,8},{8,16},{16,24},{24,32},{32,40},{40,48},{48,56},{56,64},{64,7... | collective-permute-start | bytes 786440 | tf_op jit(solution)/shard_map/ppermute | solution.py:144
  60.3 0.7 copy-start.3
  60.3 0.7 copy-start.4
  70.9 14.8 %all-to-all-start.2 = ((bf16[8,128,256]{2,1,0:T(8,128)(2,1)}), bf16[8,128,256]{2,1,0:T(8,128)(2,1)S(1)}, u32[]{:S(2)}, u32[]{:S(2)}) async-start(bf16[8,128,256]{2,1,0:T(8,128)(2,1)} %pad_maximum_fusion), calls=%async_computation.2 | async-start | bytes 1048576 | tf_op jit(solution)/shard_map/all_to_all | solution.py:185
  114.3 13.8 %all-to-all-start.6 = ((bf16[8,128,256]{2,1,0:T(8,128)(2,1)}), bf16[8,128,256]{2,1,0:T(8,128)(2,1)S(1)}, u32[]{:S(2)}, u32[]{:S(2)}) async-start(bf16[8,128,256]{2,1,0:T(8,128)(2,1)} %bitcast.17), calls=%async_computation.6 | async-start | bytes 1048576 | tf_op jit(solution)/shard_map/all_to_all | solution.py:188
  128.0 22.5 %all-to-all-start.5 = ((bf16[4,128,1024]{2,1,0:T(8,128)(2,1)}), bf16[4,128,1024]{2,1,0:T(8,128)(2,1)S(1)}, u32[]{:S(2)}, u32[]{:S(2)}) async-start(bf16[4,128,1024]{2,1,0:T(8,128)(2,1)} %bitcast.15), calls=%async_computation.5 | async-start | bytes 2097152 | tf_op jit(solution)/shard_map/all_to_all | solution.py:148
  131.7 12.2 %collective-permute-start.4 = (bf16[4,128,256]{2,1,0:T(8,128)(2,1)S(1)}, bf16[4,128,256]{2,1,0:T(8,128)(2,1)S(1)}, u32[]{:S(2)}, u32[]{:S(2)}) collective-permute-start(bf16[4,128,256]{2,1,0:T(8,128)(2,1)S(1)} %add_convert_fusion.4), channel_id=1, source_target_pairs={{8,0},{16,8},{24,16},{32,24},{40,32},{48,40},{56,48},{64,56},{72,6... | collective-permute-start | bytes 786440 | tf_op jit(solution)/shard_map/ppermute | solution.py:144
  144.0 11.9 %collective-permute-start.5 = (bf16[4,128,256]{2,1,0:T(8,128)(2,1)S(1)}, bf16[4,128,256]{2,1,0:T(8,128)(2,1)S(1)}, u32[]{:S(2)}, u32[]{:S(2)}) collective-permute-start(bf16[4,128,256]{2,1,0:T(8,128)(2,1)S(1)} %add_convert_fusion.3), channel_id=1, source_target_pairs={{8,0},{16,8},{24,16},{32,24},{40,32},{48,40},{56,48},{64,56},{72,6... | collective-permute-start | bytes 786440 | tf_op jit(solution)/shard_map/ppermute | solution.py:144
  150.5 23.1 %all-to-all-start.4 = ((bf16[4,128,1024]{2,1,0:T(8,128)(2,1)}), bf16[4,128,1024]{2,1,0:T(8,128)(2,1)S(1)}, u32[]{:S(2)}, u32[]{:S(2)}) async-start(bf16[4,128,1024]{2,1,0:T(8,128)(2,1)} %bitcast.13), calls=%async_computation.4 | async-start | bytes 2097152 | tf_op jit(solution)/shard_map/all_to_all | solution.py:148
  156.1 11.0 %collective-permute-start.6 = (bf16[4,128,256]{2,1,0:T(8,128)(2,1)S(1)}, bf16[4,128,256]{2,1,0:T(8,128)(2,1)S(1)}, u32[]{:S(2)}, u32[]{:S(2)}) collective-permute-start(bf16[4,128,256]{2,1,0:T(8,128)(2,1)S(1)} %add_convert_fusion.2), channel_id=1, source_target_pairs={{8,0},{16,8},{24,16},{32,24},{40,32},{48,40},{56,48},{64,56},{72,6... | collective-permute-start | bytes 786440 | tf_op jit(solution)/shard_map/ppermute | solution.py:144
  167.2 15.9 %collective-permute-start.7 = (bf16[4,128,256]{2,1,0:T(8,128)(2,1)S(1)}, bf16[4,128,256]{2,1,0:T(8,128)(2,1)S(1)}, u32[]{:S(2)}, u32[]{:S(2)}) collective-permute-start(bf16[4,128,256]{2,1,0:T(8,128)(2,1)S(1)} %add_convert_fusion.1), channel_id=1, source_target_pairs={{8,0},{16,8},{24,16},{32,24},{40,32},{48,40},{56,48},{64,56},{72,6... | collective-permute-start | bytes 786440 | tf_op jit(solution)/shard_map/ppermute | solution.py:144
  173.7 9.4 %all-to-all-start.7 = ((bf16[4,128,256]{2,1,0:T(8,128)(2,1)}), bf16[4,128,256]{2,1,0:T(8,128)(2,1)S(1)}, u32[]{:S(2)}, u32[]{:S(2)}) async-start(bf16[4,128,256]{2,1,0:T(8,128)(2,1)} %bitcast.18), calls=%async_computation.7 | async-start | bytes 524288 | tf_op jit(solution)/shard_map/all_to_all | solution.py:148

commit v2 on v1

v2 whole, which is shorter than its diff:
```python
import math

import jax
import jax.numpy as jnp
from jax import lax
from jax.experimental import pallas as pl
from jax.experimental.pallas import tpu as pltpu
from jax.sharding import Mesh, PartitionSpec as P

HD = 128
ROWS = 512
HALF = 256
SCALE = 1.0 / math.sqrt(HD)
SCALE2 = SCALE * math.log2(math.e)
FAR = 1e30
NEG_FILL = -1e30
STEPS = 4
HPS = 4
MIB = 1024 * 1024
NN = (((1,), (0,)), ((), ()))
NT = (((1,), (1,)), ((), ()))


def dot(a, b, dims):
    return lax.dot_general(a, b, dims, preferred_element_type=jnp.float32)


def turned(x):
    return x.astype(jnp.float32).T.astype(jnp.bfloat16)


def causal_mask():
    shape = (HALF, HALF)
    return lax.broadcasted_iota(jnp.int32, shape, 0) <= lax.broadcasted_iota(jnp.int32, shape, 1)


def units():
    return [(h, part) for h in range(HPS) for part in range(2)]


def rows_of(part):
    return slice(part * HALF, (part + 1) * HALF)


def cols_of(h):
    return slice(h * HD, (h + 1) * HD)


def own_scores(keys, q_ref, causal):
    out = []
    for h, part in units():
        s = dot(keys[: (part + 1) * HALF], q_ref[rows_of(part), cols_of(h)], NT)
        edge = jnp.where(causal, s[part * HALF :], NEG_FILL)
        out.append(edge if part == 0 else jnp.concatenate([s[:HALF], edge], 0))
    return out


def near_kernel(q_ref, g_ref, own_ref, out_ref, stat_ref, values_t):
    @pl.when(pl.program_id(0) == 0)
    def _():
        values_t[...] = turned(own_ref[:, HD:])

    keys, values = own_ref.at[:, :HD], own_ref.at[:, HD:]
    scores = own_scores(keys, q_ref, causal_mask())
    tops = [jnp.max(s, 0, keepdims=True) for s in scores]
    probs = [jnp.exp2((s - t) * SCALE2) for s, t in zip(scores, tops)]
    dprobs = [
        dot(values[: (part + 1) * HALF], g_ref[rows_of(part), cols_of(h)], NT) for h, part in units()
    ]
    for (h, part), t, p, d in zip(units(), tops, probs, dprobs):
        rows = rows_of(part)
        out_ref[h, :, rows] = dot(values_t[:, : (part + 1) * HALF], p.astype(jnp.bfloat16), NN)
        stat_ref[h, 0:1, rows] = t
        stat_ref[h, 1:2, rows] = jnp.sum(p, 0, keepdims=True)
        stat_ref[h, 2:3, rows] = jnp.sum(p * d, 0, keepdims=True)


def far_kernel(info, q_ref, g_ref, far_ref, out_ref, stat_ref, att_ref, part_ref, line_ref, back_ref,
               keys_t, values_t, dkeys, dvalues):
    step = pl.program_id(0)
    linked = info[1] > 0

    @pl.when(step == 0)
    def _():
        keys_t[...] = turned(far_ref[:, :HD])
        values_t[...] = turned(far_ref[:, HD:])
        dkeys[...] = jnp.zeros_like(dkeys)
        dvalues[...] = jnp.zeros_like(dvalues)

    keys, values = far_ref[:, :HD], far_ref[:, HD:]
    todo = units()

    def first(h, part):
        q, g = q_ref[rows_of(part), cols_of(h)], g_ref[rows_of(part), cols_of(h)]
        return dot(keys, q, NT), dot(values, g, NT), q, g

    ahead = first(*todo[0])
    for at, (h, part) in enumerate(todo):
        s, d, q, g = ahead
        if at + 1 < len(todo):
            ahead = first(*todo[at + 1])
        rows = rows_of(part)
        near_top = stat_ref[h, 0:1, rows]
        far_top = jnp.where(linked, jnp.max(s, 0, keepdims=True), NEG_FILL)
        top = jnp.maximum(far_top, near_top)
        p = jnp.exp2((s - jnp.where(linked, top, FAR)) * SCALE2)
        fade = jnp.exp2((near_top - top) * SCALE2)
        total = jnp.sum(p, 0, keepdims=True) + fade * stat_ref[h, 1:2, rows]
        inv = 1.0 / total
        fade = fade * inv
        p = p * inv
        delta = jnp.sum(p * d, 0, keepdims=True) + fade * stat_ref[h, 2:3, rows]
        line_ref[h, 0:1, rows] = top * SCALE2 + jnp.log2(total)
        line_ref[h, 1:2, rows] = delta
        low = p.astype(jnp.bfloat16)
        ds = (p * (d - delta)).astype(jnp.bfloat16)
        att_ref[h, :, rows] = (dot(values_t[...], low, NN) + fade * out_ref[h, :, rows]).astype(jnp.bfloat16)
        part_ref[h, :, rows] = dot(keys_t[...], ds, NN)
        dvalues[...] += dot(low, g, NN)
        dkeys[...] += dot(ds, q, NN)

    @pl.when(step == pl.num_programs(0) - 1)
    def _():
        lane = info[0]
        back_ref[1 - lane] = jnp.zeros((ROWS, 2 * HD), jnp.bfloat16)
        back_ref[lane, :, :HD] = (dkeys[...] * SCALE).astype(jnp.bfloat16)
        back_ref[lane, :, HD:] = dvalues[...].astype(jnp.bfloat16)


def rest_kernel(q_ref, g_ref, own_ref, out_ref, part_ref, line_ref, all_ref, keys_t, dkeys, dvalues):
    step = pl.program_id(0)
    width = HPS * HD
    half = (all_ref.shape[1] - 2 * HD) // 2

    @pl.when(step == 0)
    def _():
        keys_t[...] = turned(own_ref[:, :HD])
        dkeys[...] = jnp.zeros_like(dkeys)
        dvalues[...] = jnp.zeros_like(dvalues)

    keys, values = own_ref.at[:, :HD], own_ref.at[:, HD:]
    scores = own_scores(keys, q_ref, causal_mask())
    dprobs = [
        dot(values[: (part + 1) * HALF], g_ref[rows_of(part), cols_of(h)], NT) for h, part in units()
    ]
    lows, dscores = [], []
    for (h, part), s, d in zip(units(), scores, dprobs):
        rows = rows_of(part)
        p = jnp.exp2(s * SCALE2 - line_ref[h, 0:1, rows])
        lows.append(p.astype(jnp.bfloat16))
        dscores.append((p * (d - line_ref[h, 1:2, rows])).astype(jnp.bfloat16))
    for (h, part), ds in zip(units(), dscores):
        rows = rows_of(part)
        at = pl.multiple_of(step * width + h * HD, HD)
        all_ref[rows, pl.ds(at, HD)] = turned(out_ref[h, :, rows])
        dq = dot(keys_t[:, : (part + 1) * HALF], ds, NN) + part_ref[h, :, rows]
        all_ref[rows, pl.ds(half + at, HD)] = (dq * SCALE).T.astype(jnp.bfloat16)
    for (h, part), p, ds in zip(units(), lows, dscores):
        depth = (part + 1) * HALF
        dvalues[:depth] += dot(p, g_ref[rows_of(part), cols_of(h)], NN)
        dkeys[:depth] += dot(ds, q_ref[rows_of(part), cols_of(h)], NN)

    @pl.when(step == pl.num_programs(0) - 1)
    def _():
        tail = all_ref.shape[1] - 2 * HD
        all_ref[:, tail : tail + HD] = (dkeys[...] * SCALE).astype(jnp.bfloat16)
        all_ref[:, tail + HD :] = dvalues[...].astype(jnp.bfloat16)


def sds(shape, dtype=jnp.float32):
    return jax.ShapeDtypeStruct(shape, dtype)


def params(mib):
    return pltpu.CompilerParams(
        dimension_semantics=("arbitrary",), vmem_limit_bytes=mib * MIB
    )


def heads_of(x):
    return (x.shape[1] // HD - 2) // 2


def column(start=0):
    return pl.BlockSpec((ROWS, HPS * HD), lambda h, *_: (0, start // HPS + h))


def stack(rows):
    return pl.BlockSpec((HPS, rows, ROWS), lambda h, *_: (h, 0, 0))


def tail_of(heads):
    return pl.BlockSpec((ROWS, 2 * HD), lambda h, *_: (0, heads))


def whole(shape):
    return pl.BlockSpec(shape, lambda h, *_: (0,) * len(shape))


def near_pass(x):
    heads = heads_of(x)
    return pl.pallas_call(
        near_kernel,
        grid=(heads // HPS,),
        in_specs=[column(), column(heads), tail_of(heads)],
        out_specs=[stack(HD), stack(8)],
        scratch_shapes=[pltpu.VMEM((HD, ROWS), jnp.bfloat16)],
        out_shape=[sds((heads, HD, ROWS)), sds((heads, 8, ROWS))],
        compiler_params=params(24),
        cost_estimate=pl.CostEstimate(flops=3 * 10**9, bytes_accessed=4 * 2**20, transcendentals=2**21),
    )(x, x, x)


def far_pass(info, x, far, out, stats):
    heads = heads_of(x)
    acc = pltpu.VMEM((ROWS, HD), jnp.float32)
    turn = pltpu.VMEM((HD, ROWS), jnp.bfloat16)
    return pl.pallas_call(
        far_kernel,
        grid_spec=pltpu.PrefetchScalarGridSpec(
            num_scalar_prefetch=1,
            grid=(heads // HPS,),
            in_specs=[
                column(), column(heads),
                pl.BlockSpec((None, ROWS, 2 * HD), lambda h, info: (info[0], 0, 0)),
                stack(HD), stack(8),
            ],
            out_specs=[stack(HD), stack(HD), stack(8), whole((2, ROWS, 2 * HD))],
            scratch_shapes=[turn, turn, acc, acc],
        ),
        out_shape=[
            sds((heads, HD, ROWS), jnp.bfloat16), sds((heads, HD, ROWS)), sds((heads, 8, ROWS)),
            sds((2, ROWS, 2 * HD), jnp.bfloat16),
        ],
        compiler_params=params(24),
        cost_estimate=pl.CostEstimate(flops=6 * 10**9, bytes_accessed=8 * 2**20, transcendentals=2**21),
    )(info, x, x, far, out, stats)


def rest_pass(x, out, part, lines):
    heads = heads_of(x)
    acc = pltpu.VMEM((ROWS, HD), jnp.float32)
    return pl.pallas_call(
        rest_kernel,
        grid=(heads // HPS,),
        in_specs=[column(), column(heads), tail_of(heads), stack(HD), stack(HD), stack(8)],
        out_specs=whole(x.shape),
        scratch_shapes=[pltpu.VMEM((HD, ROWS), jnp.bfloat16), acc, acc],
        out_shape=sds(x.shape, jnp.bfloat16),
        compiler_params=params(24),
        cost_estimate=pl.CostEstimate(flops=5 * 10**9, bytes_accessed=6 * 2**20, transcendentals=2**21),
    )(x, x, x, out, part, lines)


def gate_kernel(list_ref, count_ref, info_ref):
    col, side = lax.axis_index("col"), lax.axis_index("yh")

    def gate(block):
        count = count_ref[block]
        linked, gated = jnp.int32(0), jnp.int32(0)
        for slot in range(list_ref.shape[0]):
            entry = list_ref[slot, block]
            other = jnp.logical_and(slot < count, entry != block)
            linked = jnp.where(other, 1, linked)
            gated = jnp.where(other, entry, gated)
        return linked, gated

    linked, gated = gate(2 * col + side)
    info_ref[0] = gated % 2
    info_ref[1] = linked
    for i in range(2):
        linked, gated = gate(2 * col + i)
        mine = jnp.logical_and(linked > 0, gated % 2 == side)
        gap = jnp.where(mine, col - gated // 2, -1)
        info_ref[2 + i] = gap


def gate_pass(block_list, block_count):
    smem = pl.BlockSpec(memory_space=pltpu.SMEM)
    return pl.pallas_call(
        gate_kernel,
        in_specs=[smem, smem],
        out_specs=smem,
        out_shape=sds((4,), jnp.int32),
        compiler_params=pltpu.CompilerParams(vmem_limit_bytes=2 * MIB),
    )(block_list.T, block_count)


def pick_kernel(info, *refs):
    out, pieces = refs[-1], refs[:-1]
    heads = pieces[0].shape[0]
    for i in range(2):
        for k, piece in enumerate(pieces):

            @pl.when(info[2 + i] == k if k else info[2 + i] <= 0)
            def _():
                out[i * heads : (i + 1) * heads] = piece[...]


def pick_pass(info, pieces):
    heads, rows, width = pieces[0].shape
    vmem = pl.BlockSpec(memory_space=pltpu.VMEM)
    return pl.pallas_call(
        pick_kernel,
        in_specs=[pl.BlockSpec(memory_space=pltpu.SMEM)] + [vmem] * len(pieces),
        out_specs=vmem,
        out_shape=sds((2 * heads, rows, width), jnp.bfloat16),
        compiler_params=pltpu.CompilerParams(vmem_limit_bytes=8 * MIB),
    )(info, *pieces)


def pack_kernel(key_ref, value_ref, out_ref):
    for h in range(out_ref.shape[0]):
        out_ref[h, :, :HD] = key_ref[:, cols_of(h)]
        out_ref[h, :, HD:] = value_ref[:, cols_of(h)]


def pack_pass(keys, values):
    rows, width = keys.shape
    vmem = pl.BlockSpec(memory_space=pltpu.VMEM)
    return pl.pallas_call(
        pack_kernel,
        in_specs=[vmem, vmem],
        out_specs=vmem,
        out_shape=sds((width // HD, rows, 2 * HD), jnp.bfloat16),
        compiler_params=pltpu.CompilerParams(vmem_limit_bytes=4 * MIB),
    )(keys, values)


def join_kernel(q_ref, g_ref, kv_ref, out_ref):
    width = q_ref.shape[1]
    out_ref[:, :width] = q_ref[...]
    out_ref[:, width : 2 * width] = g_ref[...]
    out_ref[:, 2 * width :] = kv_ref[...]


def join_pass(q, g, kv):
    heads, rows, pair = kv.shape
    width = q.shape[1] // heads
    block = pl.BlockSpec((rows, width), lambda h: (0, h))
    return pl.pallas_call(
        join_kernel,
        grid=(heads,),
        in_specs=[block, block, pl.BlockSpec((None, rows, pair), lambda h: (h, 0, 0))],
        out_specs=pl.BlockSpec((None, rows, 2 * width + pair), lambda h: (h, 0, 0)),
        out_shape=sds((heads, rows, 2 * width + pair), jnp.bfloat16),
        compiler_params=params(8),
    )(q, g, kv)


def split_kernel(all_ref, att_ref, dq_ref, mine_ref):
    width = att_ref.shape[1]
    att_ref[...] = all_ref[:, :width]
    dq_ref[...] = all_ref[:, width : 2 * width]
    mine_ref[...] = all_ref[:, 2 * width :]


def split_pass(grads):
    heads, rows, total = grads.shape
    pair = 2 * HD
    width = (total - pair) // 2
    block = pl.BlockSpec((rows, width), lambda h: (0, h))
    wide = sds((rows, heads * width), jnp.bfloat16)
    return pl.pallas_call(
        split_kernel,
        grid=(heads,),
        in_specs=[pl.BlockSpec((None, rows, total), lambda h: (h, 0, 0))],
        out_specs=[block, block, pl.BlockSpec((None, rows, pair), lambda h: (h, 0, 0))],
        out_shape=[wide, wide, sds((heads, rows, pair), jnp.bfloat16)],
        compiler_params=params(8),
    )(grads)


def due_kernel(info, came_ref, *outs):
    zero = jnp.zeros(outs[0].shape, outs[0].dtype)
    for k, out in enumerate(outs):
        both = jnp.logical_and(info[2] == k, info[3] == k)

        @pl.when(both)
        def _():
            out[...] = came_ref[0] + came_ref[1]

        @pl.when(jnp.logical_not(both))
        def _():
            out[...] = zero

            for i in range(2):

                @pl.when(info[2 + i] == k)
                def _():
                    out[...] = came_ref[i]


def due_pass(info, came):
    vmem = pl.BlockSpec(memory_space=pltpu.VMEM)
    return pl.pallas_call(
        due_kernel,
        in_specs=[pl.BlockSpec(memory_space=pltpu.SMEM), vmem],
        out_specs=[vmem] * (STEPS + 1),
        out_shape=[sds(came.shape[1:], jnp.bfloat16)] * (STEPS + 1),
        compiler_params=pltpu.CompilerParams(vmem_limit_bytes=8 * MIB),
    )(info, came)


def finish_kernel(came_ref, due_ref, mine_ref, key_ref, value_ref):
    wide = jnp.float32
    for h in range(came_ref.shape[0]):
        total = came_ref[h].astype(wide) + due_ref[h].astype(wide) + mine_ref[h].astype(wide)
        key_ref[:, cols_of(h)] = total[:, :HD].astype(jnp.bfloat16)
        value_ref[:, cols_of(h)] = total[:, HD:].astype(jnp.bfloat16)


def finish_pass(came, due, mine):
    heads, rows, _ = came.shape
    vmem = pl.BlockSpec(memory_space=pltpu.VMEM)
    out = sds((rows, heads * HD), jnp.bfloat16)
    return pl.pallas_call(
        finish_kernel,
        in_specs=[vmem] * 3,
        out_specs=[vmem] * 2,
        out_shape=[out, out],
        compiler_params=pltpu.CompilerParams(vmem_limit_bytes=8 * MIB),
    )(came, due, mine)


def ring(array, by):
    peers = lax.axis_size("col")
    return lax.ppermute(array, "col", [(i, i + by) for i in range(peers) if 0 <= i + by < peers])


def to_heads(array):
    return lax.all_to_all(array, "uly", split_axis=0, concat_axis=0, tiled=True)


def across(array):
    return lax.all_to_all(array, ("yh", "uly"), split_axis=0, concat_axis=0, tiled=True)


def after(array, *others):
    return lax.optimization_barrier((array, *others))[0]


def body(query_states, key_states, value_states, out_grad, block_list, block_count):
    here = query_states.shape[0]
    pair = 2 * HD

    kv = pack_pass(key_states, value_states)
    info = gate_pass(after(block_list, kv), block_count)

    pieces = [kv]
    for _ in range(STEPS):
        pieces.append(ring(pieces[-1], 1))
    x = join_pass(query_states, out_grad, kv)
    x = to_heads(after(x, pieces[1])).reshape(4 * here, -1)
    near, stats = near_pass(x)
    far = across(after(pick_pass(info, pieces), x)).reshape(2, 4 * here, pair)
    out, part, lines, back = far_pass(info, x, far, near, stats)

    came = across(back.reshape(8, here, pair)).reshape(2, 4, here, pair)
    grads = rest_pass(x, out, part, lines)
    came, grads = lax.optimization_barrier((came, grads))
    grads = to_heads(grads.reshape(4, here, -1))
    due = due_pass(info, came)
    moving = due[STEPS]
    for k in range(STEPS - 1, -1, -1):
        moving = ring(moving, -1)
        if k:
            moving = (moving.astype(jnp.float32) + due[k].astype(jnp.float32)).astype(jnp.bfloat16)

    attention, query_grad, mine = split_pass(grads)
    key_grad, value_grad = finish_pass(moving, due[0], mine)
    return attention, query_grad, key_grad, value_grad


def solution(mesh):
    blocks, places = mesh.devices.shape
    inner = Mesh(mesh.devices.reshape(blocks // 2, 2, places), ("col", "yh", "uly"))
    rows = P(("col", "yh", "uly"), None)
    return jax.shard_map(
        body,
        mesh=inner,
        in_specs=(rows, rows, rows, rows, P(), P()),
        out_specs=(rows, rows, rows, rows),
        check_vma=False,
    )
```

time: 186 us -> 150 us (0.81)
  starting transfers between devices: 64.1 us -> 44.1 us
  between operations: 9.77 us -> 0.85 us
  waiting for transfers between devices: 69.3 us -> 60.5 us
  local copies, waits for them, and re-layouts: 9.42 us -> 15.1 us
  Pallas kernels: 28.5 us -> 25.9 us
    all_to_all x6 -> x2, starting transfers between devices: 21 us -> 7.4 us  [to_heads(): return lax.all_to_all(array, 'uly', split_axis=0, concat_axis=0, tiled=True)]
    unnamed x11 -> x34, local copies, waits for them, and re-layouts: 1.62 us -> 15.1 us
    ppermute x8, waiting for transfers between devices: 42.3 us -> 53.5 us  [ring(): lax.ppermute(array, 'col', [(i, i + by) for i in range(peers) if 0 <= i +...]
    all_to_all x2, waiting for transfers between devices: 18.2 us -> 7.08 us  [across(): lax.all_to_all(array, ('yh', 'uly'), split_axis=0, concat_axis=0, tiled=T...]
    all_to_all x6 -> x2, waiting for transfers between devices: 8.82 us -> 0.01 us  [to_heads(): return lax.all_to_all(array, 'uly', split_axis=0, concat_axis=0, tiled=True)]
    reshape x7 -> x0, local copies, waits for them, and re-layouts: 6.55 us -> none  [the longest x2 2.13 us: to_tokens(): return moved.transpose(1, 0, 2).reshape(here, -1)]
    ppermute x8, starting transfers between devices: 35.1 us -> 28.8 us  [ring(): lax.ppermute(array, 'col', [(i, i + by) for i in range(peers) if 0 <= i +...]
    pallas_call x1 -> x10, Pallas kernels: 28.5 us -> 25.9 us  [the longest x1 9.19 us: far_pass(): pl.pallas_call(far_kernel, grid_spec=pltpu.PrefetchScalarGridSpec(num_sca...]
  transfers between devices with their start and end apart: 16 -> 12, of which waited for: 10 -> 10; matrix products, arithmetic and copies ran while one was open for 4% -> 1% of each run, Pallas kernels for 0% -> 10%
where the time goes in v2:
time: 150 us; the launch traced here: 148 us
  waiting for transfers between devices  60.5 us (40%)
  starting transfers between devices  44.1 us (29%)
  Pallas kernels  25.9 us (17%)
  local copies, waits for them, and re-layouts  15.1 us (10%)
  other arithmetic  1.85 us (1%)
    ppermute x8, waiting for transfers between devices, ring(): lax.ppermute(array, 'col', [(i, i + by) for i in range(peers) if 0 <= i +...  53.5 us
    ppermute x8, starting transfers between devices, ring(): lax.ppermute(array, 'col', [(i, i + by) for i in range(peers) if 0 <= i +...  28.8 us
    unnamed x34, local copies, waits for them, and re-layouts  15.1 us
    pallas_call x1, Pallas kernels, far_pass(): pl.pallas_call(far_kernel, grid_spec=pltpu.PrefetchScalarGridSpec(num_sca...  9.19 us
    all_to_all x2, starting transfers between devices, across(): lax.all_to_all(array, ('yh', 'uly'), split_axis=0, concat_axis=0, tiled=T...  7.97 us
    all_to_all x2, starting transfers between devices, to_heads(): return lax.all_to_all(array, 'uly', split_axis=0, concat_axis=0, tiled=True)  7.4 us
    all_to_all x2, waiting for transfers between devices, across(): lax.all_to_all(array, ('yh', 'uly'), split_axis=0, concat_axis=0, tiled=T...  7.08 us
    pallas_call x1, Pallas kernels, rest_pass(): pl.pallas_call(rest_kernel, grid=(heads // HPS,), in_specs=[column(), col...  4.58 us
  transfers between devices with their start and end apart: 12, of which 10 were waited for; matrix products, arithmetic and copies ran while one was open for 1% of the time, Pallas kernels for 10%

profile of v2, /device:TPU:6, one launch (start us, length us, event | category | flops | bytes accessed | tf_op | source)
XLA Modules:
  0.0 148.4 jit_solution(7372379800392813639)
XLA Ops:
  2.5 3.8 %collective-permute-start = (bf16[4,128,256]{2,1,0:T(8,128)(2,1)S(1)}, bf16[4,128,256]{2,1,0:T(8,128)(2,1)S(1)}, u32[]{:S(2)}, u32[]{:S(2)}) collective-permute-start(bf16[4,128,256]{2,1,0:T(8,128)(2,1)S(1)} %shard_map.93.kv_ref.refs_0_), channel_id=1, source_target_pairs={{0,8},{8,16},{16,24},{24,32},{32,40},{40,48},{48,56},{56,64},{64,7... | collective-permute-start | bytes 786440 | tf_op jit(solution)/shard_map/ppermute | solution.py:428
  8.8 2.0 %shard_map.95 = bf16[4,128,2304]{2,1,0:T(8,128)(2,1)} custom-call(bf16[128,4096]{1,0:T(8,128)(2,1)S(1)} %copy-done.1, bf16[128,4096]{1,0:T(8,128)(2,1)S(1)} %copy-done.2, bf16[4,128,256]{2,1,0:T(8,128)(2,1)S(1)} %shard_map.93.kv_ref.refs_0_), custom_call_target="tpu_custom_call" | custom-call | tf_op jit(solution)/shard_map/pallas_call | solution.py:341
  10.8 9.6 %collective-permute-done.refs_1_ = bf16[4,128,256]{2,1,0:T(8,128)(2,1)S(1)} collective-permute-done((bf16[4,128,256]{2,1,0:T(8,128)(2,1)S(1)}, bf16[4,128,256]{2,1,0:T(8,128)(2,1)S(1)}, u32[]{:S(2)}, u32[]{:S(2)}) %collective-permute-start) | collective-permute-done | bytes 262176 | tf_op jit(solution)/shard_map/ppermute | solution.py:428
  20.5 3.6 %all-to-all-start = ((bf16[4,128,2304]{2,1,0:T(8,128)(2,1)}), bf16[4,128,2304]{2,1,0:T(8,128)(2,1)S(1)}, u32[]{:S(2)}, u32[]{:S(2)}) async-start(bf16[4,128,2304]{2,1,0:T(8,128)(2,1)} %shard_map.95), calls=%async_computation | async-start | bytes 4718592 | tf_op jit(solution)/shard_map/all_to_all | solution.py:432
  24.1 1.9 %collective-permute-start.1 = (bf16[4,128,256]{2,1,0:T(8,128)(2,1)S(1)}, bf16[4,128,256]{2,1,0:T(8,128)(2,1)S(1)}, u32[]{:S(2)}, u32[]{:S(2)}) collective-permute-start(bf16[4,128,256]{2,1,0:T(8,128)(2,1)S(1)} %collective-permute-done.refs_1_), channel_id=1, source_target_pairs={{0,8},{8,16},{16,24},{24,32},{32,40},{40,48},{48,56},{56,64},{64,7... | collective-permute-start | bytes 786440 | tf_op jit(solution)/shard_map/ppermute | solution.py:428
  26.0 10.7 %collective-permute-done.1.refs_2_ = bf16[4,128,256]{2,1,0:T(8,128)(2,1)S(1)} collective-permute-done((bf16[4,128,256]{2,1,0:T(8,128)(2,1)S(1)}, bf16[4,128,256]{2,1,0:T(8,128)(2,1)S(1)}, u32[]{:S(2)}, u32[]{:S(2)}) %collective-permute-start.1) | collective-permute-done | bytes 262176 | tf_op jit(solution)/shard_map/ppermute | solution.py:428
  36.8 1.9 %collective-permute-start.2 = (bf16[4,128,256]{2,1,0:T(8,128)(2,1)S(1)}, bf16[4,128,256]{2,1,0:T(8,128)(2,1)S(1)}, u32[]{:S(2)}, u32[]{:S(2)}) collective-permute-start(bf16[4,128,256]{2,1,0:T(8,128)(2,1)S(1)} %collective-permute-done.1.refs_2_), channel_id=1, source_target_pairs={{0,8},{8,16},{16,24},{24,32},{32,40},{40,48},{48,56},{56,64},{64,7... | collective-permute-start | bytes 786440 | tf_op jit(solution)/shard_map/ppermute | solution.py:428
  38.7 10.0 %collective-permute-done.2.refs_3_ = bf16[4,128,256]{2,1,0:T(8,128)(2,1)S(1)} collective-permute-done((bf16[4,128,256]{2,1,0:T(8,128)(2,1)S(1)}, bf16[4,128,256]{2,1,0:T(8,128)(2,1)S(1)}, u32[]{:S(2)}, u32[]{:S(2)}) %collective-permute-start.2) | collective-permute-done | bytes 262176 | tf_op jit(solution)/shard_map/ppermute | solution.py:428
  48.6 1.9 %collective-permute-start.3 = (bf16[4,128,256]{2,1,0:T(8,128)(2,1)S(1)}, bf16[4,128,256]{2,1,0:T(8,128)(2,1)S(1)}, u32[]{:S(2)}, u32[]{:S(2)}) collective-permute-start(bf16[4,128,256]{2,1,0:T(8,128)(2,1)S(1)} %collective-permute-done.2.refs_3_), channel_id=1, source_target_pairs={{0,8},{8,16},{16,24},{24,32},{32,40},{40,48},{48,56},{56,64},{64,7... | collective-permute-start | bytes 786440 | tf_op jit(solution)/shard_map/ppermute | solution.py:428
  51.8 7.8 %collective-permute-done.3.refs_4_ = bf16[4,128,256]{2,1,0:T(8,128)(2,1)S(1)} collective-permute-done((bf16[4,128,256]{2,1,0:T(8,128)(2,1)S(1)}, bf16[4,128,256]{2,1,0:T(8,128)(2,1)S(1)}, u32[]{:S(2)}, u32[]{:S(2)}) %collective-permute-start.3) | collective-permute-done | bytes 262176 | tf_op jit(solution)/shard_map/ppermute | solution.py:428
  59.6 1.4 shard_map.96
  61.1 4.5 %all-to-all-start.1 = ((bf16[8,128,256]{2,1,0:T(8,128)(2,1)}), bf16[8,128,256]{2,1,0:T(8,128)(2,1)S(1)}, u32[]{:S(2)}, u32[]{:S(2)}) async-start(bf16[8,128,256]{2,1,0:T(8,128)(2,1)} %shard_map.96), calls=%async_computation.1 | async-start | bytes 1048576 | tf_op jit(solution)/shard_map/all_to_all | solution.py:436
  65.5 3.4 %shard_map.97 = (f32[8,128,512]{2,1,0:T(8,128)S(1)}, f32[8,8,512]{2,1,0:T(8,128)S(1)}) custom-call(bf16[512,2304]{1,0:T(8,128)(2,1)S(1)} %bitcast.6, bf16[512,2304]{1,0:T(8,128)(2,1)S(1)} %bitcast.7, bf16[512,2304]{1,0:T(8,128)(2,1)S(1)} %bitcast.8), custom_call_target="tpu_custom_call" | custom-call | flops 3000000000 | bytes 4194304 | tf_op jit(solution)/shard_map/pallas_call | solution.py:202
  70.3 5.6 %all-to-all-done.1 = bf16[8,128,256]{2,1,0:T(8,128)(2,1)S(1)} async-done(((bf16[8,128,256]{2,1,0:T(8,128)(2,1)}), bf16[8,128,256]{2,1,0:T(8,128)(2,1)S(1)}, u32[]{:S(2)}, u32[]{:S(2)}) %all-to-all-start.1) | async-done | bytes 524320 | tf_op jit(solution)/shard_map/all_to_all | solution.py:436
  75.9 1.6 %copy-done.12 = f32[8,128,512]{2,1,0:T(8,128)S(1)} copy-done((f32[8,128,512]{2,1,0:T(8,128)S(1)}, f32[8,128,512]{2,1,0:T(8,128)}, u32[]{:S(2)}) %copy-start.12) | copy-done | bytes 2097176
  77.5 9.2 %shard_map.98 = (bf16[8,128,512]{2,1,0:T(8,128)(2,1)S(1)}, f32[8,128,512]{2,1,0:T(8,128)S(1)}, f32[8,8,512]{2,1,0:T(8,128)S(1)}, bf16[2,512,256]{2,1,0:T(8,128)(2,1)}) custom-call(s32[4]{0:T(128)S(1)} %shard_map.94.info, bf16[512,2304]{1,0:T(8,128)(2,1)S(1)} %bitcast.9, bf16[512,2304]{1,0:T(8,128)(2,1)S(1)} %bitcast.10, bf16[2,512,256]{2,1,0:T(8,128)(2,1)S(1)} %bitcast.16, ...), custom_call_target="tpu_custom_call" | custom-call | flops 6000000000 | bytes 8388608 | tf_op jit(solution)/shard_map/pallas_call | solution.py:218
  89.0 3.5 %all-to-all-start.2 = ((bf16[8,128,256]{2,1,0:T(8,128)(2,1)}), bf16[8,128,256]{2,1,0:T(8,128)(2,1)S(1)}, u32[]{:S(2)}, u32[]{:S(2)}) async-start(bf16[8,128,256]{2,1,0:T(8,128)(2,1)} %bitcast.3), calls=%async_computation.2 | async-start | bytes 1048576 | tf_op jit(solution)/shard_map/all_to_all | solution.py:436
  92.5 1.6 %copy-done.14 = f32[8,128,512]{2,1,0:T(8,128)S(1)} copy-done((f32[8,128,512]{2,1,0:T(8,128)S(1)}, f32[8,128,512]{2,1,0:T(8,128)}, u32[]{:S(2)}) %copy-start.14) | copy-done | bytes 2097176
  95.3 4.6 %shard_map.99 = bf16[512,2304]{1,0:T(8,128)(2,1)S(1)} custom-call(bf16[512,2304]{1,0:T(8,128)(2,1)S(1)} %bitcast.11, bf16[512,2304]{1,0:T(8,128)(2,1)S(1)} %bitcast.12, bf16[512,2304]{1,0:T(8,128)(2,1)S(1)} %bitcast.13, bf16[8,128,512]{2,1,0:T(8,128)(2,1)S(1)} %copy-done.16, f32[8,128,512]{2,1,0:T(8,128)S(1)} %copy-done.14, ...), custom_call_target="tpu_custom_call" | custom-call | flops 5000000000 | bytes 6291456 | tf_op jit(solution)/shard_map/pallas_call | solution.py:243
  99.9 1.4 copy-done
  101.3 1.4 all-to-all-done.2
  102.8 1.4 shard_map.101
  105.6 1.9 %collective-permute-start.4 = (bf16[4,128,256]{2,1,0:T(8,128)(2,1)}, bf16[4,128,256]{2,1,0:T(8,128)(2,1)}, u32[]{:S(2)}, u32[]{:S(2)}) collective-permute-start(bf16[4,128,256]{2,1,0:T(8,128)(2,1)} %get-tuple-element.38), channel_id=1, source_target_pairs={{8,0},{16,8},{24,16},{32,24},{40,32},{48,40},{56,48},{64,56},{72,6... | collective-permute-start | bytes 786440 | tf_op jit(solution)/shard_map/ppermute | solution.py:428
  107.5 3.8 %all-to-all-start.3 = ((bf16[4,128,2304]{2,1,0:T(8,128)(2,1)}), bf16[4,128,2304]{2,1,0:T(8,128)(2,1)S(1)}, u32[]{:S(2)}, u32[]{:S(2)}) async-start(bf16[4,128,2304]{2,1,0:T(8,128)(2,1)} %bitcast.14), calls=%async_computation.3 | async-start | bytes 4718592 | tf_op jit(solution)/shard_map/all_to_all | solution.py:432
  111.3 4.3 %collective-permute-done.4 = bf16[4,128,256]{2,1,0:T(8,128)(2,1)} collective-permute-done((bf16[4,128,256]{2,1,0:T(8,128)(2,1)}, bf16[4,128,256]{2,1,0:T(8,128)(2,1)}, u32[]{:S(2)}, u32[]{:S(2)}) %collective-permute-start.4) | collective-permute-done | bytes 262176 | tf_op jit(solution)/shard_map/ppermute | solution.py:428
  116.7 4.3 %collective-permute-start.5 = (bf16[4,128,256]{2,1,0:T(8,128)(2,1)S(1)}, bf16[4,128,256]{2,1,0:T(8,128)(2,1)S(1)}, u32[]{:S(2)}, u32[]{:S(2)}) collective-permute-start(bf16[4,128,256]{2,1,0:T(8,128)(2,1)S(1)} %add_convert_fusion.2), channel_id=1, source_target_pairs={{8,0},{16,8},{24,16},{32,24},{40,32},{48,40},{56,48},{64,56},{72,6... | collective-permute-start | bytes 786440 | tf_op jit(solution)/shard_map/ppermute | solution.py:428
  121.0 4.8 %collective-permute-done.5 = bf16[4,128,256]{2,1,0:T(8,128)(2,1)S(1)} collective-permute-done((bf16[4,128,256]{2,1,0:T(8,128)(2,1)S(1)}, bf16[4,128,256]{2,1,0:T(8,128)(2,1)S(1)}, u32[]{:S(2)}, u32[]{:S(2)}) %collective-permute-start.5) | collective-permute-done | bytes 262176 | tf_op jit(solution)/shard_map/ppermute | solution.py:428
  125.8 6.5 %collective-permute-start.6 = (bf16[4,128,256]{2,1,0:T(8,128)(2,1)S(1)}, bf16[4,128,256]{2,1,0:T(8,128)(2,1)S(1)}, u32[]{:S(2)}, u32[]{:S(2)}) collective-permute-start(bf16[4,128,256]{2,1,0:T(8,128)(2,1)S(1)} %add_convert_fusion.1), channel_id=1, source_target_pairs={{8,0},{16,8},{24,16},{32,24},{40,32},{48,40},{56,48},{64,56},{72,6... | collective-permute-start | bytes 786440 | tf_op jit(solution)/shard_map/ppermute | solution.py:428
  132.3 3.9 %collective-permute-done.6 = bf16[4,128,256]{2,1,0:T(8,128)(2,1)S(1)} collective-permute-done((bf16[4,128,256]{2,1,0:T(8,128)(2,1)S(1)}, bf16[4,128,256]{2,1,0:T(8,128)(2,1)S(1)}, u32[]{:S(2)}, u32[]{:S(2)}) %collective-permute-start.6) | collective-permute-done | bytes 262176 | tf_op jit(solution)/shard_map/ppermute | solution.py:428
  137.0 6.5 %collective-permute-start.7 = (bf16[4,128,256]{2,1,0:T(8,128)(2,1)}, bf16[4,128,256]{2,1,0:T(8,128)(2,1)S(1)}, u32[]{:S(2)}, u32[]{:S(2)}) collective-permute-start(bf16[4,128,256]{2,1,0:T(8,128)(2,1)} %add_convert_fusion), channel_id=1, source_target_pairs={{8,0},{16,8},{24,16},{32,24},{40,32},{48,40},{56,48},{64,56},{72,6... | collective-permute-start | bytes 786440 | tf_op jit(solution)/shard_map/ppermute | solution.py:428
  143.5 1.9 %shard_map.100 = (bf16[128,4096]{1,0:T(8,128)(2,1)}, bf16[128,4096]{1,0:T(8,128)(2,1)}, bf16[4,128,256]{2,1,0:T(8,128)(2,1)S(1)}) custom-call(bf16[4,128,2304]{2,1,0:T(8,128)(2,1)S(1)} %all-to-all-done.3.all_ref), custom_call_target="tpu_custom_call" | custom-call | tf_op jit(solution)/shard_map/pallas_call | solution.py:364
  145.3 2.3 %collective-permute-done.7.came_ref = bf16[4,128,256]{2,1,0:T(8,128)(2,1)S(1)} collective-permute-done((bf16[4,128,256]{2,1,0:T(8,128)(2,1)}, bf16[4,128,256]{2,1,0:T(8,128)(2,1)S(1)}, u32[]{:S(2)}, u32[]{:S(2)}) %collective-permute-start.7) | collective-permute-done | bytes 262176 | tf_op jit(solution)/shard_map/ppermute | solution.py:428
  (39 shorter events, 14.5 us)
Async XLA Ops:
  0.6 0.9 copy-start.7
  1.5 0.9 copy-start.8
  2.5 18.0 %collective-permute-start = (bf16[4,128,256]{2,1,0:T(8,128)(2,1)S(1)}, bf16[4,128,256]{2,1,0:T(8,128)(2,1)S(1)}, u32[]{:S(2)}, u32[]{:S(2)}) collective-permute-start(bf16[4,128,256]{2,1,0:T(8,128)(2,1)S(1)} %shard_map.93.kv_ref.refs_0_), channel_id=1, source_target_pairs={{0,8},{8,16},{16,24},{24,32},{32,40},{40,48},{48,56},{56,64},{64,7... | collective-permute-start | bytes 786440 | tf_op jit(solution)/shard_map/ppermute | solution.py:428
  6.3 1.2 copy-start.1
  7.6 1.2 copy-start.2
  10.8 39.8 %copy-start.9 = (s32[128,2]{0,1:T(2,128)S(1)}, s32[128,2]{0,1:T(2,128)}, u32[]{:S(2)}) copy-start(s32[128,2]{0,1:T(2,128)} %param.10) | copy-start | bytes 3076
  10.8 39.8 %copy-start.10 = (s32[128]{0:T(128)S(1)}, s32[128]{0:T(128)}, u32[]{:S(2)}) copy-start(s32[128]{0:T(128)} %count_ref.1) | copy-start | bytes 1540
  20.5 40.6 %all-to-all-start = ((bf16[4,128,2304]{2,1,0:T(8,128)(2,1)}), bf16[4,128,2304]{2,1,0:T(8,128)(2,1)S(1)}, u32[]{:S(2)}, u32[]{:S(2)}) async-start(bf16[4,128,2304]{2,1,0:T(8,128)(2,1)} %shard_map.95), calls=%async_computation | async-start | bytes 4718592 | tf_op jit(solution)/shard_map/all_to_all | solution.py:432
  24.1 12.7 %collective-permute-start.1 = (bf16[4,128,256]{2,1,0:T(8,128)(2,1)S(1)}, bf16[4,128,256]{2,1,0:T(8,128)(2,1)S(1)}, u32[]{:S(2)}, u32[]{:S(2)}) collective-permute-start(bf16[4,128,256]{2,1,0:T(8,128)(2,1)S(1)} %collective-permute-done.refs_1_), channel_id=1, source_target_pairs={{0,8},{8,16},{16,24},{24,32},{32,40},{40,48},{48,56},{56,64},{64,7... | collective-permute-start | bytes 786440 | tf_op jit(solution)/shard_map/ppermute | solution.py:428
  36.8 11.9 %collective-permute-start.2 = (bf16[4,128,256]{2,1,0:T(8,128)(2,1)S(1)}, bf16[4,128,256]{2,1,0:T(8,128)(2,1)S(1)}, u32[]{:S(2)}, u32[]{:S(2)}) collective-permute-start(bf16[4,128,256]{2,1,0:T(8,128)(2,1)S(1)} %collective-permute-done.1.refs_2_), channel_id=1, source_target_pairs={{0,8},{8,16},{16,24},{24,32},{32,40},{40,48},{48,56},{56,64},{64,7... | collective-permute-start | bytes 786440 | tf_op jit(solution)/shard_map/ppermute | solution.py:428
  48.6 11.0 %collective-permute-start.3 = (bf16[4,128,256]{2,1,0:T(8,128)(2,1)S(1)}, bf16[4,128,256]{2,1,0:T(8,128)(2,1)S(1)}, u32[]{:S(2)}, u32[]{:S(2)}) collective-permute-start(bf16[4,128,256]{2,1,0:T(8,128)(2,1)S(1)} %collective-permute-done.2.refs_3_), channel_id=1, source_target_pairs={{0,8},{8,16},{16,24},{24,32},{32,40},{40,48},{48,56},{56,64},{64,7... | collective-permute-start | bytes 786440 | tf_op jit(solution)/shard_map/ppermute | solution.py:428
  61.1 14.8 %all-to-all-start.1 = ((bf16[8,128,256]{2,1,0:T(8,128)(2,1)}), bf16[8,128,256]{2,1,0:T(8,128)(2,1)S(1)}, u32[]{:S(2)}, u32[]{:S(2)}) async-start(bf16[8,128,256]{2,1,0:T(8,128)(2,1)} %shard_map.96), calls=%async_computation.1 | async-start | bytes 1048576 | tf_op jit(solution)/shard_map/all_to_all | solution.py:436
  68.9 1.4 copy-start.11
  75.9 1.6 %copy-start.12 = (f32[8,128,512]{2,1,0:T(8,128)S(1)}, f32[8,128,512]{2,1,0:T(8,128)}, u32[]{:S(2)}) copy-start(f32[8,128,512]{2,1,0:T(8,128)} %copy-done.11) | copy-start | bytes 6291460
  86.7 1.4 copy-start.13
  88.0 1.0 copy-start.15
  89.0 13.8 %all-to-all-start.2 = ((bf16[8,128,256]{2,1,0:T(8,128)(2,1)}), bf16[8,128,256]{2,1,0:T(8,128)(2,1)S(1)}, u32[]{:S(2)}, u32[]{:S(2)}) async-start(bf16[8,128,256]{2,1,0:T(8,128)(2,1)} %bitcast.3), calls=%async_computation.2 | async-start | bytes 1048576 | tf_op jit(solution)/shard_map/all_to_all | solution.py:436
  92.5 1.6 %copy-start.14 = (f32[8,128,512]{2,1,0:T(8,128)S(1)}, f32[8,128,512]{2,1,0:T(8,128)}, u32[]{:S(2)}) copy-start(f32[8,128,512]{2,1,0:T(8,128)} %copy-done.13) | copy-start | bytes 6291460
  94.1 1.2 copy-start.16
  99.9 1.4 copy-start
  104.2 0.7 copy-start.3
  104.9 0.7 copy-start.5
  105.6 10.0 %collective-permute-start.4 = (bf16[4,128,256]{2,1,0:T(8,128)(2,1)}, bf16[4,128,256]{2,1,0:T(8,128)(2,1)}, u32[]{:S(2)}, u32[]{:S(2)}) collective-permute-start(bf16[4,128,256]{2,1,0:T(8,128)(2,1)} %get-tuple-element.38), channel_id=1, source_target_pairs={{8,0},{16,8},{24,16},{32,24},{40,32},{48,40},{56,48},{64,56},{72,6... | collective-permute-start | bytes 786440 | tf_op jit(solution)/shard_map/ppermute | solution.py:428
  107.5 8.1 %copy-start.6 = (bf16[4,128,256]{2,1,0:T(8,128)(2,1)S(1)}, bf16[4,128,256]{2,1,0:T(8,128)(2,1)}, u32[]{:S(2)}) copy-start(bf16[4,128,256]{2,1,0:T(8,128)(2,1)} %copy-done.5) | copy-start | bytes 786436
  107.5 18.2 %copy-start.4 = (bf16[4,128,256]{2,1,0:T(8,128)(2,1)S(1)}, bf16[4,128,256]{2,1,0:T(8,128)(2,1)}, u32[]{:S(2)}) copy-start(bf16[4,128,256]{2,1,0:T(8,128)(2,1)} %copy-done.3) | copy-start | bytes 786436
  107.5 35.9 %all-to-all-start.3 = ((bf16[4,128,2304]{2,1,0:T(8,128)(2,1)}), bf16[4,128,2304]{2,1,0:T(8,128)(2,1)S(1)}, u32[]{:S(2)}, u32[]{:S(2)}) async-start(bf16[4,128,2304]{2,1,0:T(8,128)(2,1)} %bitcast.14), calls=%async_computation.3 | async-start | bytes 4718592 | tf_op jit(solution)/shard_map/all_to_all | solution.py:432
  116.7 9.1 %collective-permute-start.5 = (bf16[4,128,256]{2,1,0:T(8,128)(2,1)S(1)}, bf16[4,128,256]{2,1,0:T(8,128)(2,1)S(1)}, u32[]{:S(2)}, u32[]{:S(2)}) collective-permute-start(bf16[4,128,256]{2,1,0:T(8,128)(2,1)S(1)} %add_convert_fusion.2), channel_id=1, source_target_pairs={{8,0},{16,8},{24,16},{32,24},{40,32},{48,40},{56,48},{64,56},{72,6... | collective-permute-start | bytes 786440 | tf_op jit(solution)/shard_map/ppermute | solution.py:428
  125.8 10.4 %collective-permute-start.6 = (bf16[4,128,256]{2,1,0:T(8,128)(2,1)S(1)}, bf16[4,128,256]{2,1,0:T(8,128)(2,1)S(1)}, u32[]{:S(2)}, u32[]{:S(2)}) collective-permute-start(bf16[4,128,256]{2,1,0:T(8,128)(2,1)S(1)} %add_convert_fusion.1), channel_id=1, source_target_pairs={{8,0},{16,8},{24,16},{32,24},{40,32},{48,40},{56,48},{64,56},{72,6... | collective-permute-start | bytes 786440 | tf_op jit(solution)/shard_map/ppermute | solution.py:428
  137.0 10.7 %collective-permute-start.7 = (bf16[4,128,256]{2,1,0:T(8,128)(2,1)}, bf16[4,128,256]{2,1,0:T(8,128)(2,1)S(1)}, u32[]{:S(2)}, u32[]{:S(2)}) collective-permute-start(bf16[4,128,256]{2,1,0:T(8,128)(2,1)} %add_convert_fusion), channel_id=1, source_target_pairs={{8,0},{16,8},{24,16},{32,24},{40,32},{48,40},{56,48},{64,56},{72,6... | collective-permute-start | bytes 786440 | tf_op jit(solution)/shard_map/ppermute | solution.py:428

commit v3 on v2

--- a/solution.py
+++ b/solution.py
@@ -1,3 +1,4 @@
+import functools
 import math
 
 import jax
@@ -69,13 +70,14 @@
     ]
     for (h, part), t, p, d in zip(units(), tops, probs, dprobs):
         rows = rows_of(part)
-        out_ref[h, :, rows] = dot(values_t[:, : (part + 1) * HALF], p.astype(jnp.bfloat16), NN)
+        out = dot(values_t[:, : (part + 1) * HALF], p.astype(jnp.bfloat16), NN)
+        out_ref[h, :, rows] = out.astype(jnp.bfloat16)
         stat_ref[h, 0:1, rows] = t
         stat_ref[h, 1:2, rows] = jnp.sum(p, 0, keepdims=True)
         stat_ref[h, 2:3, rows] = jnp.sum(p * d, 0, keepdims=True)
 
 
-def far_kernel(info, q_ref, g_ref, far_ref, out_ref, stat_ref, att_ref, part_ref, line_ref, back_ref,
+def far_kernel(info, q_ref, g_ref, far_ref, out_ref, stat_ref, both_ref, line_ref, back_ref,
                keys_t, values_t, dkeys, dvalues):
     step = pl.program_id(0)
     linked = info[1] > 0
@@ -114,8 +116,9 @@
         line_ref[h, 1:2, rows] = delta
         low = p.astype(jnp.bfloat16)
         ds = (p * (d - delta)).astype(jnp.bfloat16)
-        att_ref[h, :, rows] = (dot(values_t[...], low, NN) + fade * out_ref[h, :, rows]).astype(jnp.bfloat16)
-        part_ref[h, :, rows] = dot(keys_t[...], ds, NN)
+        out = dot(values_t[...], low, NN) + fade * out_ref[h, :, rows].astype(jnp.float32)
+        both_ref[h, :HD, rows] = out.astype(jnp.bfloat16)
+        both_ref[h, HD:, rows] = dot(keys_t[...], ds, NN).astype(jnp.bfloat16)
         dvalues[...] += dot(low, g, NN)
         dkeys[...] += dot(ds, q, NN)
 
@@ -127,7 +130,7 @@
         back_ref[lane, :, HD:] = dvalues[...].astype(jnp.bfloat16)
 
 
-def rest_kernel(q_ref, g_ref, own_ref, out_ref, part_ref, line_ref, all_ref, keys_t, dkeys, dvalues):
+def rest_kernel(q_ref, g_ref, own_ref, both_ref, line_ref, all_ref, keys_t, dkeys, dvalues):
     step = pl.program_id(0)
     width = HPS * HD
     half = (all_ref.shape[1] - 2 * HD) // 2
@@ -152,8 +155,8 @@
     for (h, part), ds in zip(units(), dscores):
         rows = rows_of(part)
         at = pl.multiple_of(step * width + h * HD, HD)
-        all_ref[rows, pl.ds(at, HD)] = turned(out_ref[h, :, rows])
-        dq = dot(keys_t[:, : (part + 1) * HALF], ds, NN) + part_ref[h, :, rows]
+        all_ref[rows, pl.ds(at, HD)] = turned(both_ref[h, :HD, rows])
+        dq = dot(keys_t[:, : (part + 1) * HALF], ds, NN) + both_ref[h, HD:, rows].astype(jnp.float32)
         all_ref[rows, pl.ds(half + at, HD)] = (dq * SCALE).T.astype(jnp.bfloat16)
     for (h, part), p, ds in zip(units(), lows, dscores):
         depth = (part + 1) * HALF
@@ -205,7 +208,7 @@
         in_specs=[column(), column(heads), tail_of(heads)],
         out_specs=[stack(HD), stack(8)],
         scratch_shapes=[pltpu.VMEM((HD, ROWS), jnp.bfloat16)],
-        out_shape=[sds((heads, HD, ROWS)), sds((heads, 8, ROWS))],
+        out_shape=[sds((heads, HD, ROWS), jnp.bfloat16), sds((heads, 8, ROWS))],
         compiler_params=params(24),
         cost_estimate=pl.CostEstimate(flops=3 * 10**9, bytes_accessed=4 * 2**20, transcendentals=2**21),
     )(x, x, x)
@@ -225,11 +228,11 @@
                 pl.BlockSpec((None, ROWS, 2 * HD), lambda h, info: (info[0], 0, 0)),
                 stack(HD), stack(8),
             ],
-            out_specs=[stack(HD), stack(HD), stack(8), whole((2, ROWS, 2 * HD))],
+            out_specs=[stack(2 * HD), stack(8), whole((2, ROWS, 2 * HD))],
             scratch_shapes=[turn, turn, acc, acc],
         ),
         out_shape=[
-            sds((heads, HD, ROWS), jnp.bfloat16), sds((heads, HD, ROWS)), sds((heads, 8, ROWS)),
+            sds((heads, 2 * HD, ROWS), jnp.bfloat16), sds((heads, 8, ROWS)),
             sds((2, ROWS, 2 * HD), jnp.bfloat16),
         ],
         compiler_params=params(24),
@@ -237,19 +240,19 @@
     )(info, x, x, far, out, stats)
 
 
-def rest_pass(x, out, part, lines):
+def rest_pass(x, both, lines):
     heads = heads_of(x)
     acc = pltpu.VMEM((ROWS, HD), jnp.float32)
     return pl.pallas_call(
         rest_kernel,
         grid=(heads // HPS,),
-        in_specs=[column(), column(heads), tail_of(heads), stack(HD), stack(HD), stack(8)],
+        in_specs=[column(), column(heads), tail_of(heads), stack(2 * HD), stack(8)],
         out_specs=whole(x.shape),
         scratch_shapes=[pltpu.VMEM((HD, ROWS), jnp.bfloat16), acc, acc],
         out_shape=sds(x.shape, jnp.bfloat16),
         compiler_params=params(24),
         cost_estimate=pl.CostEstimate(flops=5 * 10**9, bytes_accessed=6 * 2**20, transcendentals=2**21),
-    )(x, x, x, out, part, lines)
+    )(x, x, x, both, lines)
 
 
 def gate_kernel(list_ref, count_ref, info_ref):
@@ -306,6 +309,7 @@
         out_specs=vmem,
         out_shape=sds((2 * heads, rows, width), jnp.bfloat16),
         compiler_params=pltpu.CompilerParams(vmem_limit_bytes=8 * MIB),
+        cost_estimate=pl.CostEstimate(flops=10 * 10**9, bytes_accessed=40 * MIB, transcendentals=0),
     )(info, *pieces)
 
 
@@ -371,56 +375,60 @@
     )(grads)
 
 
-def due_kernel(info, came_ref, *outs):
-    zero = jnp.zeros(outs[0].shape, outs[0].dtype)
-    for k, out in enumerate(outs):
-        both = jnp.logical_and(info[2] == k, info[3] == k)
-
-        @pl.when(both)
-        def _():
-            out[...] = came_ref[0] + came_ref[1]
-
-        @pl.when(jnp.logical_not(both))
-        def _():
-            out[...] = zero
-
-            for i in range(2):
-
-                @pl.when(info[2 + i] == k)
-                def _():
-                    out[...] = came_ref[i]
-
-
-def due_pass(info, came):
+def add_kernel(info, came_ref, *refs, gap):
+    out = refs[-1]
+    hits = [info[2 + i] == gap for i in range(2)]
+    wide = jnp.float32
+
+    def total(*terms):
+        if len(refs) > 1:
+            terms = (refs[0][...], *terms)
+        if not terms:
+            return jnp.zeros(out.shape, out.dtype)
+        return sum(t.astype(wide) for t in terms).astype(out.dtype)
+
+    for first in range(2):
+        for second in range(2):
+            case = [h if on else jnp.logical_not(h) for h, on in zip(hits, (first, second))]
+
+            @pl.when(jnp.logical_and(*case))
+            def _():
+                out[...] = total(*[came_ref[i] for i, on in enumerate((first, second)) if on])
+
+
+def add_pass(info, gap, came, *moving):
     vmem = pl.BlockSpec(memory_space=pltpu.VMEM)
     return pl.pallas_call(
-        due_kernel,
-        in_specs=[pl.BlockSpec(memory_space=pltpu.SMEM), vmem],
-        out_specs=[vmem] * (STEPS + 1),
-        out_shape=[sds(came.shape[1:], jnp.bfloat16)] * (STEPS + 1),
+        functools.partial(add_kernel, gap=gap),
+        in_specs=[pl.BlockSpec(memory_space=pltpu.SMEM), vmem] + [vmem] * len(moving),
+        out_specs=vmem,
+        out_shape=sds(came.shape[1:], jnp.bfloat16),
         compiler_params=pltpu.CompilerParams(vmem_limit_bytes=8 * MIB),
-    )(info, came)
-
-
-def finish_kernel(came_ref, due_ref, mine_ref, key_ref, value_ref):
+        cost_estimate=pl.CostEstimate(flops=(10 if gap == 1 else 0) * 10**9, bytes_accessed=4 * MIB, transcendentals=0),
+    )(info, came, *moving)
+
+
+def finish_kernel(info, moved_ref, came_ref, mine_ref, key_ref, value_ref):
     wide = jnp.float32
-    for h in range(came_ref.shape[0]):
-        total = came_ref[h].astype(wide) + due_ref[h].astype(wide) + mine_ref[h].astype(wide)
+    for h in range(moved_ref.shape[0]):
+        total = moved_ref[h].astype(wide) + mine_ref[h].astype(wide)
+        for i in range(2):
+            total += jnp.where(info[2 + i] == 0, came_ref[i, h].astype(wide), 0.0)
         key_ref[:, cols_of(h)] = total[:, :HD].astype(jnp.bfloat16)
         value_ref[:, cols_of(h)] = total[:, HD:].astype(jnp.bfloat16)
 
 
-def finish_pass(came, due, mine):
-    heads, rows, _ = came.shape
+def finish_pass(info, moved, came, mine):
+    heads, rows, _ = moved.shape
     vmem = pl.BlockSpec(memory_space=pltpu.VMEM)
     out = sds((rows, heads * HD), jnp.bfloat16)
     return pl.pallas_call(
         finish_kernel,
-        in_specs=[vmem] * 3,
+        in_specs=[pl.BlockSpec(memory_space=pltpu.SMEM)] + [vmem] * 3,
         out_specs=[vmem] * 2,
         out_shape=[out, out],
         compiler_params=pltpu.CompilerParams(vmem_limit_bytes=8 * MIB),
-    )(came, due, mine)
+    )(info, moved, came, mine)
 
 
 def ring(array, by):
@@ -451,24 +459,21 @@
     for _ in range(STEPS):
         pieces.append(ring(pieces[-1], 1))
     x = join_pass(query_states, out_grad, kv)
-    x = to_heads(after(x, pieces[1])).reshape(4 * here, -1)
+    x = to_heads(x).reshape(4 * here, -1)
     near, stats = near_pass(x)
     far = across(after(pick_pass(info, pieces), x)).reshape(2, 4 * here, pair)
-    out, part, lines, back = far_pass(info, x, far, near, stats)
+    both, lines, back = far_pass(info, x, far, near, stats)
 
     came = across(back.reshape(8, here, pair)).reshape(2, 4, here, pair)
-    grads = rest_pass(x, out, part, lines)
+    grads = rest_pass(x, both, lines)
     came, grads = lax.optimization_barrier((came, grads))
     grads = to_heads(grads.reshape(4, here, -1))
-    due = due_pass(info, came)
-    moving = due[STEPS]
-    for k in range(STEPS - 1, -1, -1):
-        moving = ring(moving, -1)
-        if k:
-            moving = (moving.astype(jnp.float32) + due[k].astype(jnp.float32)).astype(jnp.bfloat16)
-
+    moving = add_pass(info, STEPS, came)
+    for k in range(STEPS - 1, 0, -1):
+        moving = add_pass(info, k, came, ring(moving, -1))
+    moving = ring(moving, -1)
     attention, query_grad, mine = split_pass(grads)
-    key_grad, value_grad = finish_pass(moving, due[0], mine)
+    key_grad, value_grad = finish_pass(info, moving, came, mine)
     return attention, query_grad, key_grad, value_grad
 
 

time: 150 us -> 139 us (0.927)
  waiting for transfers between devices: 60.5 us -> 54.8 us
  local copies, waits for them, and re-layouts: 15.1 us -> 10.8 us
  other arithmetic: 1.85 us -> 0 us
  Pallas kernels: 25.9 us -> 27.4 us
    ppermute x8, waiting for transfers between devices: 53.5 us -> 46.1 us  [ring(): lax.ppermute(array, 'col', [(i, i + by) for i in range(peers) if 0 <= i +...]
    unnamed x34 -> x22, local copies, waits for them, and re-layouts: 15.1 us -> 10.8 us
    convert_element_type x3 -> x0, other arithmetic: 1.85 us -> none  [body(): (moving.astype(jnp.float32) + due[k].astype(jnp.float32)).astype(jnp.bflo...]
    all_to_all x2, waiting for transfers between devices: 7.08 us -> 8.69 us  [across(): lax.all_to_all(array, ('yh', 'uly'), split_axis=0, concat_axis=0, tiled=T...]
    pallas_call x2 -> x5, Pallas kernels: 2.2 us -> 3.74 us  [the longest x4 2.35 us: add_pass(): pl.pallas_call(functools.partial(add_kernel, gap=gap), in_specs=[pl.Block...]
  transfers between devices with their start and end apart: 12 -> 12, of which waited for: 10 -> 10; matrix products, arithmetic and copies ran while one was open for 1% -> 0% of each run, Pallas kernels for 10% -> 12%
where the time goes in v3:
time: 139 us; the launch traced here: 138 us
  waiting for transfers between devices  54.8 us (39%)
  starting transfers between devices  44.1 us (32%)
  Pallas kernels  27.4 us (20%)
  local copies, waits for them, and re-layouts  10.8 us (8%)
    ppermute x8, waiting for transfers between devices, ring(): lax.ppermute(array, 'col', [(i, i + by) for i in range(peers) if 0 <= i +...  46.1 us
    ppermute x8, starting transfers between devices, ring(): lax.ppermute(array, 'col', [(i, i + by) for i in range(peers) if 0 <= i +...  28.7 us
    unnamed x22, local copies, waits for them, and re-layouts  10.8 us
    pallas_call x1, Pallas kernels, far_pass(): pl.pallas_call(far_kernel, grid_spec=pltpu.PrefetchScalarGridSpec(num_sca...  9.18 us
    all_to_all x2, waiting for transfers between devices, across(): lax.all_to_all(array, ('yh', 'uly'), split_axis=0, concat_axis=0, tiled=T...  8.69 us
    all_to_all x2, starting transfers between devices, across(): lax.all_to_all(array, ('yh', 'uly'), split_axis=0, concat_axis=0, tiled=T...  7.97 us
    all_to_all x2, starting transfers between devices, to_heads(): return lax.all_to_all(array, 'uly', split_axis=0, concat_axis=0, tiled=True)  7.4 us
    pallas_call x1, Pallas kernels, rest_pass(): pl.pallas_call(rest_kernel, grid=(heads // HPS,), in_specs=[column(), col...  4.58 us
  transfers between devices with their start and end apart: 12, of which 10 were waited for; matrix products, arithmetic and copies ran while one was open for 0% of the time, Pallas kernels for 12%

profile of v3, /device:TPU:6, one launch (start us, length us, event | category | flops | bytes accessed | tf_op | source)
XLA Modules:
  0.0 138.0 jit_solution(15877373826332123286)
XLA Ops:
  2.5 3.8 %collective-permute-start = (bf16[4,128,256]{2,1,0:T(8,128)(2,1)S(1)}, bf16[4,128,256]{2,1,0:T(8,128)(2,1)S(1)}, u32[]{:S(2)}, u32[]{:S(2)}) collective-permute-start(bf16[4,128,256]{2,1,0:T(8,128)(2,1)S(1)} %shard_map.93.kv_ref.refs_0_), channel_id=1, source_target_pairs={{0,8},{8,16},{16,24},{24,32},{32,40},{40,48},{48,56},{56,64},{64,7... | collective-permute-start | bytes 786440 | tf_op jit(solution)/shard_map/ppermute | solution.py:436
  8.8 2.0 %shard_map.95 = bf16[4,128,2304]{2,1,0:T(8,128)(2,1)} custom-call(bf16[128,4096]{1,0:T(8,128)(2,1)S(1)} %copy-done.1, bf16[128,4096]{1,0:T(8,128)(2,1)S(1)} %copy-done.2, bf16[4,128,256]{2,1,0:T(8,128)(2,1)S(1)} %shard_map.93.kv_ref.refs_0_), custom_call_target="tpu_custom_call" | custom-call | tf_op jit(solution)/shard_map/pallas_call | solution.py:345
  10.8 3.8 %all-to-all-start = ((bf16[4,128,2304]{2,1,0:T(8,128)(2,1)}), bf16[4,128,2304]{2,1,0:T(8,128)(2,1)S(1)}, u32[]{:S(2)}, u32[]{:S(2)}) async-start(bf16[4,128,2304]{2,1,0:T(8,128)(2,1)} %shard_map.95), calls=%async_computation | async-start | bytes 4718592 | tf_op jit(solution)/shard_map/all_to_all | solution.py:440
  14.6 5.9 %collective-permute-done.refs_1_ = bf16[4,128,256]{2,1,0:T(8,128)(2,1)S(1)} collective-permute-done((bf16[4,128,256]{2,1,0:T(8,128)(2,1)S(1)}, bf16[4,128,256]{2,1,0:T(8,128)(2,1)S(1)}, u32[]{:S(2)}, u32[]{:S(2)}) %collective-permute-start) | collective-permute-done | bytes 262176 | tf_op jit(solution)/shard_map/ppermute | solution.py:436
  20.5 1.9 %collective-permute-start.1 = (bf16[4,128,256]{2,1,0:T(8,128)(2,1)S(1)}, bf16[4,128,256]{2,1,0:T(8,128)(2,1)S(1)}, u32[]{:S(2)}, u32[]{:S(2)}) collective-permute-start(bf16[4,128,256]{2,1,0:T(8,128)(2,1)S(1)} %collective-permute-done.refs_1_), channel_id=1, source_target_pairs={{0,8},{8,16},{16,24},{24,32},{32,40},{40,48},{48,56},{56,64},{64,7... | collective-permute-start | bytes 786440 | tf_op jit(solution)/shard_map/ppermute | solution.py:436
  22.4 9.6 %collective-permute-done.1.refs_2_ = bf16[4,128,256]{2,1,0:T(8,128)(2,1)S(1)} collective-permute-done((bf16[4,128,256]{2,1,0:T(8,128)(2,1)S(1)}, bf16[4,128,256]{2,1,0:T(8,128)(2,1)S(1)}, u32[]{:S(2)}, u32[]{:S(2)}) %collective-permute-start.1) | collective-permute-done | bytes 262176 | tf_op jit(solution)/shard_map/ppermute | solution.py:436
  31.9 1.9 %collective-permute-start.2 = (bf16[4,128,256]{2,1,0:T(8,128)(2,1)S(1)}, bf16[4,128,256]{2,1,0:T(8,128)(2,1)S(1)}, u32[]{:S(2)}, u32[]{:S(2)}) collective-permute-start(bf16[4,128,256]{2,1,0:T(8,128)(2,1)S(1)} %collective-permute-done.1.refs_2_), channel_id=1, source_target_pairs={{0,8},{8,16},{16,24},{24,32},{32,40},{40,48},{48,56},{56,64},{64,7... | collective-permute-start | bytes 786440 | tf_op jit(solution)/shard_map/ppermute | solution.py:436
  33.9 8.6 %collective-permute-done.2.refs_3_ = bf16[4,128,256]{2,1,0:T(8,128)(2,1)S(1)} collective-permute-done((bf16[4,128,256]{2,1,0:T(8,128)(2,1)S(1)}, bf16[4,128,256]{2,1,0:T(8,128)(2,1)S(1)}, u32[]{:S(2)}, u32[]{:S(2)}) %collective-permute-start.2) | collective-permute-done | bytes 262176 | tf_op jit(solution)/shard_map/ppermute | solution.py:436
  42.5 1.9 %collective-permute-start.3 = (bf16[4,128,256]{2,1,0:T(8,128)(2,1)S(1)}, bf16[4,128,256]{2,1,0:T(8,128)(2,1)S(1)}, u32[]{:S(2)}, u32[]{:S(2)}) collective-permute-start(bf16[4,128,256]{2,1,0:T(8,128)(2,1)S(1)} %collective-permute-done.2.refs_3_), channel_id=1, source_target_pairs={{0,8},{8,16},{16,24},{24,32},{32,40},{40,48},{48,56},{56,64},{64,7... | collective-permute-start | bytes 786440 | tf_op jit(solution)/shard_map/ppermute | solution.py:436
  45.6 7.2 %collective-permute-done.3.refs_4_ = bf16[4,128,256]{2,1,0:T(8,128)(2,1)S(1)} collective-permute-done((bf16[4,128,256]{2,1,0:T(8,128)(2,1)S(1)}, bf16[4,128,256]{2,1,0:T(8,128)(2,1)S(1)}, u32[]{:S(2)}, u32[]{:S(2)}) %collective-permute-start.3) | collective-permute-done | bytes 262176 | tf_op jit(solution)/shard_map/ppermute | solution.py:436
  52.9 1.4 %shard_map.96 = bf16[8,128,256]{2,1,0:T(8,128)(2,1)} custom-call(s32[4]{0:T(128)S(1)} %shard_map.94.info, bf16[4,128,256]{2,1,0:T(8,128)(2,1)S(1)} %shard_map.93.kv_ref.refs_0_, bf16[4,128,256]{2,1,0:T(8,128)(2,1)S(1)} %collective-permute-done.refs_1_, bf16[4,128,256]{2,1,0:T(8,128)(2,1)S(1)} %collective-permute-done.1.refs_2_, ...), custom_call_target="tpu_custom_call" | custom-call | flops 10000000000 | bytes 41943040 | tf_op jit(solution)/shard_map/pallas_call | solution.py:306
  54.3 4.5 %all-to-all-start.1 = ((bf16[8,128,256]{2,1,0:T(8,128)(2,1)}), bf16[8,128,256]{2,1,0:T(8,128)(2,1)S(1)}, u32[]{:S(2)}, u32[]{:S(2)}) async-start(bf16[8,128,256]{2,1,0:T(8,128)(2,1)} %shard_map.96), calls=%async_computation.1 | async-start | bytes 1048576 | tf_op jit(solution)/shard_map/all_to_all | solution.py:444
  58.8 3.3 %shard_map.97 = (bf16[8,128,512]{2,1,0:T(8,128)(2,1)S(1)}, f32[8,8,512]{2,1,0:T(8,128)S(1)}) custom-call(bf16[512,2304]{1,0:T(8,128)(2,1)S(1)} %bitcast.11, bf16[512,2304]{1,0:T(8,128)(2,1)S(1)} %bitcast.12, bf16[512,2304]{1,0:T(8,128)(2,1)S(1)} %bitcast.13), custom_call_target="tpu_custom_call" | custom-call | flops 3000000000 | bytes 4194304 | tf_op jit(solution)/shard_map/pallas_call | solution.py:205
  63.1 6.0 %all-to-all-done.1 = bf16[8,128,256]{2,1,0:T(8,128)(2,1)S(1)} async-done(((bf16[8,128,256]{2,1,0:T(8,128)(2,1)}), bf16[8,128,256]{2,1,0:T(8,128)(2,1)S(1)}, u32[]{:S(2)}, u32[]{:S(2)}) %all-to-all-start.1) | async-done | bytes 524320 | tf_op jit(solution)/shard_map/all_to_all | solution.py:444
  70.4 9.2 %shard_map.98 = (bf16[8,256,512]{2,1,0:T(8,128)(2,1)S(1)}, f32[8,8,512]{2,1,0:T(8,128)S(1)}, bf16[2,512,256]{2,1,0:T(8,128)(2,1)}) custom-call(s32[4]{0:T(128)S(1)} %shard_map.94.info, bf16[512,2304]{1,0:T(8,128)(2,1)S(1)} %bitcast.14, bf16[512,2304]{1,0:T(8,128)(2,1)S(1)} %bitcast.15, bf16[2,512,256]{2,1,0:T(8,128)(2,1)S(1)} %bitcast.20, ...), custom_call_target="tpu_custom_call" | custom-call | flops 6000000000 | bytes 8388608 | tf_op jit(solution)/shard_map/pallas_call | solution.py:221
  79.5 1.4 copy-done.9
  80.9 3.5 %all-to-all-start.2 = ((bf16[8,128,256]{2,1,0:T(8,128)(2,1)}), bf16[8,128,256]{2,1,0:T(8,128)(2,1)S(1)}, u32[]{:S(2)}, u32[]{:S(2)}) async-start(bf16[8,128,256]{2,1,0:T(8,128)(2,1)} %bitcast.3), calls=%async_computation.2 | async-start | bytes 1048576 | tf_op jit(solution)/shard_map/all_to_all | solution.py:444
  84.4 1.6 %copy-done.10 = bf16[8,256,512]{2,1,0:T(8,128)(2,1)S(1)} copy-done((bf16[8,256,512]{2,1,0:T(8,128)(2,1)S(1)}, bf16[8,256,512]{2,1,0:T(8,128)(2,1)}, u32[]{:S(2)}) %copy-start.10) | copy-done | bytes 2097176
  86.0 4.6 %shard_map.99 = bf16[512,2304]{1,0:T(8,128)(2,1)S(1)} custom-call(bf16[512,2304]{1,0:T(8,128)(2,1)S(1)} %bitcast.16, bf16[512,2304]{1,0:T(8,128)(2,1)S(1)} %bitcast.17, bf16[512,2304]{1,0:T(8,128)(2,1)S(1)} %bitcast.18, bf16[8,256,512]{2,1,0:T(8,128)(2,1)S(1)} %copy-done.10, f32[8,8,512]{2,1,0:T(8,128)S(1)} %get-tuple-element.24.line_ref), custom_call_target="tpu_custom_call" | custom-call | flops 5000000000 | bytes 6291456 | tf_op jit(solution)/shard_map/pallas_call | solution.py:246
  90.6 1.4 %copy-done = bf16[512,2304]{1,0:T(8,128)(2,1)} copy-done((bf16[512,2304]{1,0:T(8,128)(2,1)}, bf16[512,2304]{1,0:T(8,128)(2,1)S(1)}, u32[]{:S(2)}) %copy-start) | copy-done | bytes 2359320
  92.0 2.7 %all-to-all-done.2 = bf16[8,128,256]{2,1,0:T(8,128)(2,1)S(1)} async-done(((bf16[8,128,256]{2,1,0:T(8,128)(2,1)}), bf16[8,128,256]{2,1,0:T(8,128)(2,1)S(1)}, u32[]{:S(2)}, u32[]{:S(2)}) %all-to-all-start.2) | async-done | bytes 524320 | tf_op jit(solution)/shard_map/all_to_all | solution.py:444
  95.2 1.9 %collective-permute-start.4 = (bf16[4,128,256]{2,1,0:T(8,128)(2,1)S(1)}, bf16[4,128,256]{2,1,0:T(8,128)(2,1)S(1)}, u32[]{:S(2)}, u32[]{:S(2)}) collective-permute-start(bf16[4,128,256]{2,1,0:T(8,128)(2,1)S(1)} %shard_map.101), channel_id=1, source_target_pairs={{8,0},{16,8},{24,16},{32,24},{40,32},{48,40},{56,48},{64,56},{72,6... | collective-permute-start | bytes 786440 | tf_op jit(solution)/shard_map/ppermute | solution.py:436
  97.2 3.6 %all-to-all-start.3 = ((bf16[4,128,2304]{2,1,0:T(8,128)(2,1)}), bf16[4,128,2304]{2,1,0:T(8,128)(2,1)S(1)}, u32[]{:S(2)}, u32[]{:S(2)}) async-start(bf16[4,128,2304]{2,1,0:T(8,128)(2,1)} %bitcast.19), calls=%async_computation.3 | async-start | bytes 4718592 | tf_op jit(solution)/shard_map/all_to_all | solution.py:440
  100.8 4.2 %collective-permute-done.4.refs_0_ = bf16[4,128,256]{2,1,0:T(8,128)(2,1)S(1)} collective-permute-done((bf16[4,128,256]{2,1,0:T(8,128)(2,1)S(1)}, bf16[4,128,256]{2,1,0:T(8,128)(2,1)S(1)}, u32[]{:S(2)}, u32[]{:S(2)}) %collective-permute-start.4) | collective-permute-done | bytes 262176 | tf_op jit(solution)/shard_map/ppermute | solution.py:436
  105.6 4.3 %collective-permute-start.5 = (bf16[4,128,256]{2,1,0:T(8,128)(2,1)S(1)}, bf16[4,128,256]{2,1,0:T(8,128)(2,1)S(1)}, u32[]{:S(2)}, u32[]{:S(2)}) collective-permute-start(bf16[4,128,256]{2,1,0:T(8,128)(2,1)S(1)} %shard_map.102), channel_id=1, source_target_pairs={{8,0},{16,8},{24,16},{32,24},{40,32},{48,40},{56,48},{64,56},{72,6... | collective-permute-start | bytes 786440 | tf_op jit(solution)/shard_map/ppermute | solution.py:436
  109.9 4.8 %collective-permute-done.5.refs_0_ = bf16[4,128,256]{2,1,0:T(8,128)(2,1)S(1)} collective-permute-done((bf16[4,128,256]{2,1,0:T(8,128)(2,1)S(1)}, bf16[4,128,256]{2,1,0:T(8,128)(2,1)S(1)}, u32[]{:S(2)}, u32[]{:S(2)}) %collective-permute-start.5) | collective-permute-done | bytes 262176 | tf_op jit(solution)/shard_map/ppermute | solution.py:436
  115.2 6.5 %collective-permute-start.6 = (bf16[4,128,256]{2,1,0:T(8,128)(2,1)S(1)}, bf16[4,128,256]{2,1,0:T(8,128)(2,1)S(1)}, u32[]{:S(2)}, u32[]{:S(2)}) collective-permute-start(bf16[4,128,256]{2,1,0:T(8,128)(2,1)S(1)} %shard_map.103), channel_id=1, source_target_pairs={{8,0},{16,8},{24,16},{32,24},{40,32},{48,40},{56,48},{64,56},{72,6... | collective-permute-start | bytes 786440 | tf_op jit(solution)/shard_map/ppermute | solution.py:436
  121.7 3.9 %collective-permute-done.6.refs_0_ = bf16[4,128,256]{2,1,0:T(8,128)(2,1)S(1)} collective-permute-done((bf16[4,128,256]{2,1,0:T(8,128)(2,1)S(1)}, bf16[4,128,256]{2,1,0:T(8,128)(2,1)S(1)}, u32[]{:S(2)}, u32[]{:S(2)}) %collective-permute-start.6) | collective-permute-done | bytes 262176 | tf_op jit(solution)/shard_map/ppermute | solution.py:436
  126.2 6.5 %collective-permute-start.7 = (bf16[4,128,256]{2,1,0:T(8,128)(2,1)S(1)}, bf16[4,128,256]{2,1,0:T(8,128)(2,1)S(1)}, u32[]{:S(2)}, u32[]{:S(2)}) collective-permute-start(bf16[4,128,256]{2,1,0:T(8,128)(2,1)S(1)} %shard_map.104), channel_id=1, source_target_pairs={{8,0},{16,8},{24,16},{32,24},{40,32},{48,40},{56,48},{64,56},{72,6... | collective-permute-start | bytes 786440 | tf_op jit(solution)/shard_map/ppermute | solution.py:436
  132.7 1.9 %shard_map.100 = (bf16[128,4096]{1,0:T(8,128)(2,1)}, bf16[128,4096]{1,0:T(8,128)(2,1)}, bf16[4,128,256]{2,1,0:T(8,128)(2,1)S(1)}) custom-call(bf16[4,128,2304]{2,1,0:T(8,128)(2,1)S(1)} %all-to-all-done.3.all_ref), custom_call_target="tpu_custom_call" | custom-call | tf_op jit(solution)/shard_map/pallas_call | solution.py:368
  134.6 2.0 %collective-permute-done.7.moved_ref = bf16[4,128,256]{2,1,0:T(8,128)(2,1)S(1)} collective-permute-done((bf16[4,128,256]{2,1,0:T(8,128)(2,1)S(1)}, bf16[4,128,256]{2,1,0:T(8,128)(2,1)S(1)}, u32[]{:S(2)}, u32[]{:S(2)}) %collective-permute-start.7) | collective-permute-done | bytes 262176 | tf_op jit(solution)/shard_map/ppermute | solution.py:436
  136.6 1.4 %shard_map.105 = (bf16[128,512]{1,0:T(8,128)(2,1)}, bf16[128,512]{1,0:T(8,128)(2,1)}) custom-call(s32[4]{0:T(128)S(1)} %shard_map.94.info, bf16[4,128,256]{2,1,0:T(8,128)(2,1)S(1)} %collective-permute-done.7.moved_ref, bf16[2,4,128,256]{3,2,1,0:T(8,128)(2,1)S(1)} %bitcast.10, bf16[4,128,256]{2,1,0:T(8,128)(2,1)S(1)} %get-tuple-element.29.mine_ref), custom_call_target="tpu_custom_call" | custom-call | tf_op jit(solution)/shard_map/pallas_call | solution.py:425
  (27 shorter events, 10.0 us)
Async XLA Ops:
  0.6 0.9 copy-start.3
  1.5 0.9 copy-start.4
  2.5 18.0 %collective-permute-start = (bf16[4,128,256]{2,1,0:T(8,128)(2,1)S(1)}, bf16[4,128,256]{2,1,0:T(8,128)(2,1)S(1)}, u32[]{:S(2)}, u32[]{:S(2)}) collective-permute-start(bf16[4,128,256]{2,1,0:T(8,128)(2,1)S(1)} %shard_map.93.kv_ref.refs_0_), channel_id=1, source_target_pairs={{0,8},{8,16},{16,24},{24,32},{32,40},{40,48},{48,56},{56,64},{64,7... | collective-permute-start | bytes 786440 | tf_op jit(solution)/shard_map/ppermute | solution.py:436
  6.3 1.2 copy-start.1
  7.6 1.2 copy-start.2
  10.8 33.6 %copy-start.5 = (s32[128,2]{0,1:T(2,128)S(1)}, s32[128,2]{0,1:T(2,128)}, u32[]{:S(2)}) copy-start(s32[128,2]{0,1:T(2,128)} %param.10) | copy-start | bytes 3076
  10.8 33.6 %copy-start.6 = (s32[128]{0:T(128)S(1)}, s32[128]{0:T(128)}, u32[]{:S(2)}) copy-start(s32[128]{0:T(128)} %count_ref.1) | copy-start | bytes 1540
  10.8 43.5 %all-to-all-start = ((bf16[4,128,2304]{2,1,0:T(8,128)(2,1)}), bf16[4,128,2304]{2,1,0:T(8,128)(2,1)S(1)}, u32[]{:S(2)}, u32[]{:S(2)}) async-start(bf16[4,128,2304]{2,1,0:T(8,128)(2,1)} %shard_map.95), calls=%async_computation | async-start | bytes 4718592 | tf_op jit(solution)/shard_map/all_to_all | solution.py:440
  20.5 11.5 %collective-permute-start.1 = (bf16[4,128,256]{2,1,0:T(8,128)(2,1)S(1)}, bf16[4,128,256]{2,1,0:T(8,128)(2,1)S(1)}, u32[]{:S(2)}, u32[]{:S(2)}) collective-permute-start(bf16[4,128,256]{2,1,0:T(8,128)(2,1)S(1)} %collective-permute-done.refs_1_), channel_id=1, source_target_pairs={{0,8},{8,16},{16,24},{24,32},{32,40},{40,48},{48,56},{56,64},{64,7... | collective-permute-start | bytes 786440 | tf_op jit(solution)/shard_map/ppermute | solution.py:436
  31.9 10.6 %collective-permute-start.2 = (bf16[4,128,256]{2,1,0:T(8,128)(2,1)S(1)}, bf16[4,128,256]{2,1,0:T(8,128)(2,1)S(1)}, u32[]{:S(2)}, u32[]{:S(2)}) collective-permute-start(bf16[4,128,256]{2,1,0:T(8,128)(2,1)S(1)} %collective-permute-done.1.refs_2_), channel_id=1, source_target_pairs={{0,8},{8,16},{16,24},{24,32},{32,40},{40,48},{48,56},{56,64},{64,7... | collective-permute-start | bytes 786440 | tf_op jit(solution)/shard_map/ppermute | solution.py:436
  42.5 10.4 %collective-permute-start.3 = (bf16[4,128,256]{2,1,0:T(8,128)(2,1)S(1)}, bf16[4,128,256]{2,1,0:T(8,128)(2,1)S(1)}, u32[]{:S(2)}, u32[]{:S(2)}) collective-permute-start(bf16[4,128,256]{2,1,0:T(8,128)(2,1)S(1)} %collective-permute-done.2.refs_3_), channel_id=1, source_target_pairs={{0,8},{8,16},{16,24},{24,32},{32,40},{40,48},{48,56},{56,64},{64,7... | collective-permute-start | bytes 786440 | tf_op jit(solution)/shard_map/ppermute | solution.py:436
  54.3 14.8 %all-to-all-start.1 = ((bf16[8,128,256]{2,1,0:T(8,128)(2,1)}), bf16[8,128,256]{2,1,0:T(8,128)(2,1)S(1)}, u32[]{:S(2)}, u32[]{:S(2)}) async-start(bf16[8,128,256]{2,1,0:T(8,128)(2,1)} %shard_map.96), calls=%async_computation.1 | async-start | bytes 1048576 | tf_op jit(solution)/shard_map/all_to_all | solution.py:444
  62.1 1.0 copy-start.7
  69.1 1.2 copy-start.8
  79.5 1.4 copy-start.9
  80.9 13.8 %all-to-all-start.2 = ((bf16[8,128,256]{2,1,0:T(8,128)(2,1)}), bf16[8,128,256]{2,1,0:T(8,128)(2,1)S(1)}, u32[]{:S(2)}, u32[]{:S(2)}) async-start(bf16[8,128,256]{2,1,0:T(8,128)(2,1)} %bitcast.3), calls=%async_computation.2 | async-start | bytes 1048576 | tf_op jit(solution)/shard_map/all_to_all | solution.py:444
  84.4 1.6 %copy-start.10 = (bf16[8,256,512]{2,1,0:T(8,128)(2,1)S(1)}, bf16[8,256,512]{2,1,0:T(8,128)(2,1)}, u32[]{:S(2)}) copy-start(bf16[8,256,512]{2,1,0:T(8,128)(2,1)} %copy-done.9) | copy-start | bytes 6291460
  90.6 1.4 %copy-start = (bf16[512,2304]{1,0:T(8,128)(2,1)}, bf16[512,2304]{1,0:T(8,128)(2,1)S(1)}, u32[]{:S(2)}) copy-start(bf16[512,2304]{1,0:T(8,128)(2,1)S(1)} %shard_map.99) | copy-start | bytes 7077892
  95.2 9.7 %collective-permute-start.4 = (bf16[4,128,256]{2,1,0:T(8,128)(2,1)S(1)}, bf16[4,128,256]{2,1,0:T(8,128)(2,1)S(1)}, u32[]{:S(2)}, u32[]{:S(2)}) collective-permute-start(bf16[4,128,256]{2,1,0:T(8,128)(2,1)S(1)} %shard_map.101), channel_id=1, source_target_pairs={{8,0},{16,8},{24,16},{32,24},{40,32},{48,40},{56,48},{64,56},{72,6... | collective-permute-start | bytes 786440 | tf_op jit(solution)/shard_map/ppermute | solution.py:436
  97.2 35.5 %all-to-all-start.3 = ((bf16[4,128,2304]{2,1,0:T(8,128)(2,1)}), bf16[4,128,2304]{2,1,0:T(8,128)(2,1)S(1)}, u32[]{:S(2)}, u32[]{:S(2)}) async-start(bf16[4,128,2304]{2,1,0:T(8,128)(2,1)} %bitcast.19), calls=%async_computation.3 | async-start | bytes 4718592 | tf_op jit(solution)/shard_map/all_to_all | solution.py:440
  105.6 9.0 %collective-permute-start.5 = (bf16[4,128,256]{2,1,0:T(8,128)(2,1)S(1)}, bf16[4,128,256]{2,1,0:T(8,128)(2,1)S(1)}, u32[]{:S(2)}, u32[]{:S(2)}) collective-permute-start(bf16[4,128,256]{2,1,0:T(8,128)(2,1)S(1)} %shard_map.102), channel_id=1, source_target_pairs={{8,0},{16,8},{24,16},{32,24},{40,32},{48,40},{56,48},{64,56},{72,6... | collective-permute-start | bytes 786440 | tf_op jit(solution)/shard_map/ppermute | solution.py:436
  115.2 10.4 %collective-permute-start.6 = (bf16[4,128,256]{2,1,0:T(8,128)(2,1)S(1)}, bf16[4,128,256]{2,1,0:T(8,128)(2,1)S(1)}, u32[]{:S(2)}, u32[]{:S(2)}) collective-permute-start(bf16[4,128,256]{2,1,0:T(8,128)(2,1)S(1)} %shard_map.103), channel_id=1, source_target_pairs={{8,0},{16,8},{24,16},{32,24},{40,32},{48,40},{56,48},{64,56},{72,6... | collective-permute-start | bytes 786440 | tf_op jit(solution)/shard_map/ppermute | solution.py:436
  126.2 10.4 %collective-permute-start.7 = (bf16[4,128,256]{2,1,0:T(8,128)(2,1)S(1)}, bf16[4,128,256]{2,1,0:T(8,128)(2,1)S(1)}, u32[]{:S(2)}, u32[]{:S(2)}) collective-permute-start(bf16[4,128,256]{2,1,0:T(8,128)(2,1)S(1)} %shard_map.104), channel_id=1, source_target_pairs={{8,0},{16,8},{24,16},{32,24},{40,32},{48,40},{56,48},{64,56},{72,6... | collective-permute-start | bytes 786440 | tf_op jit(solution)/shard_map/ppermute | solution.py:436

commit v4 on v3

--- a/solution.py
+++ b/solution.py
@@ -174,6 +174,10 @@
     return jax.ShapeDtypeStruct(shape, dtype)
 
 
+def in_hbm(array):
+    return pltpu.with_memory_space_constraint(array, pltpu.HBM)
+
+
 def params(mib):
     return pltpu.CompilerParams(
         dimension_semantics=("arbitrary",), vmem_limit_bytes=mib * MIB
@@ -208,7 +212,7 @@
         in_specs=[column(), column(heads), tail_of(heads)],
         out_specs=[stack(HD), stack(8)],
         scratch_shapes=[pltpu.VMEM((HD, ROWS), jnp.bfloat16)],
-        out_shape=[sds((heads, HD, ROWS), jnp.bfloat16), sds((heads, 8, ROWS))],
+        out_shape=[pltpu.HBM((heads, HD, ROWS), jnp.bfloat16), sds((heads, 8, ROWS))],
         compiler_params=params(24),
         cost_estimate=pl.CostEstimate(flops=3 * 10**9, bytes_accessed=4 * 2**20, transcendentals=2**21),
     )(x, x, x)
@@ -232,12 +236,12 @@
             scratch_shapes=[turn, turn, acc, acc],
         ),
         out_shape=[
-            sds((heads, 2 * HD, ROWS), jnp.bfloat16), sds((heads, 8, ROWS)),
+            pltpu.HBM((heads, 2 * HD, ROWS), jnp.bfloat16), sds((heads, 8, ROWS)),
             sds((2, ROWS, 2 * HD), jnp.bfloat16),
         ],
         compiler_params=params(24),
         cost_estimate=pl.CostEstimate(flops=6 * 10**9, bytes_accessed=8 * 2**20, transcendentals=2**21),
-    )(info, x, x, far, out, stats)
+    )(info, x, x, far, in_hbm(out), stats)
 
 
 def rest_pass(x, both, lines):
@@ -249,10 +253,10 @@
         in_specs=[column(), column(heads), tail_of(heads), stack(2 * HD), stack(8)],
         out_specs=whole(x.shape),
         scratch_shapes=[pltpu.VMEM((HD, ROWS), jnp.bfloat16), acc, acc],
-        out_shape=sds(x.shape, jnp.bfloat16),
+        out_shape=pltpu.HBM(x.shape, jnp.bfloat16),
         compiler_params=params(24),
         cost_estimate=pl.CostEstimate(flops=5 * 10**9, bytes_accessed=6 * 2**20, transcendentals=2**21),
-    )(x, x, x, both, lines)
+    )(x, x, x, in_hbm(both), lines)
 
 
 def gate_kernel(list_ref, count_ref, info_ref):
@@ -349,30 +353,39 @@
         out_specs=pl.BlockSpec((None, rows, 2 * width + pair), lambda h: (h, 0, 0)),
         out_shape=sds((heads, rows, 2 * width + pair), jnp.bfloat16),
         compiler_params=params(8),
-    )(q, g, kv)
-
-
-def split_kernel(all_ref, att_ref, dq_ref, mine_ref):
+    )(in_hbm(q), in_hbm(g), kv)
+
+
+def split_kernel(info, all_ref, came_ref, att_ref, dq_ref, base_ref):
     width = att_ref.shape[1]
     att_ref[...] = all_ref[:, :width]
     dq_ref[...] = all_ref[:, width : 2 * width]
-    mine_ref[...] = all_ref[:, 2 * width :]
-
-
-def split_pass(grads):
+    total = all_ref[:, 2 * width :].astype(jnp.float32)
+    for i in range(2):
+        total += jnp.where(info[2 + i] == 0, came_ref[i].astype(jnp.float32), 0.0)
+    base_ref[...] = total
+
+
+def split_pass(info, grads, came):
     heads, rows, total = grads.shape
     pair = 2 * HD
     width = (total - pair) // 2
-    block = pl.BlockSpec((rows, width), lambda h: (0, h))
+    block = pl.BlockSpec((rows, width), lambda h, info: (0, h))
     wide = sds((rows, heads * width), jnp.bfloat16)
     return pl.pallas_call(
         split_kernel,
-        grid=(heads,),
-        in_specs=[pl.BlockSpec((None, rows, total), lambda h: (h, 0, 0))],
-        out_specs=[block, block, pl.BlockSpec((None, rows, pair), lambda h: (h, 0, 0))],
-        out_shape=[wide, wide, sds((heads, rows, pair), jnp.bfloat16)],
+        grid_spec=pltpu.PrefetchScalarGridSpec(
+            num_scalar_prefetch=1,
+            grid=(heads,),
+            in_specs=[
+                pl.BlockSpec((None, rows, total), lambda h, info: (h, 0, 0)),
+                pl.BlockSpec((2, None, rows, pair), lambda h, info: (0, h, 0, 0)),
+            ],
+            out_specs=[block, block, pl.BlockSpec((None, rows, pair), lambda h, info: (h, 0, 0))],
+        ),
+        out_shape=[wide, wide, sds((heads, rows, pair))],
         compiler_params=params(8),
-    )(grads)
+    )(info, grads, came)
 
 
 def add_kernel(info, came_ref, *refs, gap):
@@ -408,27 +421,24 @@
     )(info, came, *moving)
 
 
-def finish_kernel(info, moved_ref, came_ref, mine_ref, key_ref, value_ref):
-    wide = jnp.float32
+def finish_kernel(moved_ref, base_ref, key_ref, value_ref):
     for h in range(moved_ref.shape[0]):
-        total = moved_ref[h].astype(wide) + mine_ref[h].astype(wide)
-        for i in range(2):
-            total += jnp.where(info[2 + i] == 0, came_ref[i, h].astype(wide), 0.0)
+        total = moved_ref[h].astype(jnp.float32) + base_ref[h]
         key_ref[:, cols_of(h)] = total[:, :HD].astype(jnp.bfloat16)
         value_ref[:, cols_of(h)] = total[:, HD:].astype(jnp.bfloat16)
 
 
-def finish_pass(info, moved, came, mine):
+def finish_pass(moved, base):
     heads, rows, _ = moved.shape
     vmem = pl.BlockSpec(memory_space=pltpu.VMEM)
     out = sds((rows, heads * HD), jnp.bfloat16)
     return pl.pallas_call(
         finish_kernel,
-        in_specs=[pl.BlockSpec(memory_space=pltpu.SMEM)] + [vmem] * 3,
+        in_specs=[vmem] * 2,
         out_specs=[vmem] * 2,
         out_shape=[out, out],
         compiler_params=pltpu.CompilerParams(vmem_limit_bytes=8 * MIB),
-    )(info, moved, came, mine)
+    )(moved, base)
 
 
 def ring(array, by):
@@ -472,8 +482,8 @@
     for k in range(STEPS - 1, 0, -1):
         moving = add_pass(info, k, came, ring(moving, -1))
     moving = ring(moving, -1)
-    attention, query_grad, mine = split_pass(grads)
-    key_grad, value_grad = finish_pass(info, moving, came, mine)
+    attention, query_grad, base = split_pass(info, grads, came)
+    key_grad, value_grad = finish_pass(moving, base)
     return attention, query_grad, key_grad, value_grad
 
 

time: 139 us -> 137 us (0.986)
  local copies, waits for them, and re-layouts: 10.8 us -> 1.81 us
  Pallas kernels: 27.4 us -> 33.9 us
    unnamed x22 -> x8, local copies, waits for them, and re-layouts: 10.8 us -> 1.81 us
    pallas_call x1, Pallas kernels: 4.58 us -> 7.14 us  [rest_pass(): pl.pallas_call(rest_kernel, grid=(heads // HPS,), in_specs=[column(), col...]
    pallas_call x1, Pallas kernels: 2.04 us -> 3.84 us  [join_pass(): pl.pallas_call(join_kernel, grid=(heads,), in_specs=[block, block, pl.Blo...]
    pallas_call x1, Pallas kernels: 9.18 us -> 10.6 us  [far_pass(): pl.pallas_call(far_kernel, grid_spec=pltpu.PrefetchScalarGridSpec(num_sca...]
  transfers between devices with their start and end apart: 12 -> 12, of which waited for: 10 -> 10; matrix products, arithmetic and copies ran while one was open for 0% -> 0% of each run, Pallas kernels for 12% -> 16%
where the time goes in v4:
time: 137 us; the launch traced here: 136 us
  waiting for transfers between devices  55.5 us (41%)
  starting transfers between devices  44.1 us (32%)
  Pallas kernels  33.9 us (25%)
  local copies, waits for them, and re-layouts  1.81 us (1%)
    ppermute x8, waiting for transfers between devices, ring(): lax.ppermute(array, 'col', [(i, i + by) for i in range(peers) if 0 <= i +...  46.2 us
    ppermute x8, starting transfers between devices, ring(): lax.ppermute(array, 'col', [(i, i + by) for i in range(peers) if 0 <= i +...  28.7 us
    pallas_call x1, Pallas kernels, far_pass(): pl.pallas_call(far_kernel, grid_spec=pltpu.PrefetchScalarGridSpec(num_sca...  10.6 us
    all_to_all x2, waiting for transfers between devices, across(): lax.all_to_all(array, ('yh', 'uly'), split_axis=0, concat_axis=0, tiled=T...  9.31 us
    all_to_all x2, starting transfers between devices, across(): lax.all_to_all(array, ('yh', 'uly'), split_axis=0, concat_axis=0, tiled=T...  7.97 us
    all_to_all x2, starting transfers between devices, to_heads(): return lax.all_to_all(array, 'uly', split_axis=0, concat_axis=0, tiled=True)  7.4 us
    pallas_call x1, Pallas kernels, rest_pass(): pl.pallas_call(rest_kernel, grid=(heads // HPS,), in_specs=[column(), col...  7.14 us
    pallas_call x1, Pallas kernels, near_pass(): pl.pallas_call(near_kernel, grid=(heads // HPS,), in_specs=[column(), col...  4.17 us
  transfers between devices with their start and end apart: 12, of which 10 were waited for; matrix products, arithmetic and copies ran while one was open for 0% of the time, Pallas kernels for 16%

profile of v4, /device:TPU:6, one launch (start us, length us, event | category | flops | bytes accessed | tf_op | source)
XLA Modules:
  0.0 136.2 jit_solution(8700177521902872339)
XLA Ops:
  0.6 0.9 copy-done
  1.5 0.9 copy-done.1
  2.5 3.8 %collective-permute-start = (bf16[4,128,256]{2,1,0:T(8,128)(2,1)S(1)}, bf16[4,128,256]{2,1,0:T(8,128)(2,1)S(1)}, u32[]{:S(2)}, u32[]{:S(2)}) collective-permute-start(bf16[4,128,256]{2,1,0:T(8,128)(2,1)S(1)} %shard_map.93.kv_ref.refs_0_), channel_id=1, source_target_pairs={{0,8},{8,16},{16,24},{24,32},{32,40},{40,48},{48,56},{56,64},{64,7... | collective-permute-start | bytes 786440 | tf_op jit(solution)/shard_map/ppermute | solution.py:446
  6.3 3.8 %shard_map.95 = bf16[4,128,2304]{2,1,0:T(8,128)(2,1)} custom-call(bf16[128,4096]{1,0:T(8,128)(2,1)} %q_ref.1, bf16[128,4096]{1,0:T(8,128)(2,1)} %g_ref.1, bf16[4,128,256]{2,1,0:T(8,128)(2,1)S(1)} %shard_map.93.kv_ref.refs_0_), custom_call_target="tpu_custom_call" | custom-call | tf_op jit(solution)/shard_map/pallas_call | solution.py:349
  10.2 3.8 %all-to-all-start = ((bf16[4,128,2304]{2,1,0:T(8,128)(2,1)}), bf16[4,128,2304]{2,1,0:T(8,128)(2,1)S(1)}, u32[]{:S(2)}, u32[]{:S(2)}) async-start(bf16[4,128,2304]{2,1,0:T(8,128)(2,1)} %shard_map.95), calls=%async_computation | async-start | bytes 4718592 | tf_op jit(solution)/shard_map/all_to_all | solution.py:450
  13.9 6.5 %collective-permute-done.refs_1_ = bf16[4,128,256]{2,1,0:T(8,128)(2,1)S(1)} collective-permute-done((bf16[4,128,256]{2,1,0:T(8,128)(2,1)S(1)}, bf16[4,128,256]{2,1,0:T(8,128)(2,1)S(1)}, u32[]{:S(2)}, u32[]{:S(2)}) %collective-permute-start) | collective-permute-done | bytes 262176 | tf_op jit(solution)/shard_map/ppermute | solution.py:446
  20.5 1.9 %collective-permute-start.1 = (bf16[4,128,256]{2,1,0:T(8,128)(2,1)S(1)}, bf16[4,128,256]{2,1,0:T(8,128)(2,1)S(1)}, u32[]{:S(2)}, u32[]{:S(2)}) collective-permute-start(bf16[4,128,256]{2,1,0:T(8,128)(2,1)S(1)} %collective-permute-done.refs_1_), channel_id=1, source_target_pairs={{0,8},{8,16},{16,24},{24,32},{32,40},{40,48},{48,56},{56,64},{64,7... | collective-permute-start | bytes 786440 | tf_op jit(solution)/shard_map/ppermute | solution.py:446
  22.4 9.6 %collective-permute-done.1.refs_2_ = bf16[4,128,256]{2,1,0:T(8,128)(2,1)S(1)} collective-permute-done((bf16[4,128,256]{2,1,0:T(8,128)(2,1)S(1)}, bf16[4,128,256]{2,1,0:T(8,128)(2,1)S(1)}, u32[]{:S(2)}, u32[]{:S(2)}) %collective-permute-start.1) | collective-permute-done | bytes 262176 | tf_op jit(solution)/shard_map/ppermute | solution.py:446
  31.9 1.9 %collective-permute-start.2 = (bf16[4,128,256]{2,1,0:T(8,128)(2,1)S(1)}, bf16[4,128,256]{2,1,0:T(8,128)(2,1)S(1)}, u32[]{:S(2)}, u32[]{:S(2)}) collective-permute-start(bf16[4,128,256]{2,1,0:T(8,128)(2,1)S(1)} %collective-permute-done.1.refs_2_), channel_id=1, source_target_pairs={{0,8},{8,16},{16,24},{24,32},{32,40},{40,48},{48,56},{56,64},{64,7... | collective-permute-start | bytes 786440 | tf_op jit(solution)/shard_map/ppermute | solution.py:446
  33.9 8.6 %collective-permute-done.2.refs_3_ = bf16[4,128,256]{2,1,0:T(8,128)(2,1)S(1)} collective-permute-done((bf16[4,128,256]{2,1,0:T(8,128)(2,1)S(1)}, bf16[4,128,256]{2,1,0:T(8,128)(2,1)S(1)}, u32[]{:S(2)}, u32[]{:S(2)}) %collective-permute-start.2) | collective-permute-done | bytes 262176 | tf_op jit(solution)/shard_map/ppermute | solution.py:446
  42.5 1.9 %collective-permute-start.3 = (bf16[4,128,256]{2,1,0:T(8,128)(2,1)S(1)}, bf16[4,128,256]{2,1,0:T(8,128)(2,1)S(1)}, u32[]{:S(2)}, u32[]{:S(2)}) collective-permute-start(bf16[4,128,256]{2,1,0:T(8,128)(2,1)S(1)} %collective-permute-done.2.refs_3_), channel_id=1, source_target_pairs={{0,8},{8,16},{16,24},{24,32},{32,40},{40,48},{48,56},{56,64},{64,7... | collective-permute-start | bytes 786440 | tf_op jit(solution)/shard_map/ppermute | solution.py:446
  44.4 1.2 shard_map.94.info
  45.6 7.2 %collective-permute-done.3.refs_4_ = bf16[4,128,256]{2,1,0:T(8,128)(2,1)S(1)} collective-permute-done((bf16[4,128,256]{2,1,0:T(8,128)(2,1)S(1)}, bf16[4,128,256]{2,1,0:T(8,128)(2,1)S(1)}, u32[]{:S(2)}, u32[]{:S(2)}) %collective-permute-start.3) | collective-permute-done | bytes 262176 | tf_op jit(solution)/shard_map/ppermute | solution.py:446
  52.9 1.4 %shard_map.96 = bf16[8,128,256]{2,1,0:T(8,128)(2,1)} custom-call(s32[4]{0:T(128)S(1)} %shard_map.94.info, bf16[4,128,256]{2,1,0:T(8,128)(2,1)S(1)} %shard_map.93.kv_ref.refs_0_, bf16[4,128,256]{2,1,0:T(8,128)(2,1)S(1)} %collective-permute-done.refs_1_, bf16[4,128,256]{2,1,0:T(8,128)(2,1)S(1)} %collective-permute-done.1.refs_2_, ...), custom_call_target="tpu_custom_call" | custom-call | flops 10000000000 | bytes 41943040 | tf_op jit(solution)/shard_map/pallas_call | solution.py:310
  54.3 4.5 %all-to-all-start.1 = ((bf16[8,128,256]{2,1,0:T(8,128)(2,1)}), bf16[8,128,256]{2,1,0:T(8,128)(2,1)S(1)}, u32[]{:S(2)}, u32[]{:S(2)}) async-start(bf16[8,128,256]{2,1,0:T(8,128)(2,1)} %shard_map.96), calls=%async_computation.1 | async-start | bytes 1048576 | tf_op jit(solution)/shard_map/all_to_all | solution.py:454
  58.8 4.2 %shard_map.97 = (bf16[8,128,512]{2,1,0:T(8,128)(2,1)}, f32[8,8,512]{2,1,0:T(8,128)S(1)}) custom-call(bf16[512,2304]{1,0:T(8,128)(2,1)S(1)} %bitcast.11, bf16[512,2304]{1,0:T(8,128)(2,1)S(1)} %bitcast.12, bf16[512,2304]{1,0:T(8,128)(2,1)S(1)} %bitcast.13), custom_call_target="tpu_custom_call" | custom-call | flops 3000000000 | bytes 4194304 | tf_op jit(solution)/shard_map/pallas_call | solution.py:209
  63.0 6.2 %all-to-all-done.1 = bf16[8,128,256]{2,1,0:T(8,128)(2,1)S(1)} async-done(((bf16[8,128,256]{2,1,0:T(8,128)(2,1)}), bf16[8,128,256]{2,1,0:T(8,128)(2,1)S(1)}, u32[]{:S(2)}, u32[]{:S(2)}) %all-to-all-start.1) | async-done | bytes 524320 | tf_op jit(solution)/shard_map/all_to_all | solution.py:454
  69.1 10.6 %shard_map.98 = (bf16[8,256,512]{2,1,0:T(8,128)(2,1)}, f32[8,8,512]{2,1,0:T(8,128)S(1)}, bf16[2,512,256]{2,1,0:T(8,128)(2,1)}) custom-call(s32[4]{0:T(128)S(1)} %shard_map.94.info, bf16[512,2304]{1,0:T(8,128)(2,1)S(1)} %bitcast.14, bf16[512,2304]{1,0:T(8,128)(2,1)S(1)} %bitcast.15, bf16[2,512,256]{2,1,0:T(8,128)(2,1)S(1)} %bitcast.19, ...), custom_call_target="tpu_custom_call" | custom-call | flops 6000000000 | bytes 8388608 | tf_op jit(solution)/shard_map/pallas_call | solution.py:225
  79.7 3.5 %all-to-all-start.2 = ((bf16[8,128,256]{2,1,0:T(8,128)(2,1)}), bf16[8,128,256]{2,1,0:T(8,128)(2,1)S(1)}, u32[]{:S(2)}, u32[]{:S(2)}) async-start(bf16[8,128,256]{2,1,0:T(8,128)(2,1)} %bitcast.3), calls=%async_computation.2 | async-start | bytes 1048576 | tf_op jit(solution)/shard_map/all_to_all | solution.py:454
  83.2 7.1 %shard_map.99 = bf16[512,2304]{1,0:T(8,128)(2,1)} custom-call(bf16[512,2304]{1,0:T(8,128)(2,1)S(1)} %bitcast.16, bf16[512,2304]{1,0:T(8,128)(2,1)S(1)} %bitcast.17, bf16[512,2304]{1,0:T(8,128)(2,1)S(1)} %bitcast.18, bf16[8,256,512]{2,1,0:T(8,128)(2,1)} %get-tuple-element.23.both_ref, f32[8,8,512]{2,1,0:T(8,128)S(1)} %get-tuple-element.24.line_ref), custom_call_target="tpu_custom_call" | custom-call | flops 5000000000 | bytes 6291456 | tf_op jit(solution)/shard_map/pallas_call | solution.py:250
  90.4 3.1 %all-to-all-done.2 = bf16[8,128,256]{2,1,0:T(8,128)(2,1)S(1)} async-done(((bf16[8,128,256]{2,1,0:T(8,128)(2,1)}), bf16[8,128,256]{2,1,0:T(8,128)(2,1)S(1)}, u32[]{:S(2)}, u32[]{:S(2)}) %all-to-all-start.2) | async-done | bytes 524320 | tf_op jit(solution)/shard_map/all_to_all | solution.py:454
  94.1 1.9 %collective-permute-start.4 = (bf16[4,128,256]{2,1,0:T(8,128)(2,1)S(1)}, bf16[4,128,256]{2,1,0:T(8,128)(2,1)S(1)}, u32[]{:S(2)}, u32[]{:S(2)}) collective-permute-start(bf16[4,128,256]{2,1,0:T(8,128)(2,1)S(1)} %shard_map.101), channel_id=1, source_target_pairs={{8,0},{16,8},{24,16},{32,24},{40,32},{48,40},{56,48},{64,56},{72,6... | collective-permute-start | bytes 786440 | tf_op jit(solution)/shard_map/ppermute | solution.py:446
  96.0 3.6 %all-to-all-start.3 = ((bf16[4,128,2304]{2,1,0:T(8,128)(2,1)}), bf16[4,128,2304]{2,1,0:T(8,128)(2,1)S(1)}, u32[]{:S(2)}, u32[]{:S(2)}) async-start(bf16[4,128,2304]{2,1,0:T(8,128)(2,1)} %bitcast.21), calls=%async_computation.3 | async-start | bytes 4718592 | tf_op jit(solution)/shard_map/all_to_all | solution.py:450
  99.6 4.2 %collective-permute-done.4.refs_0_ = bf16[4,128,256]{2,1,0:T(8,128)(2,1)S(1)} collective-permute-done((bf16[4,128,256]{2,1,0:T(8,128)(2,1)S(1)}, bf16[4,128,256]{2,1,0:T(8,128)(2,1)S(1)}, u32[]{:S(2)}, u32[]{:S(2)}) %collective-permute-start.4) | collective-permute-done | bytes 262176 | tf_op jit(solution)/shard_map/ppermute | solution.py:446
  104.4 4.3 %collective-permute-start.5 = (bf16[4,128,256]{2,1,0:T(8,128)(2,1)S(1)}, bf16[4,128,256]{2,1,0:T(8,128)(2,1)S(1)}, u32[]{:S(2)}, u32[]{:S(2)}) collective-permute-start(bf16[4,128,256]{2,1,0:T(8,128)(2,1)S(1)} %shard_map.102), channel_id=1, source_target_pairs={{8,0},{16,8},{24,16},{32,24},{40,32},{48,40},{56,48},{64,56},{72,6... | collective-permute-start | bytes 786440 | tf_op jit(solution)/shard_map/ppermute | solution.py:446
  108.7 4.8 %collective-permute-done.5.refs_0_ = bf16[4,128,256]{2,1,0:T(8,128)(2,1)S(1)} collective-permute-done((bf16[4,128,256]{2,1,0:T(8,128)(2,1)S(1)}, bf16[4,128,256]{2,1,0:T(8,128)(2,1)S(1)}, u32[]{:S(2)}, u32[]{:S(2)}) %collective-permute-start.5) | collective-permute-done | bytes 262176 | tf_op jit(solution)/shard_map/ppermute | solution.py:446
  114.1 6.5 %collective-permute-start.6 = (bf16[4,128,256]{2,1,0:T(8,128)(2,1)S(1)}, bf16[4,128,256]{2,1,0:T(8,128)(2,1)S(1)}, u32[]{:S(2)}, u32[]{:S(2)}) collective-permute-start(bf16[4,128,256]{2,1,0:T(8,128)(2,1)S(1)} %shard_map.103), channel_id=1, source_target_pairs={{8,0},{16,8},{24,16},{32,24},{40,32},{48,40},{56,48},{64,56},{72,6... | collective-permute-start | bytes 786440 | tf_op jit(solution)/shard_map/ppermute | solution.py:446
  120.6 3.9 %collective-permute-done.6.refs_0_ = bf16[4,128,256]{2,1,0:T(8,128)(2,1)S(1)} collective-permute-done((bf16[4,128,256]{2,1,0:T(8,128)(2,1)S(1)}, bf16[4,128,256]{2,1,0:T(8,128)(2,1)S(1)}, u32[]{:S(2)}, u32[]{:S(2)}) %collective-permute-start.6) | collective-permute-done | bytes 262176 | tf_op jit(solution)/shard_map/ppermute | solution.py:446
  125.0 6.5 %collective-permute-start.7 = (bf16[4,128,256]{2,1,0:T(8,128)(2,1)S(1)}, bf16[4,128,256]{2,1,0:T(8,128)(2,1)S(1)}, u32[]{:S(2)}, u32[]{:S(2)}) collective-permute-start(bf16[4,128,256]{2,1,0:T(8,128)(2,1)S(1)} %shard_map.104), channel_id=1, source_target_pairs={{8,0},{16,8},{24,16},{32,24},{40,32},{48,40},{56,48},{64,56},{72,6... | collective-permute-start | bytes 786440 | tf_op jit(solution)/shard_map/ppermute | solution.py:446
  131.5 2.4 %shard_map.100 = (bf16[128,4096]{1,0:T(8,128)(2,1)}, bf16[128,4096]{1,0:T(8,128)(2,1)}, f32[4,128,256]{2,1,0:T(8,128)S(1)}) custom-call(s32[4]{0:T(128)S(1)} %shard_map.94.info, bf16[4,128,2304]{2,1,0:T(8,128)(2,1)S(1)} %all-to-all-done.3.all_ref, bf16[2,4,128,256]{3,2,1,0:T(8,128)(2,1)S(1)} %bitcast.10), custom_call_target="tpu_custom_call" | custom-call | tf_op jit(solution)/shard_map/pallas_call | solution.py:375
  134.0 1.4 %collective-permute-done.7.moved_ref = bf16[4,128,256]{2,1,0:T(8,128)(2,1)S(1)} collective-permute-done((bf16[4,128,256]{2,1,0:T(8,128)(2,1)S(1)}, bf16[4,128,256]{2,1,0:T(8,128)(2,1)S(1)}, u32[]{:S(2)}, u32[]{:S(2)}) %collective-permute-start.7) | collective-permute-done | bytes 262176 | tf_op jit(solution)/shard_map/ppermute | solution.py:446
  135.4 0.8 shard_map.105
  (13 shorter events, 2.4 us)
Async XLA Ops:
  0.6 0.9 copy-start
  1.5 0.9 copy-start.1
  2.5 18.0 %collective-permute-start = (bf16[4,128,256]{2,1,0:T(8,128)(2,1)S(1)}, bf16[4,128,256]{2,1,0:T(8,128)(2,1)S(1)}, u32[]{:S(2)}, u32[]{:S(2)}) collective-permute-start(bf16[4,128,256]{2,1,0:T(8,128)(2,1)S(1)} %shard_map.93.kv_ref.refs_0_), channel_id=1, source_target_pairs={{0,8},{8,16},{16,24},{24,32},{32,40},{40,48},{48,56},{56,64},{64,7... | collective-permute-start | bytes 786440 | tf_op jit(solution)/shard_map/ppermute | solution.py:446
  10.2 34.3 %copy-start.2 = (s32[128,2]{0,1:T(2,128)S(1)}, s32[128,2]{0,1:T(2,128)}, u32[]{:S(2)}) copy-start(s32[128,2]{0,1:T(2,128)} %param.10) | copy-start | bytes 3076
  10.2 34.3 %copy-start.3 = (s32[128]{0:T(128)S(1)}, s32[128]{0:T(128)}, u32[]{:S(2)}) copy-start(s32[128]{0:T(128)} %count_ref.1) | copy-start | bytes 1540
  10.2 44.1 %all-to-all-start = ((bf16[4,128,2304]{2,1,0:T(8,128)(2,1)}), bf16[4,128,2304]{2,1,0:T(8,128)(2,1)S(1)}, u32[]{:S(2)}, u32[]{:S(2)}) async-start(bf16[4,128,2304]{2,1,0:T(8,128)(2,1)} %shard_map.95), calls=%async_computation | async-start | bytes 4718592 | tf_op jit(solution)/shard_map/all_to_all | solution.py:450
  20.5 11.5 %collective-permute-start.1 = (bf16[4,128,256]{2,1,0:T(8,128)(2,1)S(1)}, bf16[4,128,256]{2,1,0:T(8,128)(2,1)S(1)}, u32[]{:S(2)}, u32[]{:S(2)}) collective-permute-start(bf16[4,128,256]{2,1,0:T(8,128)(2,1)S(1)} %collective-permute-done.refs_1_), channel_id=1, source_target_pairs={{0,8},{8,16},{16,24},{24,32},{32,40},{40,48},{48,56},{56,64},{64,7... | collective-permute-start | bytes 786440 | tf_op jit(solution)/shard_map/ppermute | solution.py:446
  31.9 10.6 %collective-permute-start.2 = (bf16[4,128,256]{2,1,0:T(8,128)(2,1)S(1)}, bf16[4,128,256]{2,1,0:T(8,128)(2,1)S(1)}, u32[]{:S(2)}, u32[]{:S(2)}) collective-permute-start(bf16[4,128,256]{2,1,0:T(8,128)(2,1)S(1)} %collective-permute-done.1.refs_2_), channel_id=1, source_target_pairs={{0,8},{8,16},{16,24},{24,32},{32,40},{40,48},{48,56},{56,64},{64,7... | collective-permute-start | bytes 786440 | tf_op jit(solution)/shard_map/ppermute | solution.py:446
  42.5 10.4 %collective-permute-start.3 = (bf16[4,128,256]{2,1,0:T(8,128)(2,1)S(1)}, bf16[4,128,256]{2,1,0:T(8,128)(2,1)S(1)}, u32[]{:S(2)}, u32[]{:S(2)}) collective-permute-start(bf16[4,128,256]{2,1,0:T(8,128)(2,1)S(1)} %collective-permute-done.2.refs_3_), channel_id=1, source_target_pairs={{0,8},{8,16},{16,24},{24,32},{32,40},{40,48},{48,56},{56,64},{64,7... | collective-permute-start | bytes 786440 | tf_op jit(solution)/shard_map/ppermute | solution.py:446
  54.3 14.8 %all-to-all-start.1 = ((bf16[8,128,256]{2,1,0:T(8,128)(2,1)}), bf16[8,128,256]{2,1,0:T(8,128)(2,1)S(1)}, u32[]{:S(2)}, u32[]{:S(2)}) async-start(bf16[8,128,256]{2,1,0:T(8,128)(2,1)} %shard_map.96), calls=%async_computation.1 | async-start | bytes 1048576 | tf_op jit(solution)/shard_map/all_to_all | solution.py:454
  79.7 13.8 %all-to-all-start.2 = ((bf16[8,128,256]{2,1,0:T(8,128)(2,1)}), bf16[8,128,256]{2,1,0:T(8,128)(2,1)S(1)}, u32[]{:S(2)}, u32[]{:S(2)}) async-start(bf16[8,128,256]{2,1,0:T(8,128)(2,1)} %bitcast.3), calls=%async_computation.2 | async-start | bytes 1048576 | tf_op jit(solution)/shard_map/all_to_all | solution.py:454
  94.1 9.7 %collective-permute-start.4 = (bf16[4,128,256]{2,1,0:T(8,128)(2,1)S(1)}, bf16[4,128,256]{2,1,0:T(8,128)(2,1)S(1)}, u32[]{:S(2)}, u32[]{:S(2)}) collective-permute-start(bf16[4,128,256]{2,1,0:T(8,128)(2,1)S(1)} %shard_map.101), channel_id=1, source_target_pairs={{8,0},{16,8},{24,16},{32,24},{40,32},{48,40},{56,48},{64,56},{72,6... | collective-permute-start | bytes 786440 | tf_op jit(solution)/shard_map/ppermute | solution.py:446
  96.0 35.5 %all-to-all-start.3 = ((bf16[4,128,2304]{2,1,0:T(8,128)(2,1)}), bf16[4,128,2304]{2,1,0:T(8,128)(2,1)S(1)}, u32[]{:S(2)}, u32[]{:S(2)}) async-start(bf16[4,128,2304]{2,1,0:T(8,128)(2,1)} %bitcast.21), calls=%async_computation.3 | async-start | bytes 4718592 | tf_op jit(solution)/shard_map/all_to_all | solution.py:450
  104.4 9.0 %collective-permute-start.5 = (bf16[4,128,256]{2,1,0:T(8,128)(2,1)S(1)}, bf16[4,128,256]{2,1,0:T(8,128)(2,1)S(1)}, u32[]{:S(2)}, u32[]{:S(2)}) collective-permute-start(bf16[4,128,256]{2,1,0:T(8,128)(2,1)S(1)} %shard_map.102), channel_id=1, source_target_pairs={{8,0},{16,8},{24,16},{32,24},{40,32},{48,40},{56,48},{64,56},{72,6... | collective-permute-start | bytes 786440 | tf_op jit(solution)/shard_map/ppermute | solution.py:446
  114.1 10.4 %collective-permute-start.6 = (bf16[4,128,256]{2,1,0:T(8,128)(2,1)S(1)}, bf16[4,128,256]{2,1,0:T(8,128)(2,1)S(1)}, u32[]{:S(2)}, u32[]{:S(2)}) collective-permute-start(bf16[4,128,256]{2,1,0:T(8,128)(2,1)S(1)} %shard_map.103), channel_id=1, source_target_pairs={{8,0},{16,8},{24,16},{32,24},{40,32},{48,40},{56,48},{64,56},{72,6... | collective-permute-start | bytes 786440 | tf_op jit(solution)/shard_map/ppermute | solution.py:446
  125.0 10.4 %collective-permute-start.7 = (bf16[4,128,256]{2,1,0:T(8,128)(2,1)S(1)}, bf16[4,128,256]{2,1,0:T(8,128)(2,1)S(1)}, u32[]{:S(2)}, u32[]{:S(2)}) collective-permute-start(bf16[4,128,256]{2,1,0:T(8,128)(2,1)S(1)} %shard_map.104), channel_id=1, source_target_pairs={{8,0},{16,8},{24,16},{32,24},{40,32},{48,40},{56,48},{64,56},{72,6... | collective-permute-start | bytes 786440 | tf_op jit(solution)/shard_map/ppermute | solution.py:446

commit v5 on v4

--- a/solution.py
+++ b/solution.py
@@ -313,7 +313,7 @@
         out_specs=vmem,
         out_shape=sds((2 * heads, rows, width), jnp.bfloat16),
         compiler_params=pltpu.CompilerParams(vmem_limit_bytes=8 * MIB),
-        cost_estimate=pl.CostEstimate(flops=10 * 10**9, bytes_accessed=40 * MIB, transcendentals=0),
+        cost_estimate=pl.CostEstimate(flops=12 * 10**9, bytes_accessed=40 * MIB, transcendentals=0),
     )(info, *pieces)
 
 
@@ -465,10 +465,11 @@
     kv = pack_pass(key_states, value_states)
     info = gate_pass(after(block_list, kv), block_count)
 
-    pieces = [kv]
-    for _ in range(STEPS):
+    pieces = [kv, ring(kv, 1)]
+    x = join_pass(query_states, out_grad, kv)
+    pieces[1], x = lax.optimization_barrier((pieces[1], x))
+    for _ in range(STEPS - 1):
         pieces.append(ring(pieces[-1], 1))
-    x = join_pass(query_states, out_grad, kv)
     x = to_heads(x).reshape(4 * here, -1)
     near, stats = near_pass(x)
     far = across(after(pick_pass(info, pieces), x)).reshape(2, 4 * here, pair)

time: 137 us -> 141 us (1.029)
  starting transfers between devices: 44.1 us -> 50.3 us
  waiting for transfers between devices: 55.5 us -> 53 us
    ppermute x8, starting transfers between devices: 28.7 us -> 35 us  [ring(): lax.ppermute(array, 'col', [(i, i + by) for i in range(peers) if 0 <= i +...]
    ppermute x8, waiting for transfers between devices: 46.2 us -> 43.5 us  [ring(): lax.ppermute(array, 'col', [(i, i + by) for i in range(peers) if 0 <= i +...]
  transfers between devices with their start and end apart: 12 -> 12, of which waited for: 10 -> 11; matrix products, arithmetic and copies ran while one was open for 0% -> 0% of each run, Pallas kernels for 16% -> 16%
where the time goes in v5:
time: 141 us; the launch traced here: 140 us
  waiting for transfers between devices  53 us (38%)
  starting transfers between devices  50.3 us (36%)
  Pallas kernels  33.9 us (24%)
  local copies, waits for them, and re-layouts  1.81 us (1%)
    ppermute x8, waiting for transfers between devices, ring(): lax.ppermute(array, 'col', [(i, i + by) for i in range(peers) if 0 <= i +...  43.5 us
    ppermute x8, starting transfers between devices, ring(): lax.ppermute(array, 'col', [(i, i + by) for i in range(peers) if 0 <= i +...  35 us
    pallas_call x1, Pallas kernels, far_pass(): pl.pallas_call(far_kernel, grid_spec=pltpu.PrefetchScalarGridSpec(num_sca...  10.6 us
    all_to_all x2, waiting for transfers between devices, across(): lax.all_to_all(array, ('yh', 'uly'), split_axis=0, concat_axis=0, tiled=T...  9.31 us
    all_to_all x2, starting transfers between devices, across(): lax.all_to_all(array, ('yh', 'uly'), split_axis=0, concat_axis=0, tiled=T...  7.97 us
    all_to_all x2, starting transfers between devices, to_heads(): return lax.all_to_all(array, 'uly', split_axis=0, concat_axis=0, tiled=True)  7.28 us
    pallas_call x1, Pallas kernels, rest_pass(): pl.pallas_call(rest_kernel, grid=(heads // HPS,), in_specs=[column(), col...  7.14 us
    pallas_call x1, Pallas kernels, near_pass(): pl.pallas_call(near_kernel, grid=(heads // HPS,), in_specs=[column(), col...  4.17 us
  transfers between devices with their start and end apart: 12, of which 11 were waited for; matrix products, arithmetic and copies ran while one was open for 0% of the time, Pallas kernels for 16%

profile of v5, /device:TPU:6, one launch (start us, length us, event | category | flops | bytes accessed | tf_op | source)
XLA Modules:
  0.0 139.9 jit_solution(10968090731719839885)
XLA Ops:
  0.6 0.9 copy-done
  1.5 0.9 copy-done.1
  2.5 3.8 %collective-permute-start = (bf16[4,128,256]{2,1,0:T(8,128)(2,1)S(1)}, bf16[4,128,256]{2,1,0:T(8,128)(2,1)S(1)}, u32[]{:S(2)}, u32[]{:S(2)}) collective-permute-start(bf16[4,128,256]{2,1,0:T(8,128)(2,1)S(1)} %shard_map.93.kv_ref.refs_0_), channel_id=1, source_target_pairs={{0,8},{8,16},{16,24},{24,32},{32,40},{40,48},{48,56},{56,64},{64,7... | collective-permute-start | bytes 786440 | tf_op jit(solution)/shard_map/ppermute | solution.py:446
  6.3 3.8 %shard_map.95 = bf16[4,128,2304]{2,1,0:T(8,128)(2,1)} custom-call(bf16[128,4096]{1,0:T(8,128)(2,1)} %q_ref.1, bf16[128,4096]{1,0:T(8,128)(2,1)} %g_ref.1, bf16[4,128,256]{2,1,0:T(8,128)(2,1)S(1)} %shard_map.93.kv_ref.refs_0_), custom_call_target="tpu_custom_call" | custom-call | tf_op jit(solution)/shard_map/pallas_call | solution.py:349
  10.2 10.3 %collective-permute-done.refs_1_ = bf16[4,128,256]{2,1,0:T(8,128)(2,1)S(1)} collective-permute-done((bf16[4,128,256]{2,1,0:T(8,128)(2,1)S(1)}, bf16[4,128,256]{2,1,0:T(8,128)(2,1)S(1)}, u32[]{:S(2)}, u32[]{:S(2)}) %collective-permute-start) | collective-permute-done | bytes 262176 | tf_op jit(solution)/shard_map/ppermute | solution.py:446
  20.5 1.9 %collective-permute-start.1 = (bf16[4,128,256]{2,1,0:T(8,128)(2,1)S(1)}, bf16[4,128,256]{2,1,0:T(8,128)(2,1)S(1)}, u32[]{:S(2)}, u32[]{:S(2)}) collective-permute-start(bf16[4,128,256]{2,1,0:T(8,128)(2,1)S(1)} %collective-permute-done.refs_1_), channel_id=1, source_target_pairs={{0,8},{8,16},{16,24},{24,32},{32,40},{40,48},{48,56},{56,64},{64,7... | collective-permute-start | bytes 786440 | tf_op jit(solution)/shard_map/ppermute | solution.py:446
  22.4 3.6 %all-to-all-start = ((bf16[4,128,2304]{2,1,0:T(8,128)(2,1)}), bf16[4,128,2304]{2,1,0:T(8,128)(2,1)S(1)}, u32[]{:S(2)}, u32[]{:S(2)}) async-start(bf16[4,128,2304]{2,1,0:T(8,128)(2,1)} %shard_map.95), calls=%async_computation | async-start | bytes 4718592 | tf_op jit(solution)/shard_map/all_to_all | solution.py:450
  26.0 5.9 %collective-permute-done.1.refs_2_ = bf16[4,128,256]{2,1,0:T(8,128)(2,1)S(1)} collective-permute-done((bf16[4,128,256]{2,1,0:T(8,128)(2,1)S(1)}, bf16[4,128,256]{2,1,0:T(8,128)(2,1)S(1)}, u32[]{:S(2)}, u32[]{:S(2)}) %collective-permute-start.1) | collective-permute-done | bytes 262176 | tf_op jit(solution)/shard_map/ppermute | solution.py:446
  31.9 1.9 %collective-permute-start.2 = (bf16[4,128,256]{2,1,0:T(8,128)(2,1)S(1)}, bf16[4,128,256]{2,1,0:T(8,128)(2,1)S(1)}, u32[]{:S(2)}, u32[]{:S(2)}) collective-permute-start(bf16[4,128,256]{2,1,0:T(8,128)(2,1)S(1)} %collective-permute-done.1.refs_2_), channel_id=1, source_target_pairs={{0,8},{8,16},{16,24},{24,32},{32,40},{40,48},{48,56},{56,64},{64,7... | collective-permute-start | bytes 786440 | tf_op jit(solution)/shard_map/ppermute | solution.py:446
  33.9 8.6 %collective-permute-done.2.refs_3_ = bf16[4,128,256]{2,1,0:T(8,128)(2,1)S(1)} collective-permute-done((bf16[4,128,256]{2,1,0:T(8,128)(2,1)S(1)}, bf16[4,128,256]{2,1,0:T(8,128)(2,1)S(1)}, u32[]{:S(2)}, u32[]{:S(2)}) %collective-permute-start.2) | collective-permute-done | bytes 262176 | tf_op jit(solution)/shard_map/ppermute | solution.py:446
  42.5 1.9 %collective-permute-start.3 = (bf16[4,128,256]{2,1,0:T(8,128)(2,1)S(1)}, bf16[4,128,256]{2,1,0:T(8,128)(2,1)S(1)}, u32[]{:S(2)}, u32[]{:S(2)}) collective-permute-start(bf16[4,128,256]{2,1,0:T(8,128)(2,1)S(1)} %collective-permute-done.2.refs_3_), channel_id=1, source_target_pairs={{0,8},{8,16},{16,24},{24,32},{32,40},{40,48},{48,56},{56,64},{64,7... | collective-permute-start | bytes 786440 | tf_op jit(solution)/shard_map/ppermute | solution.py:446
  44.4 1.2 shard_map.94.info
  45.6 7.2 %collective-permute-done.3.refs_4_ = bf16[4,128,256]{2,1,0:T(8,128)(2,1)S(1)} collective-permute-done((bf16[4,128,256]{2,1,0:T(8,128)(2,1)S(1)}, bf16[4,128,256]{2,1,0:T(8,128)(2,1)S(1)}, u32[]{:S(2)}, u32[]{:S(2)}) %collective-permute-start.3) | collective-permute-done | bytes 262176 | tf_op jit(solution)/shard_map/ppermute | solution.py:446
  52.9 1.4 %shard_map.96 = bf16[8,128,256]{2,1,0:T(8,128)(2,1)} custom-call(s32[4]{0:T(128)S(1)} %shard_map.94.info, bf16[4,128,256]{2,1,0:T(8,128)(2,1)S(1)} %shard_map.93.kv_ref.refs_0_, bf16[4,128,256]{2,1,0:T(8,128)(2,1)S(1)} %collective-permute-done.refs_1_, bf16[4,128,256]{2,1,0:T(8,128)(2,1)S(1)} %collective-permute-done.1.refs_2_, ...), custom_call_target="tpu_custom_call" | custom-call | flops 12000000000 | bytes 41943040 | tf_op jit(solution)/shard_map/pallas_call | solution.py:310
  54.5 4.5 %all-to-all-start.1 = ((bf16[8,128,256]{2,1,0:T(8,128)(2,1)}), bf16[8,128,256]{2,1,0:T(8,128)(2,1)S(1)}, u32[]{:S(2)}, u32[]{:S(2)}) async-start(bf16[8,128,256]{2,1,0:T(8,128)(2,1)} %shard_map.96), calls=%async_computation.1 | async-start | bytes 1048576 | tf_op jit(solution)/shard_map/all_to_all | solution.py:454
  59.0 4.2 %shard_map.97 = (bf16[8,128,512]{2,1,0:T(8,128)(2,1)}, f32[8,8,512]{2,1,0:T(8,128)S(1)}) custom-call(bf16[512,2304]{1,0:T(8,128)(2,1)S(1)} %bitcast.11, bf16[512,2304]{1,0:T(8,128)(2,1)S(1)} %bitcast.12, bf16[512,2304]{1,0:T(8,128)(2,1)S(1)} %bitcast.13), custom_call_target="tpu_custom_call" | custom-call | flops 3000000000 | bytes 4194304 | tf_op jit(solution)/shard_map/pallas_call | solution.py:209
  63.1 6.2 %all-to-all-done.1 = bf16[8,128,256]{2,1,0:T(8,128)(2,1)S(1)} async-done(((bf16[8,128,256]{2,1,0:T(8,128)(2,1)}), bf16[8,128,256]{2,1,0:T(8,128)(2,1)S(1)}, u32[]{:S(2)}, u32[]{:S(2)}) %all-to-all-start.1) | async-done | bytes 524320 | tf_op jit(solution)/shard_map/all_to_all | solution.py:454
  69.3 10.6 %shard_map.98 = (bf16[8,256,512]{2,1,0:T(8,128)(2,1)}, f32[8,8,512]{2,1,0:T(8,128)S(1)}, bf16[2,512,256]{2,1,0:T(8,128)(2,1)}) custom-call(s32[4]{0:T(128)S(1)} %shard_map.94.info, bf16[512,2304]{1,0:T(8,128)(2,1)S(1)} %bitcast.14, bf16[512,2304]{1,0:T(8,128)(2,1)S(1)} %bitcast.15, bf16[2,512,256]{2,1,0:T(8,128)(2,1)S(1)} %bitcast.19, ...), custom_call_target="tpu_custom_call" | custom-call | flops 6000000000 | bytes 8388608 | tf_op jit(solution)/shard_map/pallas_call | solution.py:225
  79.9 3.5 %all-to-all-start.2 = ((bf16[8,128,256]{2,1,0:T(8,128)(2,1)}), bf16[8,128,256]{2,1,0:T(8,128)(2,1)S(1)}, u32[]{:S(2)}, u32[]{:S(2)}) async-start(bf16[8,128,256]{2,1,0:T(8,128)(2,1)} %bitcast.3), calls=%async_computation.2 | async-start | bytes 1048576 | tf_op jit(solution)/shard_map/all_to_all | solution.py:454
  83.4 7.1 %shard_map.99 = bf16[512,2304]{1,0:T(8,128)(2,1)} custom-call(bf16[512,2304]{1,0:T(8,128)(2,1)S(1)} %bitcast.16, bf16[512,2304]{1,0:T(8,128)(2,1)S(1)} %bitcast.17, bf16[512,2304]{1,0:T(8,128)(2,1)S(1)} %bitcast.18, bf16[8,256,512]{2,1,0:T(8,128)(2,1)} %get-tuple-element.27.both_ref, f32[8,8,512]{2,1,0:T(8,128)S(1)} %get-tuple-element.28.line_ref), custom_call_target="tpu_custom_call" | custom-call | flops 5000000000 | bytes 6291456 | tf_op jit(solution)/shard_map/pallas_call | solution.py:250
  90.5 3.1 %all-to-all-done.2 = bf16[8,128,256]{2,1,0:T(8,128)(2,1)S(1)} async-done(((bf16[8,128,256]{2,1,0:T(8,128)(2,1)}), bf16[8,128,256]{2,1,0:T(8,128)(2,1)S(1)}, u32[]{:S(2)}, u32[]{:S(2)}) %all-to-all-start.2) | async-done | bytes 524320 | tf_op jit(solution)/shard_map/all_to_all | solution.py:454
  94.3 6.0 %collective-permute-start.4 = (bf16[4,128,256]{2,1,0:T(8,128)(2,1)S(1)}, bf16[4,128,256]{2,1,0:T(8,128)(2,1)S(1)}, u32[]{:S(2)}, u32[]{:S(2)}) collective-permute-start(bf16[4,128,256]{2,1,0:T(8,128)(2,1)S(1)} %shard_map.101), channel_id=1, source_target_pairs={{8,0},{16,8},{24,16},{32,24},{40,32},{48,40},{56,48},{64,56},{72,6... | collective-permute-start | bytes 786440 | tf_op jit(solution)/shard_map/ppermute | solution.py:446
  100.3 3.6 %all-to-all-start.3 = ((bf16[4,128,2304]{2,1,0:T(8,128)(2,1)}), bf16[4,128,2304]{2,1,0:T(8,128)(2,1)S(1)}, u32[]{:S(2)}, u32[]{:S(2)}) async-start(bf16[4,128,2304]{2,1,0:T(8,128)(2,1)} %bitcast.21), calls=%async_computation.3 | async-start | bytes 4718592 | tf_op jit(solution)/shard_map/all_to_all | solution.py:450
  103.9 1.7 %collective-permute-done.4.refs_0_ = bf16[4,128,256]{2,1,0:T(8,128)(2,1)S(1)} collective-permute-done((bf16[4,128,256]{2,1,0:T(8,128)(2,1)S(1)}, bf16[4,128,256]{2,1,0:T(8,128)(2,1)S(1)}, u32[]{:S(2)}, u32[]{:S(2)}) %collective-permute-start.4) | collective-permute-done | bytes 262176 | tf_op jit(solution)/shard_map/ppermute | solution.py:446
  106.3 6.5 %collective-permute-start.5 = (bf16[4,128,256]{2,1,0:T(8,128)(2,1)S(1)}, bf16[4,128,256]{2,1,0:T(8,128)(2,1)S(1)}, u32[]{:S(2)}, u32[]{:S(2)}) collective-permute-start(bf16[4,128,256]{2,1,0:T(8,128)(2,1)S(1)} %shard_map.102), channel_id=1, source_target_pairs={{8,0},{16,8},{24,16},{32,24},{40,32},{48,40},{56,48},{64,56},{72,6... | collective-permute-start | bytes 786440 | tf_op jit(solution)/shard_map/ppermute | solution.py:446
  112.7 4.4 %collective-permute-done.5.refs_0_ = bf16[4,128,256]{2,1,0:T(8,128)(2,1)S(1)} collective-permute-done((bf16[4,128,256]{2,1,0:T(8,128)(2,1)S(1)}, bf16[4,128,256]{2,1,0:T(8,128)(2,1)S(1)}, u32[]{:S(2)}, u32[]{:S(2)}) %collective-permute-start.5) | collective-permute-done | bytes 262176 | tf_op jit(solution)/shard_map/ppermute | solution.py:446
  117.8 6.5 %collective-permute-start.6 = (bf16[4,128,256]{2,1,0:T(8,128)(2,1)S(1)}, bf16[4,128,256]{2,1,0:T(8,128)(2,1)S(1)}, u32[]{:S(2)}, u32[]{:S(2)}) collective-permute-start(bf16[4,128,256]{2,1,0:T(8,128)(2,1)S(1)} %shard_map.103), channel_id=1, source_target_pairs={{8,0},{16,8},{24,16},{32,24},{40,32},{48,40},{56,48},{64,56},{72,6... | collective-permute-start | bytes 786440 | tf_op jit(solution)/shard_map/ppermute | solution.py:446
  124.3 3.9 %collective-permute-done.6.refs_0_ = bf16[4,128,256]{2,1,0:T(8,128)(2,1)S(1)} collective-permute-done((bf16[4,128,256]{2,1,0:T(8,128)(2,1)S(1)}, bf16[4,128,256]{2,1,0:T(8,128)(2,1)S(1)}, u32[]{:S(2)}, u32[]{:S(2)}) %collective-permute-start.6) | collective-permute-done | bytes 262176 | tf_op jit(solution)/shard_map/ppermute | solution.py:446
  128.7 6.5 %collective-permute-start.7 = (bf16[4,128,256]{2,1,0:T(8,128)(2,1)S(1)}, bf16[4,128,256]{2,1,0:T(8,128)(2,1)S(1)}, u32[]{:S(2)}, u32[]{:S(2)}) collective-permute-start(bf16[4,128,256]{2,1,0:T(8,128)(2,1)S(1)} %shard_map.104), channel_id=1, source_target_pairs={{8,0},{16,8},{24,16},{32,24},{40,32},{48,40},{56,48},{64,56},{72,6... | collective-permute-start | bytes 786440 | tf_op jit(solution)/shard_map/ppermute | solution.py:446
  135.2 2.4 %shard_map.100 = (bf16[128,4096]{1,0:T(8,128)(2,1)}, bf16[128,4096]{1,0:T(8,128)(2,1)}, f32[4,128,256]{2,1,0:T(8,128)S(1)}) custom-call(s32[4]{0:T(128)S(1)} %shard_map.94.info, bf16[4,128,2304]{2,1,0:T(8,128)(2,1)S(1)} %all-to-all-done.3.all_ref, bf16[2,4,128,256]{3,2,1,0:T(8,128)(2,1)S(1)} %bitcast.10), custom_call_target="tpu_custom_call" | custom-call | tf_op jit(solution)/shard_map/pallas_call | solution.py:375
  137.7 1.4 %collective-permute-done.7.moved_ref = bf16[4,128,256]{2,1,0:T(8,128)(2,1)S(1)} collective-permute-done((bf16[4,128,256]{2,1,0:T(8,128)(2,1)S(1)}, bf16[4,128,256]{2,1,0:T(8,128)(2,1)S(1)}, u32[]{:S(2)}, u32[]{:S(2)}) %collective-permute-start.7) | collective-permute-done | bytes 262176 | tf_op jit(solution)/shard_map/ppermute | solution.py:446
  139.1 0.8 shard_map.105
  (13 shorter events, 2.6 us)
Async XLA Ops:
  0.6 0.9 copy-start
  1.5 0.9 copy-start.1
  2.5 18.0 %collective-permute-start = (bf16[4,128,256]{2,1,0:T(8,128)(2,1)S(1)}, bf16[4,128,256]{2,1,0:T(8,128)(2,1)S(1)}, u32[]{:S(2)}, u32[]{:S(2)}) collective-permute-start(bf16[4,128,256]{2,1,0:T(8,128)(2,1)S(1)} %shard_map.93.kv_ref.refs_0_), channel_id=1, source_target_pairs={{0,8},{8,16},{16,24},{24,32},{32,40},{40,48},{48,56},{56,64},{64,7... | collective-permute-start | bytes 786440 | tf_op jit(solution)/shard_map/ppermute | solution.py:446
  10.2 34.3 %copy-start.2 = (s32[128,2]{0,1:T(2,128)S(1)}, s32[128,2]{0,1:T(2,128)}, u32[]{:S(2)}) copy-start(s32[128,2]{0,1:T(2,128)} %param.10) | copy-start | bytes 3076
  10.2 34.3 %copy-start.3 = (s32[128]{0:T(128)S(1)}, s32[128]{0:T(128)}, u32[]{:S(2)}) copy-start(s32[128]{0:T(128)} %count_ref.1) | copy-start | bytes 1540
  20.5 11.5 %collective-permute-start.1 = (bf16[4,128,256]{2,1,0:T(8,128)(2,1)S(1)}, bf16[4,128,256]{2,1,0:T(8,128)(2,1)S(1)}, u32[]{:S(2)}, u32[]{:S(2)}) collective-permute-start(bf16[4,128,256]{2,1,0:T(8,128)(2,1)S(1)} %collective-permute-done.refs_1_), channel_id=1, source_target_pairs={{0,8},{8,16},{16,24},{24,32},{32,40},{40,48},{48,56},{56,64},{64,7... | collective-permute-start | bytes 786440 | tf_op jit(solution)/shard_map/ppermute | solution.py:446
  22.4 32.1 %all-to-all-start = ((bf16[4,128,2304]{2,1,0:T(8,128)(2,1)}), bf16[4,128,2304]{2,1,0:T(8,128)(2,1)S(1)}, u32[]{:S(2)}, u32[]{:S(2)}) async-start(bf16[4,128,2304]{2,1,0:T(8,128)(2,1)} %shard_map.95), calls=%async_computation | async-start | bytes 4718592 | tf_op jit(solution)/shard_map/all_to_all | solution.py:450
  31.9 10.6 %collective-permute-start.2 = (bf16[4,128,256]{2,1,0:T(8,128)(2,1)S(1)}, bf16[4,128,256]{2,1,0:T(8,128)(2,1)S(1)}, u32[]{:S(2)}, u32[]{:S(2)}) collective-permute-start(bf16[4,128,256]{2,1,0:T(8,128)(2,1)S(1)} %collective-permute-done.1.refs_2_), channel_id=1, source_target_pairs={{0,8},{8,16},{16,24},{24,32},{32,40},{40,48},{48,56},{56,64},{64,7... | collective-permute-start | bytes 786440 | tf_op jit(solution)/shard_map/ppermute | solution.py:446
  42.5 10.4 %collective-permute-start.3 = (bf16[4,128,256]{2,1,0:T(8,128)(2,1)S(1)}, bf16[4,128,256]{2,1,0:T(8,128)(2,1)S(1)}, u32[]{:S(2)}, u32[]{:S(2)}) collective-permute-start(bf16[4,128,256]{2,1,0:T(8,128)(2,1)S(1)} %collective-permute-done.2.refs_3_), channel_id=1, source_target_pairs={{0,8},{8,16},{16,24},{24,32},{32,40},{40,48},{48,56},{56,64},{64,7... | collective-permute-start | bytes 786440 | tf_op jit(solution)/shard_map/ppermute | solution.py:446
  54.5 14.8 %all-to-all-start.1 = ((bf16[8,128,256]{2,1,0:T(8,128)(2,1)}), bf16[8,128,256]{2,1,0:T(8,128)(2,1)S(1)}, u32[]{:S(2)}, u32[]{:S(2)}) async-start(bf16[8,128,256]{2,1,0:T(8,128)(2,1)} %shard_map.96), calls=%async_computation.1 | async-start | bytes 1048576 | tf_op jit(solution)/shard_map/all_to_all | solution.py:454
  79.9 13.8 %all-to-all-start.2 = ((bf16[8,128,256]{2,1,0:T(8,128)(2,1)}), bf16[8,128,256]{2,1,0:T(8,128)(2,1)S(1)}, u32[]{:S(2)}, u32[]{:S(2)}) async-start(bf16[8,128,256]{2,1,0:T(8,128)(2,1)} %bitcast.3), calls=%async_computation.2 | async-start | bytes 1048576 | tf_op jit(solution)/shard_map/all_to_all | solution.py:454
  94.3 11.4 %collective-permute-start.4 = (bf16[4,128,256]{2,1,0:T(8,128)(2,1)S(1)}, bf16[4,128,256]{2,1,0:T(8,128)(2,1)S(1)}, u32[]{:S(2)}, u32[]{:S(2)}) collective-permute-start(bf16[4,128,256]{2,1,0:T(8,128)(2,1)S(1)} %shard_map.101), channel_id=1, source_target_pairs={{8,0},{16,8},{24,16},{32,24},{40,32},{48,40},{56,48},{64,56},{72,6... | collective-permute-start | bytes 786440 | tf_op jit(solution)/shard_map/ppermute | solution.py:446
  100.3 34.9 %all-to-all-start.3 = ((bf16[4,128,2304]{2,1,0:T(8,128)(2,1)}), bf16[4,128,2304]{2,1,0:T(8,128)(2,1)S(1)}, u32[]{:S(2)}, u32[]{:S(2)}) async-start(bf16[4,128,2304]{2,1,0:T(8,128)(2,1)} %bitcast.21), calls=%async_computation.3 | async-start | bytes 4718592 | tf_op jit(solution)/shard_map/all_to_all | solution.py:450
  106.3 10.9 %collective-permute-start.5 = (bf16[4,128,256]{2,1,0:T(8,128)(2,1)S(1)}, bf16[4,128,256]{2,1,0:T(8,128)(2,1)S(1)}, u32[]{:S(2)}, u32[]{:S(2)}) collective-permute-start(bf16[4,128,256]{2,1,0:T(8,128)(2,1)S(1)} %shard_map.102), channel_id=1, source_target_pairs={{8,0},{16,8},{24,16},{32,24},{40,32},{48,40},{56,48},{64,56},{72,6... | collective-permute-start | bytes 786440 | tf_op jit(solution)/shard_map/ppermute | solution.py:446
  117.8 10.4 %collective-permute-start.6 = (bf16[4,128,256]{2,1,0:T(8,128)(2,1)S(1)}, bf16[4,128,256]{2,1,0:T(8,128)(2,1)S(1)}, u32[]{:S(2)}, u32[]{:S(2)}) collective-permute-start(bf16[4,128,256]{2,1,0:T(8,128)(2,1)S(1)} %shard_map.103), channel_id=1, source_target_pairs={{8,0},{16,8},{24,16},{32,24},{40,32},{48,40},{56,48},{64,56},{72,6... | collective-permute-start | bytes 786440 | tf_op jit(solution)/shard_map/ppermute | solution.py:446
  128.7 10.4 %collective-permute-start.7 = (bf16[4,128,256]{2,1,0:T(8,128)(2,1)S(1)}, bf16[4,128,256]{2,1,0:T(8,128)(2,1)S(1)}, u32[]{:S(2)}, u32[]{:S(2)}) collective-permute-start(bf16[4,128,256]{2,1,0:T(8,128)(2,1)S(1)} %shard_map.104), channel_id=1, source_target_pairs={{8,0},{16,8},{24,16},{32,24},{40,32},{48,40},{56,48},{64,56},{72,6... | collective-permute-start | bytes 786440 | tf_op jit(solution)/shard_map/ppermute | solution.py:446

commit v6 on v4

--- a/solution.py
+++ b/solution.py
@@ -335,24 +335,47 @@
     )(keys, values)
 
 
-def join_kernel(q_ref, g_ref, kv_ref, out_ref):
-    width = q_ref.shape[1]
-    out_ref[:, :width] = q_ref[...]
-    out_ref[:, width : 2 * width] = g_ref[...]
-    out_ref[:, 2 * width :] = kv_ref[...]
+def join_kernel(q_ref, g_ref, kv_ref, out_ref, rows_ref, in_sems, out_sems):
+    heads, _, total = out_ref.shape
+    width = (total - 2 * HD) // 2
+    moves = []
+    for h in range(heads):
+        cols = slice(h * width, (h + 1) * width)
+        parts = [
+            (q_ref.at[:, cols], rows_ref.at[h, :, :width]),
+            (g_ref.at[:, cols], rows_ref.at[h, :, width : 2 * width]),
+            (kv_ref.at[h], rows_ref.at[h, :, 2 * width :]),
+        ]
+        moves.append(
+            [pltpu.make_async_copy(a, b, in_sems.at[h, n]) for n, (a, b) in enumerate(parts)]
+        )
+        for move in moves[h]:
+            move.start()
+    outs = [pltpu.make_async_copy(rows_ref.at[h], out_ref.at[h], out_sems.at[h]) for h in range(heads)]
+    for h in range(heads):
+        for move in moves[h]:
+            move.wait()
+        outs[h].start()
+    for out in outs:
+        out.wait()
 
 
 def join_pass(q, g, kv):
     heads, rows, pair = kv.shape
-    width = q.shape[1] // heads
-    block = pl.BlockSpec((rows, width), lambda h: (0, h))
+    shape = (heads, rows, 2 * q.shape[1] // heads + pair)
+    anywhere = pl.BlockSpec(memory_space=pl.ANY)
     return pl.pallas_call(
         join_kernel,
-        grid=(heads,),
-        in_specs=[block, block, pl.BlockSpec((None, rows, pair), lambda h: (h, 0, 0))],
-        out_specs=pl.BlockSpec((None, rows, 2 * width + pair), lambda h: (h, 0, 0)),
-        out_shape=sds((heads, rows, 2 * width + pair), jnp.bfloat16),
-        compiler_params=params(8),
+        in_specs=[anywhere] * 3,
+        out_specs=anywhere,
+        scratch_shapes=[
+            pltpu.VMEM(shape, jnp.bfloat16),
+            pltpu.SemaphoreType.DMA((heads, 3)),
+            pltpu.SemaphoreType.DMA((heads,)),
+        ],
+        out_shape=pltpu.HBM(shape, jnp.bfloat16),
+        compiler_params=pltpu.CompilerParams(vmem_limit_bytes=8 * MIB),
+        cost_estimate=pl.CostEstimate(flops=2 * 10**9, bytes_accessed=5 * MIB, transcendentals=0),
     )(in_hbm(q), in_hbm(g), kv)
 
 

time: 137 us -> 137 us (level)
  transfers between devices with their start and end apart: 12 -> 12, of which waited for: 10 -> 10; matrix products, arithmetic and copies ran while one was open for 0% -> 0% of each run, Pallas kernels for 16% -> 15%
where the time goes in v6:
time: 137 us; the launch traced here: 136 us
  waiting for transfers between devices  56.8 us (41%)
  starting transfers between devices  43.9 us (32%)
  Pallas kernels  32.8 us (24%)
  local copies, waits for them, and re-layouts  1.81 us (1%)
    ppermute x8, waiting for transfers between devices, ring(): lax.ppermute(array, 'col', [(i, i + by) for i in range(peers) if 0 <= i +...  47.5 us
    ppermute x8, starting transfers between devices, ring(): lax.ppermute(array, 'col', [(i, i + by) for i in range(peers) if 0 <= i +...  28.7 us
    pallas_call x1, Pallas kernels, far_pass(): pl.pallas_call(far_kernel, grid_spec=pltpu.PrefetchScalarGridSpec(num_sca...  10.6 us
    all_to_all x2, waiting for transfers between devices, across(): lax.all_to_all(array, ('yh', 'uly'), split_axis=0, concat_axis=0, tiled=T...  9.31 us
    all_to_all x2, starting transfers between devices, across(): lax.all_to_all(array, ('yh', 'uly'), split_axis=0, concat_axis=0, tiled=T...  7.97 us
    all_to_all x2, starting transfers between devices, to_heads(): return lax.all_to_all(array, 'uly', split_axis=0, concat_axis=0, tiled=True)  7.28 us
    pallas_call x1, Pallas kernels, rest_pass(): pl.pallas_call(rest_kernel, grid=(heads // HPS,), in_specs=[column(), col...  7.14 us
    pallas_call x1, Pallas kernels, near_pass(): pl.pallas_call(near_kernel, grid=(heads // HPS,), in_specs=[column(), col...  4.17 us
  transfers between devices with their start and end apart: 12, of which 10 were waited for; matrix products, arithmetic and copies ran while one was open for 0% of the time, Pallas kernels for 15%

profile of v6, /device:TPU:6, one launch (start us, length us, event | category | flops | bytes accessed | tf_op | source)
XLA Modules:
  0.0 136.2 jit_solution(2309377390958694932)
XLA Ops:
  0.6 0.9 copy-done
  1.5 0.9 copy-done.1
  2.5 3.8 %collective-permute-start = (bf16[4,128,256]{2,1,0:T(8,128)(2,1)S(1)}, bf16[4,128,256]{2,1,0:T(8,128)(2,1)S(1)}, u32[]{:S(2)}, u32[]{:S(2)}) collective-permute-start(bf16[4,128,256]{2,1,0:T(8,128)(2,1)S(1)} %shard_map.93.kv_ref.refs_0_), channel_id=1, source_target_pairs={{0,8},{8,16},{16,24},{24,32},{32,40},{40,48},{48,56},{56,64},{64,7... | collective-permute-start | bytes 786440 | tf_op jit(solution)/shard_map/ppermute | solution.py:469
  6.3 2.6 %shard_map.95 = bf16[4,128,2304]{2,1,0:T(8,128)(2,1)} custom-call(bf16[128,4096]{1,0:T(8,128)(2,1)} %q_ref.1, bf16[128,4096]{1,0:T(8,128)(2,1)} %g_ref.1, bf16[4,128,256]{2,1,0:T(8,128)(2,1)S(1)} %shard_map.93.kv_ref.refs_0_), custom_call_target="tpu_custom_call" | custom-call | flops 2000000000 | bytes 5242880 | tf_op jit(solution)/shard_map/pallas_call | solution.py:367
  9.0 3.6 %all-to-all-start = ((bf16[4,128,2304]{2,1,0:T(8,128)(2,1)}), bf16[4,128,2304]{2,1,0:T(8,128)(2,1)S(1)}, u32[]{:S(2)}, u32[]{:S(2)}) async-start(bf16[4,128,2304]{2,1,0:T(8,128)(2,1)} %shard_map.95), calls=%async_computation | async-start | bytes 4718592 | tf_op jit(solution)/shard_map/all_to_all | solution.py:473
  12.6 7.8 %collective-permute-done.refs_1_ = bf16[4,128,256]{2,1,0:T(8,128)(2,1)S(1)} collective-permute-done((bf16[4,128,256]{2,1,0:T(8,128)(2,1)S(1)}, bf16[4,128,256]{2,1,0:T(8,128)(2,1)S(1)}, u32[]{:S(2)}, u32[]{:S(2)}) %collective-permute-start) | collective-permute-done | bytes 262176 | tf_op jit(solution)/shard_map/ppermute | solution.py:469
  20.5 1.9 %collective-permute-start.1 = (bf16[4,128,256]{2,1,0:T(8,128)(2,1)S(1)}, bf16[4,128,256]{2,1,0:T(8,128)(2,1)S(1)}, u32[]{:S(2)}, u32[]{:S(2)}) collective-permute-start(bf16[4,128,256]{2,1,0:T(8,128)(2,1)S(1)} %collective-permute-done.refs_1_), channel_id=1, source_target_pairs={{0,8},{8,16},{16,24},{24,32},{32,40},{40,48},{48,56},{56,64},{64,7... | collective-permute-start | bytes 786440 | tf_op jit(solution)/shard_map/ppermute | solution.py:469
  22.4 9.6 %collective-permute-done.1.refs_2_ = bf16[4,128,256]{2,1,0:T(8,128)(2,1)S(1)} collective-permute-done((bf16[4,128,256]{2,1,0:T(8,128)(2,1)S(1)}, bf16[4,128,256]{2,1,0:T(8,128)(2,1)S(1)}, u32[]{:S(2)}, u32[]{:S(2)}) %collective-permute-start.1) | collective-permute-done | bytes 262176 | tf_op jit(solution)/shard_map/ppermute | solution.py:469
  31.9 1.9 %collective-permute-start.2 = (bf16[4,128,256]{2,1,0:T(8,128)(2,1)S(1)}, bf16[4,128,256]{2,1,0:T(8,128)(2,1)S(1)}, u32[]{:S(2)}, u32[]{:S(2)}) collective-permute-start(bf16[4,128,256]{2,1,0:T(8,128)(2,1)S(1)} %collective-permute-done.1.refs_2_), channel_id=1, source_target_pairs={{0,8},{8,16},{16,24},{24,32},{32,40},{40,48},{48,56},{56,64},{64,7... | collective-permute-start | bytes 786440 | tf_op jit(solution)/shard_map/ppermute | solution.py:469
  33.9 8.6 %collective-permute-done.2.refs_3_ = bf16[4,128,256]{2,1,0:T(8,128)(2,1)S(1)} collective-permute-done((bf16[4,128,256]{2,1,0:T(8,128)(2,1)S(1)}, bf16[4,128,256]{2,1,0:T(8,128)(2,1)S(1)}, u32[]{:S(2)}, u32[]{:S(2)}) %collective-permute-start.2) | collective-permute-done | bytes 262176 | tf_op jit(solution)/shard_map/ppermute | solution.py:469
  42.5 1.9 %collective-permute-start.3 = (bf16[4,128,256]{2,1,0:T(8,128)(2,1)S(1)}, bf16[4,128,256]{2,1,0:T(8,128)(2,1)S(1)}, u32[]{:S(2)}, u32[]{:S(2)}) collective-permute-start(bf16[4,128,256]{2,1,0:T(8,128)(2,1)S(1)} %collective-permute-done.2.refs_3_), channel_id=1, source_target_pairs={{0,8},{8,16},{16,24},{24,32},{32,40},{40,48},{48,56},{56,64},{64,7... | collective-permute-start | bytes 786440 | tf_op jit(solution)/shard_map/ppermute | solution.py:469
  44.4 1.2 shard_map.94.info
  45.6 7.2 %collective-permute-done.3.refs_4_ = bf16[4,128,256]{2,1,0:T(8,128)(2,1)S(1)} collective-permute-done((bf16[4,128,256]{2,1,0:T(8,128)(2,1)S(1)}, bf16[4,128,256]{2,1,0:T(8,128)(2,1)S(1)}, u32[]{:S(2)}, u32[]{:S(2)}) %collective-permute-start.3) | collective-permute-done | bytes 262176 | tf_op jit(solution)/shard_map/ppermute | solution.py:469
  52.9 1.4 %shard_map.96 = bf16[8,128,256]{2,1,0:T(8,128)(2,1)} custom-call(s32[4]{0:T(128)S(1)} %shard_map.94.info, bf16[4,128,256]{2,1,0:T(8,128)(2,1)S(1)} %shard_map.93.kv_ref.refs_0_, bf16[4,128,256]{2,1,0:T(8,128)(2,1)S(1)} %collective-permute-done.refs_1_, bf16[4,128,256]{2,1,0:T(8,128)(2,1)S(1)} %collective-permute-done.1.refs_2_, ...), custom_call_target="tpu_custom_call" | custom-call | flops 10000000000 | bytes 41943040 | tf_op jit(solution)/shard_map/pallas_call | solution.py:310
  54.3 4.5 %all-to-all-start.1 = ((bf16[8,128,256]{2,1,0:T(8,128)(2,1)}), bf16[8,128,256]{2,1,0:T(8,128)(2,1)S(1)}, u32[]{:S(2)}, u32[]{:S(2)}) async-start(bf16[8,128,256]{2,1,0:T(8,128)(2,1)} %shard_map.96), calls=%async_computation.1 | async-start | bytes 1048576 | tf_op jit(solution)/shard_map/all_to_all | solution.py:477
  58.8 4.2 %shard_map.97 = (bf16[8,128,512]{2,1,0:T(8,128)(2,1)}, f32[8,8,512]{2,1,0:T(8,128)S(1)}) custom-call(bf16[512,2304]{1,0:T(8,128)(2,1)S(1)} %bitcast.11, bf16[512,2304]{1,0:T(8,128)(2,1)S(1)} %bitcast.12, bf16[512,2304]{1,0:T(8,128)(2,1)S(1)} %bitcast.13), custom_call_target="tpu_custom_call" | custom-call | flops 3000000000 | bytes 4194304 | tf_op jit(solution)/shard_map/pallas_call | solution.py:209
  63.0 6.2 %all-to-all-done.1 = bf16[8,128,256]{2,1,0:T(8,128)(2,1)S(1)} async-done(((bf16[8,128,256]{2,1,0:T(8,128)(2,1)}), bf16[8,128,256]{2,1,0:T(8,128)(2,1)S(1)}, u32[]{:S(2)}, u32[]{:S(2)}) %all-to-all-start.1) | async-done | bytes 524320 | tf_op jit(solution)/shard_map/all_to_all | solution.py:477
  69.1 10.6 %shard_map.98 = (bf16[8,256,512]{2,1,0:T(8,128)(2,1)}, f32[8,8,512]{2,1,0:T(8,128)S(1)}, bf16[2,512,256]{2,1,0:T(8,128)(2,1)}) custom-call(s32[4]{0:T(128)S(1)} %shard_map.94.info, bf16[512,2304]{1,0:T(8,128)(2,1)S(1)} %bitcast.14, bf16[512,2304]{1,0:T(8,128)(2,1)S(1)} %bitcast.15, bf16[2,512,256]{2,1,0:T(8,128)(2,1)S(1)} %bitcast.19, ...), custom_call_target="tpu_custom_call" | custom-call | flops 6000000000 | bytes 8388608 | tf_op jit(solution)/shard_map/pallas_call | solution.py:225
  79.7 3.5 %all-to-all-start.2 = ((bf16[8,128,256]{2,1,0:T(8,128)(2,1)}), bf16[8,128,256]{2,1,0:T(8,128)(2,1)S(1)}, u32[]{:S(2)}, u32[]{:S(2)}) async-start(bf16[8,128,256]{2,1,0:T(8,128)(2,1)} %bitcast.3), calls=%async_computation.2 | async-start | bytes 1048576 | tf_op jit(solution)/shard_map/all_to_all | solution.py:477
  83.2 7.1 %shard_map.99 = bf16[512,2304]{1,0:T(8,128)(2,1)} custom-call(bf16[512,2304]{1,0:T(8,128)(2,1)S(1)} %bitcast.16, bf16[512,2304]{1,0:T(8,128)(2,1)S(1)} %bitcast.17, bf16[512,2304]{1,0:T(8,128)(2,1)S(1)} %bitcast.18, bf16[8,256,512]{2,1,0:T(8,128)(2,1)} %get-tuple-element.23.both_ref, f32[8,8,512]{2,1,0:T(8,128)S(1)} %get-tuple-element.24.line_ref), custom_call_target="tpu_custom_call" | custom-call | flops 5000000000 | bytes 6291456 | tf_op jit(solution)/shard_map/pallas_call | solution.py:250
  90.4 3.1 %all-to-all-done.2 = bf16[8,128,256]{2,1,0:T(8,128)(2,1)S(1)} async-done(((bf16[8,128,256]{2,1,0:T(8,128)(2,1)}), bf16[8,128,256]{2,1,0:T(8,128)(2,1)S(1)}, u32[]{:S(2)}, u32[]{:S(2)}) %all-to-all-start.2) | async-done | bytes 524320 | tf_op jit(solution)/shard_map/all_to_all | solution.py:477
  94.1 1.9 %collective-permute-start.4 = (bf16[4,128,256]{2,1,0:T(8,128)(2,1)S(1)}, bf16[4,128,256]{2,1,0:T(8,128)(2,1)S(1)}, u32[]{:S(2)}, u32[]{:S(2)}) collective-permute-start(bf16[4,128,256]{2,1,0:T(8,128)(2,1)S(1)} %shard_map.101), channel_id=1, source_target_pairs={{8,0},{16,8},{24,16},{32,24},{40,32},{48,40},{56,48},{64,56},{72,6... | collective-permute-start | bytes 786440 | tf_op jit(solution)/shard_map/ppermute | solution.py:469
  96.0 3.6 %all-to-all-start.3 = ((bf16[4,128,2304]{2,1,0:T(8,128)(2,1)}), bf16[4,128,2304]{2,1,0:T(8,128)(2,1)S(1)}, u32[]{:S(2)}, u32[]{:S(2)}) async-start(bf16[4,128,2304]{2,1,0:T(8,128)(2,1)} %bitcast.21), calls=%async_computation.3 | async-start | bytes 4718592 | tf_op jit(solution)/shard_map/all_to_all | solution.py:473
  99.6 4.2 %collective-permute-done.4.refs_0_ = bf16[4,128,256]{2,1,0:T(8,128)(2,1)S(1)} collective-permute-done((bf16[4,128,256]{2,1,0:T(8,128)(2,1)S(1)}, bf16[4,128,256]{2,1,0:T(8,128)(2,1)S(1)}, u32[]{:S(2)}, u32[]{:S(2)}) %collective-permute-start.4) | collective-permute-done | bytes 262176 | tf_op jit(solution)/shard_map/ppermute | solution.py:469
  104.4 4.3 %collective-permute-start.5 = (bf16[4,128,256]{2,1,0:T(8,128)(2,1)S(1)}, bf16[4,128,256]{2,1,0:T(8,128)(2,1)S(1)}, u32[]{:S(2)}, u32[]{:S(2)}) collective-permute-start(bf16[4,128,256]{2,1,0:T(8,128)(2,1)S(1)} %shard_map.102), channel_id=1, source_target_pairs={{8,0},{16,8},{24,16},{32,24},{40,32},{48,40},{56,48},{64,56},{72,6... | collective-permute-start | bytes 786440 | tf_op jit(solution)/shard_map/ppermute | solution.py:469
  108.7 4.8 %collective-permute-done.5.refs_0_ = bf16[4,128,256]{2,1,0:T(8,128)(2,1)S(1)} collective-permute-done((bf16[4,128,256]{2,1,0:T(8,128)(2,1)S(1)}, bf16[4,128,256]{2,1,0:T(8,128)(2,1)S(1)}, u32[]{:S(2)}, u32[]{:S(2)}) %collective-permute-start.5) | collective-permute-done | bytes 262176 | tf_op jit(solution)/shard_map/ppermute | solution.py:469
  114.1 6.5 %collective-permute-start.6 = (bf16[4,128,256]{2,1,0:T(8,128)(2,1)S(1)}, bf16[4,128,256]{2,1,0:T(8,128)(2,1)S(1)}, u32[]{:S(2)}, u32[]{:S(2)}) collective-permute-start(bf16[4,128,256]{2,1,0:T(8,128)(2,1)S(1)} %shard_map.103), channel_id=1, source_target_pairs={{8,0},{16,8},{24,16},{32,24},{40,32},{48,40},{56,48},{64,56},{72,6... | collective-permute-start | bytes 786440 | tf_op jit(solution)/shard_map/ppermute | solution.py:469
  120.6 3.9 %collective-permute-done.6.refs_0_ = bf16[4,128,256]{2,1,0:T(8,128)(2,1)S(1)} collective-permute-done((bf16[4,128,256]{2,1,0:T(8,128)(2,1)S(1)}, bf16[4,128,256]{2,1,0:T(8,128)(2,1)S(1)}, u32[]{:S(2)}, u32[]{:S(2)}) %collective-permute-start.6) | collective-permute-done | bytes 262176 | tf_op jit(solution)/shard_map/ppermute | solution.py:469
  125.1 6.5 %collective-permute-start.7 = (bf16[4,128,256]{2,1,0:T(8,128)(2,1)S(1)}, bf16[4,128,256]{2,1,0:T(8,128)(2,1)S(1)}, u32[]{:S(2)}, u32[]{:S(2)}) collective-permute-start(bf16[4,128,256]{2,1,0:T(8,128)(2,1)S(1)} %shard_map.104), channel_id=1, source_target_pairs={{8,0},{16,8},{24,16},{32,24},{40,32},{48,40},{56,48},{64,56},{72,6... | collective-permute-start | bytes 786440 | tf_op jit(solution)/shard_map/ppermute | solution.py:469
  131.5 2.4 %shard_map.100 = (bf16[128,4096]{1,0:T(8,128)(2,1)}, bf16[128,4096]{1,0:T(8,128)(2,1)}, f32[4,128,256]{2,1,0:T(8,128)S(1)}) custom-call(s32[4]{0:T(128)S(1)} %shard_map.94.info, bf16[4,128,2304]{2,1,0:T(8,128)(2,1)S(1)} %all-to-all-done.3.all_ref, bf16[2,4,128,256]{3,2,1,0:T(8,128)(2,1)S(1)} %bitcast.10), custom_call_target="tpu_custom_call" | custom-call | tf_op jit(solution)/shard_map/pallas_call | solution.py:398
  134.0 1.4 %collective-permute-done.7.moved_ref = bf16[4,128,256]{2,1,0:T(8,128)(2,1)S(1)} collective-permute-done((bf16[4,128,256]{2,1,0:T(8,128)(2,1)S(1)}, bf16[4,128,256]{2,1,0:T(8,128)(2,1)S(1)}, u32[]{:S(2)}, u32[]{:S(2)}) %collective-permute-start.7) | collective-permute-done | bytes 262176 | tf_op jit(solution)/shard_map/ppermute | solution.py:469
  135.4 0.8 shard_map.105
  (13 shorter events, 2.5 us)
Async XLA Ops:
  0.6 0.9 copy-start
  1.5 0.9 copy-start.1
  2.5 18.0 %collective-permute-start = (bf16[4,128,256]{2,1,0:T(8,128)(2,1)S(1)}, bf16[4,128,256]{2,1,0:T(8,128)(2,1)S(1)}, u32[]{:S(2)}, u32[]{:S(2)}) collective-permute-start(bf16[4,128,256]{2,1,0:T(8,128)(2,1)S(1)} %shard_map.93.kv_ref.refs_0_), channel_id=1, source_target_pairs={{0,8},{8,16},{16,24},{24,32},{32,40},{40,48},{48,56},{56,64},{64,7... | collective-permute-start | bytes 786440 | tf_op jit(solution)/shard_map/ppermute | solution.py:469
  8.9 35.5 %copy-start.2 = (s32[128,2]{0,1:T(2,128)S(1)}, s32[128,2]{0,1:T(2,128)}, u32[]{:S(2)}) copy-start(s32[128,2]{0,1:T(2,128)} %param.10) | copy-start | bytes 3076
  9.0 35.5 %copy-start.3 = (s32[128]{0:T(128)S(1)}, s32[128]{0:T(128)}, u32[]{:S(2)}) copy-start(s32[128]{0:T(128)} %count_ref.1) | copy-start | bytes 1540
  9.0 45.3 %all-to-all-start = ((bf16[4,128,2304]{2,1,0:T(8,128)(2,1)}), bf16[4,128,2304]{2,1,0:T(8,128)(2,1)S(1)}, u32[]{:S(2)}, u32[]{:S(2)}) async-start(bf16[4,128,2304]{2,1,0:T(8,128)(2,1)} %shard_map.95), calls=%async_computation | async-start | bytes 4718592 | tf_op jit(solution)/shard_map/all_to_all | solution.py:473
  20.5 11.5 %collective-permute-start.1 = (bf16[4,128,256]{2,1,0:T(8,128)(2,1)S(1)}, bf16[4,128,256]{2,1,0:T(8,128)(2,1)S(1)}, u32[]{:S(2)}, u32[]{:S(2)}) collective-permute-start(bf16[4,128,256]{2,1,0:T(8,128)(2,1)S(1)} %collective-permute-done.refs_1_), channel_id=1, source_target_pairs={{0,8},{8,16},{16,24},{24,32},{32,40},{40,48},{48,56},{56,64},{64,7... | collective-permute-start | bytes 786440 | tf_op jit(solution)/shard_map/ppermute | solution.py:469
  31.9 10.6 %collective-permute-start.2 = (bf16[4,128,256]{2,1,0:T(8,128)(2,1)S(1)}, bf16[4,128,256]{2,1,0:T(8,128)(2,1)S(1)}, u32[]{:S(2)}, u32[]{:S(2)}) collective-permute-start(bf16[4,128,256]{2,1,0:T(8,128)(2,1)S(1)} %collective-permute-done.1.refs_2_), channel_id=1, source_target_pairs={{0,8},{8,16},{16,24},{24,32},{32,40},{40,48},{48,56},{56,64},{64,7... | collective-permute-start | bytes 786440 | tf_op jit(solution)/shard_map/ppermute | solution.py:469
  42.5 10.4 %collective-permute-start.3 = (bf16[4,128,256]{2,1,0:T(8,128)(2,1)S(1)}, bf16[4,128,256]{2,1,0:T(8,128)(2,1)S(1)}, u32[]{:S(2)}, u32[]{:S(2)}) collective-permute-start(bf16[4,128,256]{2,1,0:T(8,128)(2,1)S(1)} %collective-permute-done.2.refs_3_), channel_id=1, source_target_pairs={{0,8},{8,16},{16,24},{24,32},{32,40},{40,48},{48,56},{56,64},{64,7... | collective-permute-start | bytes 786440 | tf_op jit(solution)/shard_map/ppermute | solution.py:469
  54.3 14.8 %all-to-all-start.1 = ((bf16[8,128,256]{2,1,0:T(8,128)(2,1)}), bf16[8,128,256]{2,1,0:T(8,128)(2,1)S(1)}, u32[]{:S(2)}, u32[]{:S(2)}) async-start(bf16[8,128,256]{2,1,0:T(8,128)(2,1)} %shard_map.96), calls=%async_computation.1 | async-start | bytes 1048576 | tf_op jit(solution)/shard_map/all_to_all | solution.py:477
  79.7 13.8 %all-to-all-start.2 = ((bf16[8,128,256]{2,1,0:T(8,128)(2,1)}), bf16[8,128,256]{2,1,0:T(8,128)(2,1)S(1)}, u32[]{:S(2)}, u32[]{:S(2)}) async-start(bf16[8,128,256]{2,1,0:T(8,128)(2,1)} %bitcast.3), calls=%async_computation.2 | async-start | bytes 1048576 | tf_op jit(solution)/shard_map/all_to_all | solution.py:477
  94.1 9.7 %collective-permute-start.4 = (bf16[4,128,256]{2,1,0:T(8,128)(2,1)S(1)}, bf16[4,128,256]{2,1,0:T(8,128)(2,1)S(1)}, u32[]{:S(2)}, u32[]{:S(2)}) collective-permute-start(bf16[4,128,256]{2,1,0:T(8,128)(2,1)S(1)} %shard_map.101), channel_id=1, source_target_pairs={{8,0},{16,8},{24,16},{32,24},{40,32},{48,40},{56,48},{64,56},{72,6... | collective-permute-start | bytes 786440 | tf_op jit(solution)/shard_map/ppermute | solution.py:469
  96.0 35.5 %all-to-all-start.3 = ((bf16[4,128,2304]{2,1,0:T(8,128)(2,1)}), bf16[4,128,2304]{2,1,0:T(8,128)(2,1)S(1)}, u32[]{:S(2)}, u32[]{:S(2)}) async-start(bf16[4,128,2304]{2,1,0:T(8,128)(2,1)} %bitcast.21), calls=%async_computation.3 | async-start | bytes 4718592 | tf_op jit(solution)/shard_map/all_to_all | solution.py:473
  104.4 9.1 %collective-permute-start.5 = (bf16[4,128,256]{2,1,0:T(8,128)(2,1)S(1)}, bf16[4,128,256]{2,1,0:T(8,128)(2,1)S(1)}, u32[]{:S(2)}, u32[]{:S(2)}) collective-permute-start(bf16[4,128,256]{2,1,0:T(8,128)(2,1)S(1)} %shard_map.102), channel_id=1, source_target_pairs={{8,0},{16,8},{24,16},{32,24},{40,32},{48,40},{56,48},{64,56},{72,6... | collective-permute-start | bytes 786440 | tf_op jit(solution)/shard_map/ppermute | solution.py:469
  114.1 10.3 %collective-permute-start.6 = (bf16[4,128,256]{2,1,0:T(8,128)(2,1)S(1)}, bf16[4,128,256]{2,1,0:T(8,128)(2,1)S(1)}, u32[]{:S(2)}, u32[]{:S(2)}) collective-permute-start(bf16[4,128,256]{2,1,0:T(8,128)(2,1)S(1)} %shard_map.103), channel_id=1, source_target_pairs={{8,0},{16,8},{24,16},{32,24},{40,32},{48,40},{56,48},{64,56},{72,6... | collective-permute-start | bytes 786440 | tf_op jit(solution)/shard_map/ppermute | solution.py:469
  125.1 10.3 %collective-permute-start.7 = (bf16[4,128,256]{2,1,0:T(8,128)(2,1)S(1)}, bf16[4,128,256]{2,1,0:T(8,128)(2,1)S(1)}, u32[]{:S(2)}, u32[]{:S(2)}) collective-permute-start(bf16[4,128,256]{2,1,0:T(8,128)(2,1)S(1)} %shard_map.104), channel_id=1, source_target_pairs={{8,0},{16,8},{24,16},{32,24},{40,32},{48,40},{56,48},{64,56},{72,6... | collective-permute-start | bytes 786440 | tf_op jit(solution)/shard_map/ppermute | solution.py:469
